TPU v7x, 32 devices: a whole 2x2x4 slice. The times are simulated.
32 devices in a mesh: grp: 4 (over y, core), seq: 8 (over z, x).
Axes of the slice: x: 2, y: 2, z: 4, core: 2. Of those that a mesh axis runs over, the one named last changes fastest.
Arguments:
- hidden_in: bfloat16 [4096, 1024], P(('grp', 'seq')), may hold values from -6 to 6
- skips: bfloat16 [4096, 1024], P(('grp', 'seq')), may hold values from -6 to 6
- lengths: int32 [4, 8], P('grp'), may hold values from 1 to 896, as said below
- times: int32 [4, 8], P('grp'), may hold values from 0 to 999
- skip_weight: bfloat16 [2048, 1024], P('seq'), may hold values from -0.125 to 0.125
- cond_weight: bfloat16 [1024, 2048], P('seq'), may hold values from -0.1875 to 0.1875
- qkv_weight: bfloat16 [1024, 3072], P('seq'), may hold values from -0.1875 to 0.1875
- out_weight: bfloat16 [1024, 1024], P('seq'), may hold values from -1.5 to 1.5
- up_weight: bfloat16 [1024, 4096], P('seq'), may hold values from -0.1875 to 0.1875
- down_weight: bfloat16 [4096, 1024], P('seq'), may hold values from -0.09375 to 0.09375
- cotangent: bfloat16 [4096, 1024], P(('grp', 'seq')), may hold values from -6 to 6
Outputs:
- block_out: bfloat16 [4096, 1024], P(('grp', 'seq'))
- in_grad: bfloat16 [4096, 1024], P(('grp', 'seq'))
- skip_grad: bfloat16 [4096, 1024], P(('grp', 'seq'))
- skip_weight_grad: float32 [2048, 1024], P('seq')
- cond_weight_grad: float32 [1024, 2048], P('seq')
- qkv_weight_grad: float32 [1024, 3072], P('seq')
- out_weight_grad: float32 [1024, 1024], P('seq')
- up_weight_grad: float32 [1024, 4096], P('seq')
- down_weight_grad: float32 [4096, 1024], P('seq')
Inputs may be any that keep to these rules, and one draw needn't show every extreme that they name: Each row holds one group's 8 utterance lengths in frame order, summing to 1024; exactly one of them, never the first or the last, has 896 frames, and the others together have 128.
All inputs are finite; a program needn't handle non-finite values.
Results may differ from a plain program's by a relative error of at most 0.029.
Values may be sent and summed in bfloat16 or wider, within the bound.
No kernel may reach another device: no remote copies, remote signals or barrier semaphores. Data moves between devices by JAX's collectives and lax.ppermute only.
A program may use at most 256 MiB of HBM per device.

v0:
```python
import math

import jax
import jax.numpy as jnp
from jax import lax
from jax.sharding import PartitionSpec as P

HEADS = 16


EPS = 1e-06


def contract(left, right, left_dim, right_dim):
    return lax.dot_general(
        left, right, (((left_dim,), (right_dim,)), ((), ())), preferred_element_type=jnp.float32
    )


def matmul(left, right):
    return jnp.dot(left, right, preferred_element_type=jnp.float32)


def owner_of(frames, utt_ends):
    return jnp.sum((frames[:, None] >= utt_ends[None, :]).astype(jnp.int32), axis=1)


def same_owner(query_owner, key_owner):
    return (query_owner[:, None] == key_owner[None, :])[:, None, :]


def embed_steps(time_steps, model_width):
    half_width = model_width // 2
    freqs = jnp.exp(-math.log(10000.0) * jnp.arange(half_width, dtype=jnp.float32) / half_width)
    angles = time_steps[:, None] * freqs[None, :]
    return jnp.concatenate([jnp.sin(angles), jnp.cos(angles)], axis=1)


def rotate(vectors, positions, head_count, direction):
    tok_rows, model_width = vectors.shape
    head_size = model_width // head_count
    half_size = head_size // 2
    inverse = jnp.exp(-math.log(10000.0) * jnp.arange(half_size, dtype=jnp.float32) / half_size)
    angles = positions[:, None] * inverse[None, :]
    cosine = jnp.cos(angles)[:, None, :]
    sine = direction * jnp.sin(angles)[:, None, :]
    split = vectors.reshape(tok_rows, head_count, head_size)
    first_half = split[..., :half_size]
    second_half = split[..., half_size:]
    turned = jnp.concatenate(
        [first_half * cosine - second_half * sine, first_half * sine + second_half * cosine],
        axis=-1,
    )
    return turned.reshape(tok_rows, model_width)


def scale_norm(hidden, cond_part):
    return (
        hidden
        * lax.rsqrt(jnp.mean(hidden * hidden, axis=1, keepdims=True) + EPS)
        * (1.0 + cond_part)
    )


def over_blocks(update, running, arrays, first_row, block_cap):
    row_count = arrays[0].shape[0]
    block_size = math.gcd(row_count, block_cap)
    number = row_count // block_size
    if number == 1:
        return update(running, arrays, first_row)
    stacked = tuple((array.reshape((number, block_size) + array.shape[1:]) for array in arrays))
    offsets = first_row + block_size * jnp.arange(number, dtype=jnp.int32)

    def over_scan_step(inner, scan_in):
        return (update(inner, scan_in[0], scan_in[1]), None)

    result, unused = lax.scan(over_scan_step, running, (stacked, offsets))
    return result


def grad_terms(
    q_heads, do_heads, log_total, row_delta, key_heads, value_heads, same_utt, score_scale
):
    scores = (
        jnp.einsum("qhd,khd->qhk", q_heads, key_heads, preferred_element_type=jnp.float32)
        * score_scale
    )
    probs = jnp.where(same_utt, jnp.exp(scores - log_total[..., None]), 0.0)
    d_probs = jnp.einsum("qhd,khd->qhk", do_heads, value_heads, preferred_element_type=jnp.float32)
    d_scores = (probs * (d_probs - row_delta[..., None]) * score_scale).astype(jnp.bfloat16)
    return (probs.astype(jnp.bfloat16), d_scores)


def body(
    hidden_in,
    skips,
    lengths,
    times,
    skip_weight,
    cond_weight,
    qkv_weight,
    out_weight,
    up_weight,
    down_weight,
    cotangent,
):
    tok_rows, model_width = hidden_in.shape
    head_count = HEADS
    head_size = model_width // head_count
    score_scale = head_size ** (-0.5)
    first_frame = lax.axis_index("seq") * tok_rows
    utt_lengths = lengths[0]
    utt_ends = jnp.cumsum(utt_lengths)
    starts = utt_ends - utt_lengths
    frames = first_frame + jnp.arange(tok_rows, dtype=jnp.int32)
    query_owner = owner_of(frames, utt_ends)
    onehot = query_owner[:, None] == jnp.arange(utt_lengths.shape[0], dtype=jnp.int32)[None, :]
    positions = (frames - jnp.sum(jnp.where(onehot, starts[None, :], 0), axis=1)).astype(
        jnp.float32
    )
    time_steps = jnp.sum(jnp.where(onehot, times[0][None, :], 0), axis=1).astype(jnp.float32)
    gathered = (
        lax.all_gather(skip_weight, "seq", axis=0, tiled=True),
        lax.all_gather(cond_weight, "seq", axis=0, tiled=True),
        lax.all_gather(qkv_weight, "seq", axis=0, tiled=True),
        lax.all_gather(out_weight, "seq", axis=0, tiled=True),
        lax.all_gather(up_weight, "seq", axis=0, tiled=True),
        lax.all_gather(down_weight, "seq", axis=0, tiled=True),
    )
    w_skip, w_cond, w_qkv, w_out, w_up, w_down = gathered
    h_zero = matmul(hidden_in, w_skip[:model_width]) + matmul(skips, w_skip[model_width:])
    emb = embed_steps(time_steps, model_width).astype(jnp.bfloat16)
    cond = matmul(emb, w_cond)
    cond_attn = cond[:, :model_width]
    cond_ffn = cond[:, model_width:]
    normed = scale_norm(h_zero, cond_attn).astype(jnp.bfloat16)
    qkv = matmul(normed, w_qkv)
    queries = rotate(qkv[:, :model_width], positions, head_count, 1.0).astype(jnp.bfloat16)
    keys = rotate(qkv[:, model_width : 2 * model_width], positions, head_count, 1.0).astype(
        jnp.bfloat16
    )
    values = qkv[:, 2 * model_width :].astype(jnp.bfloat16)
    q_heads = queries.reshape(tok_rows, head_count, head_size)

    def forward_step(running, blocks, first_row):
        weighted, run_max, run_sum = running
        key_heads = blocks[0].reshape(-1, head_count, head_size)
        value_heads = blocks[1].reshape(-1, head_count, head_size)
        key_owner = owner_of(first_row + jnp.arange(key_heads.shape[0], dtype=jnp.int32), utt_ends)
        same_utt = same_owner(query_owner, key_owner)
        scores = (
            jnp.einsum("qhd,khd->qhk", q_heads, key_heads, preferred_element_type=jnp.float32)
            * score_scale
        )
        new_max = jnp.maximum(run_max, jnp.max(jnp.where(same_utt, scores, -1e30), axis=-1))
        weights_b = jnp.where(same_utt, jnp.exp(scores - new_max[..., None]), 0.0)
        factor = jnp.exp(run_max - new_max)
        run_sum = run_sum * factor + jnp.sum(weights_b, axis=-1)
        weighted = weighted * factor[..., None] + jnp.einsum(
            "qhk,khd->qhd",
            weights_b.astype(jnp.bfloat16),
            value_heads,
            preferred_element_type=jnp.float32,
        )
        return (weighted, new_max, run_sum)

    start_state = (
        jnp.zeros((tok_rows, head_count, head_size), jnp.float32),
        jnp.full((tok_rows, head_count), -1e30, jnp.float32),
        jnp.zeros((tok_rows, head_count), jnp.float32),
    )
    weighted, run_max, run_sum = over_blocks(
        forward_step,
        start_state,
        (
            lax.all_gather(keys, "seq", axis=0, tiled=True),
            lax.all_gather(values, "seq", axis=0, tiled=True),
        ),
        jnp.int32(0),
        1024,
    )
    attended_full = (weighted / run_sum[..., None]).reshape(tok_rows, model_width)
    log_total = run_max + jnp.log(run_sum)
    attended = attended_full.astype(jnp.bfloat16)
    h_one = h_zero + matmul(attended, w_out)
    normed_two = scale_norm(h_one, cond_ffn).astype(jnp.bfloat16)
    pre = matmul(normed_two, w_up)
    act = jax.nn.gelu(pre, approximate=False).astype(jnp.bfloat16)
    block_out = (h_one + matmul(act, w_down)).astype(jnp.bfloat16)
    regathered = (
        lax.all_gather(skip_weight, "seq", axis=0, tiled=True),
        lax.all_gather(cond_weight, "seq", axis=0, tiled=True),
        lax.all_gather(qkv_weight, "seq", axis=0, tiled=True),
        lax.all_gather(out_weight, "seq", axis=0, tiled=True),
        lax.all_gather(up_weight, "seq", axis=0, tiled=True),
        lax.all_gather(down_weight, "seq", axis=0, tiled=True),
    )
    w_skip, w_cond, w_qkv, w_out, w_up, w_down = regathered
    d_act = contract(cotangent, w_down, 1, 1)
    grad_down = contract(act, cotangent, 0, 0)
    unused, gelu_back = jax.vjp(lambda inner: jax.nn.gelu(inner, approximate=False), pre)
    d_pre = gelu_back(d_act)[0].astype(jnp.bfloat16)
    grad_up = contract(normed_two, d_pre, 0, 0)
    d_normed_two = contract(d_pre, w_up, 1, 1)
    unused, norm_back_two = jax.vjp(scale_norm, h_one, cond_ffn)
    d_h_norm, d_cond_ffn = norm_back_two(d_normed_two)
    d_h_one = cotangent.astype(jnp.float32) + d_h_norm
    d_h_low = d_h_one.astype(jnp.bfloat16)
    grad_out = contract(attended, d_h_low, 0, 0)
    d_attended = contract(d_h_low, w_out, 1, 1).astype(jnp.bfloat16)
    row_delta = jnp.sum(
        (d_attended.astype(jnp.float32) * attended_full).reshape(tok_rows, head_count, head_size),
        axis=-1,
    )
    do_heads = d_attended.reshape(tok_rows, head_count, head_size)
    keys_all, values_all = (
        lax.all_gather(keys, "seq", axis=0, tiled=True),
        lax.all_gather(values, "seq", axis=0, tiled=True),
    )
    key_total = keys_all.shape[0]
    block_size = math.gcd(key_total, 1024)
    number = key_total // block_size

    def body_scan_step(d_query, scan_in):
        key_block, value_block, offset = scan_in
        key_heads = key_block.reshape(block_size, head_count, head_size)
        value_heads = value_block.reshape(block_size, head_count, head_size)
        key_owner = owner_of(offset + jnp.arange(block_size, dtype=jnp.int32), utt_ends)
        probs_low, d_scores = grad_terms(
            q_heads,
            do_heads,
            log_total,
            row_delta,
            key_heads,
            value_heads,
            same_owner(query_owner, key_owner),
            score_scale,
        )
        d_query = d_query + jnp.einsum(
            "qhk,khd->qhd", d_scores, key_heads, preferred_element_type=jnp.float32
        )
        d_key = jnp.einsum(
            "qhk,qhd->khd", d_scores, q_heads, preferred_element_type=jnp.float32
        ).reshape(block_size, model_width)
        d_value = jnp.einsum(
            "qhk,qhd->khd", probs_low, do_heads, preferred_element_type=jnp.float32
        ).reshape(block_size, model_width)
        return (d_query, jnp.concatenate([d_key, d_value], axis=1))

    d_query, terms = lax.scan(
        body_scan_step,
        jnp.zeros((tok_rows, head_count, head_size), jnp.float32),
        (
            keys_all.reshape(number, block_size, model_width),
            values_all.reshape(number, block_size, model_width),
            block_size * jnp.arange(number, dtype=jnp.int32),
        ),
    )
    key_grads = lax.psum_scatter(
        terms.reshape(key_total, 2 * model_width), "seq", scatter_dimension=0, tiled=True
    )
    d_key = key_grads[:, :model_width]
    d_value = key_grads[:, model_width:]
    d_qkv = jnp.concatenate(
        [
            rotate(d_query.reshape(tok_rows, model_width), positions, head_count, -1.0),
            rotate(d_key, positions, head_count, -1.0),
            d_value,
        ],
        axis=1,
    ).astype(jnp.bfloat16)
    grad_qkv = contract(normed, d_qkv, 0, 0)
    d_normed = contract(d_qkv, w_qkv, 1, 1)
    unused, norm_back_one = jax.vjp(scale_norm, h_zero, cond_attn)
    d_h_first, d_cond_attn = norm_back_one(d_normed)
    d_h_zero = (d_h_one + d_h_first).astype(jnp.bfloat16)
    d_cond = jnp.concatenate([d_cond_attn, d_cond_ffn], axis=1).astype(jnp.bfloat16)
    grad_cond = contract(emb, d_cond, 0, 0)
    grad_skip_w = jnp.concatenate(
        [contract(hidden_in, d_h_zero, 0, 0), contract(skips, d_h_zero, 0, 0)], axis=0
    )
    in_grad = contract(d_h_zero, w_skip[:model_width], 1, 1).astype(jnp.bfloat16)
    skip_grad = contract(d_h_zero, w_skip[model_width:], 1, 1).astype(jnp.bfloat16)
    shards = (
        lax.psum_scatter(grad_skip_w, "seq", scatter_dimension=0, tiled=True),
        lax.psum_scatter(grad_cond, "seq", scatter_dimension=0, tiled=True),
        lax.psum_scatter(grad_qkv, "seq", scatter_dimension=0, tiled=True),
        lax.psum_scatter(grad_out, "seq", scatter_dimension=0, tiled=True),
        lax.psum_scatter(grad_up, "seq", scatter_dimension=0, tiled=True),
        lax.psum_scatter(grad_down, "seq", scatter_dimension=0, tiled=True),
    )
    summed = (
        lax.psum(shards[0].astype(jnp.bfloat16), "grp").astype(jnp.float32),
        lax.psum(shards[1].astype(jnp.bfloat16), "grp").astype(jnp.float32),
        lax.psum(shards[2].astype(jnp.bfloat16), "grp").astype(jnp.float32),
        lax.psum(shards[3].astype(jnp.bfloat16), "grp").astype(jnp.float32),
        lax.psum(shards[4].astype(jnp.bfloat16), "grp").astype(jnp.float32),
        lax.psum(shards[5].astype(jnp.bfloat16), "grp").astype(jnp.float32),
    )
    return (
        block_out,
        in_grad,
        skip_grad,
        summed[0],
        summed[1],
        summed[2],
        summed[3],
        summed[4],
        summed[5],
    )


def solution(mesh):
    placed = (
        P(("grp", "seq"), None),
        P(("grp", "seq"), None),
        P("grp", None),
        P("grp", None),
        P("seq", None),
        P("seq", None),
        P("seq", None),
        P("seq", None),
        P("seq", None),
        P("seq", None),
        P(("grp", "seq"), None),
    )
    return jax.shard_map(
        body,
        mesh=mesh,
        in_specs=placed,
        out_specs=(
            P(("grp", "seq"), None),
            P(("grp", "seq"), None),
            P(("grp", "seq"), None),
            P("seq", None),
            P("seq", None),
            P("seq", None),
            P("seq", None),
            P("seq", None),
            P("seq", None),
        ),
        check_vma=False,
    )
```

profile of v0, /device:TPU:9, one launch (start us, length us, event | category | flops | bytes accessed | tf_op | source)
XLA Modules:
  0.0 2130.0 jit_solution(2586535807317065713)
XLA Ops:
  13.0 70.1 %all-gather.9.cloned.1.call-done = bf16[2048,1024]{1,0:T(8,128)(2,1)} async-done(((bf16[256,1024]{1,0:T(8,128)(2,1)}), bf16[2048,1024]{1,0:T(8,128)(2,1)}) %all-gather.9.cloned.1.call-update) | async-done | bytes 4194320 | tf_op jit(solution)/shard_map/all_gather | solution.py:123
  87.3 69.7 %all-gather.11.cloned.1.call-done = bf16[1024,2048]{1,0:T(8,128)(2,1)} async-done(((bf16[128,2048]{1,0:T(8,128)(2,1)}), bf16[1024,2048]{1,0:T(8,128)(2,1)}) %all-gather.11.cloned.1.call-update) | async-done | bytes 4194320 | tf_op jit(solution)/shard_map/all_gather | solution.py:124
  160.7 95.1 %all-gather.13.cloned.1.call-done = bf16[1024,3072]{1,0:T(8,128)(2,1)} async-done(((bf16[128,3072]{1,0:T(8,128)(2,1)}), bf16[1024,3072]{1,0:T(8,128)(2,1)}) %all-gather.13.cloned.1.call-update) | async-done | bytes 6291472 | tf_op jit(solution)/shard_map/all_gather | solution.py:125
  255.8 3.9 fusion.90
  268.4 41.2 %all-gather.17.cloned.1.call-done = bf16[1024,1024]{1,0:T(8,128)(2,1)} async-done(((bf16[128,1024]{1,0:T(8,128)(2,1)}), bf16[1024,1024]{1,0:T(8,128)(2,1)}) %all-gather.17.cloned.1.call-update) | async-done | bytes 2097168 | tf_op jit(solution)/shard_map/all_gather | solution.py:177
  309.6 3.9 copy.45
  313.5 46.7 %all-gather.15.cloned.1.call-done = bf16[1024,1024]{0,1:T(8,128)(2,1)} async-done(((bf16[128,1024]{0,1:T(8,128)(2,1)}), bf16[1024,1024]{0,1:T(8,128)(2,1)}) %all-gather.15.cloned.1.call-update) | async-done | bytes 2097168 | tf_op jit(solution)/shard_map/all_gather | solution.py:176
  360.2 3.5 fusion.3
  370.2 40.9 %all-gather.19.cloned.1.call-done = bf16[1024,1024]{1,0:T(8,128)(2,1)} async-done(((bf16[128,1024]{1,0:T(8,128)(2,1)}), bf16[1024,1024]{1,0:T(8,128)(2,1)}) %all-gather.19.cloned.1.call-update) | async-done | bytes 2097168 | tf_op jit(solution)/shard_map/all_gather | solution.py:126
  413.9 121.4 %all-gather.21.cloned.1.call-done = bf16[1024,4096]{1,0:T(8,128)(2,1)} async-done(((bf16[128,4096]{1,0:T(8,128)(2,1)}), bf16[1024,4096]{1,0:T(8,128)(2,1)}) %all-gather.21.cloned.1.call-update) | async-done | bytes 8388624 | tf_op jit(solution)/shard_map/all_gather | solution.py:127
  535.3 6.0 fusion.91
  541.3 119.3 %all-gather.23.cloned.1.call-done = bf16[4096,1024]{1,0:T(8,128)(2,1)} async-done(((bf16[512,1024]{1,0:T(8,128)(2,1)}), bf16[4096,1024]{1,0:T(8,128)(2,1)}) %all-gather.23.cloned.1.call-update) | async-done | bytes 8388624 | tf_op jit(solution)/shard_map/all_gather | solution.py:128
  660.6 10.9 add_convert_fusion
  681.7 5.4 fusion.11
  687.1 5.7 fusion.2
  694.9 4.1 pad_maximum_fusion
  703.1 9.6 fusion.92
  715.8 8.1 fusion.93
  724.0 4.6 convolution_bitcast_fusion.2
  728.5 119.0 %reduce-scatter.8.cloned.1.call-done = f32[128,2048]{0,1:T(8,128)} async-done(((f32[1024,2048]{0,1:T(8,128)}), f32[128,2048]{0,1:T(8,128)}) %reduce-scatter.8.cloned.1.call-update) | async-done | bytes 1048592 | tf_op jit(solution)/shard_map/reduce_scatter | solution.py:259
  851.1 5.3 multiply_reduce_fusion
  857.5 4.5 fusion.56
  864.6 4.1 pad_maximum_fusion.1
  869.9 6.4 fusion.62
  876.5 63.4 %reduce-scatter.16.cloned.1.call-done = f32[128,1024]{1,0:T(8,128)} async-done(((f32[1024,1024]{1,0:T(8,128)}), f32[128,1024]{1,0:T(8,128)}) %reduce-scatter.16.cloned.1.call-update) | async-done | bytes 524304 | tf_op jit(solution)/shard_map/reduce_scatter | solution.py:288
  941.7 283.1 %reduce-scatter.18.cloned.1.call-done = f32[128,4096]{1,0:T(8,128)} async-done(((f32[1024,4096]{1,0:T(8,128)}), f32[128,4096]{1,0:T(8,128)}) %reduce-scatter.18.cloned.1.call-update) | async-done | bytes 2097168 | tf_op jit(solution)/shard_map/reduce_scatter | solution.py:289
  1227.5 283.1 %reduce-scatter.20.cloned.1.call-done = f32[512,1024]{1,0:T(8,128)} async-done(((f32[4096,1024]{1,0:T(8,128)}), f32[512,1024]{1,0:T(8,128)}) %reduce-scatter.20.cloned.1.call-update) | async-done | bytes 2097168 | tf_op jit(solution)/shard_map/reduce_scatter | solution.py:290
  1513.3 148.8 %reduce-scatter.12.cloned.1.call-done = f32[128,2048]{1,0:T(8,128)} async-done(((f32[1024,2048]{1,0:T(8,128)}), f32[128,2048]{1,0:T(8,128)}) %reduce-scatter.12.cloned.1.call-update) | async-done | bytes 1048592 | tf_op jit(solution)/shard_map/reduce_scatter | solution.py:286
  1664.2 149.9 %reduce-scatter.10.cloned.1.call-done = f32[256,1024]{1,0:T(8,128)} async-done(((f32[2048,1024]{1,0:T(8,128)}), f32[256,1024]{1,0:T(8,128)}) %reduce-scatter.10.cloned.1.call-update) | async-done | bytes 1048592 | tf_op jit(solution)/shard_map/reduce_scatter | solution.py:285
  1816.2 207.4 %reduce-scatter.14.cloned.1.call-done = f32[128,3072]{1,0:T(8,128)} async-done(((f32[1024,3072]{1,0:T(8,128)}), f32[128,3072]{1,0:T(8,128)}) %reduce-scatter.14.cloned.1.call-update) | async-done | bytes 1572880 | tf_op jit(solution)/shard_map/reduce_scatter | solution.py:287
  2026.0 5.5 fusion.43
  2034.6 79.9 %all-reduce.3.cloned.1.call-done = (bf16[256,1024]{1,0:T(8,128)(2,1)}, bf16[128,2048]{1,0:T(8,128)(2,1)}, bf16[128,3072]{1,0:T(8,128)(2,1)}, bf16[128,1024]{1,0:...) async-done(((bf16[256,1024]{1,0:T(8,128)(2,1)}, bf16[128,2048]{1,0:T(8,128)(2,1)}, bf16[128,3072]{1,0:T(8,128)(2,1)}, bf16[128,1024]{1,0:T(8,128)(2,1)}, ...) | async-done | bytes 4194320 | tf_op jit(solution)/shard_map/psum | solution.py:293
  (200 shorter events, 84.6 us)
Async XLA Ops:
  7.2 77.9 %copy-start = (bf16[128,1024]{1,0:T(8,128)(2,1)S(1)}, bf16[128,1024]{1,0:T(8,128)(2,1)}, u32[]{:S(2)}) copy-start(bf16[128,1024]{1,0:T(8,128)(2,1)} %param.11) | copy-start | bytes 786436
  7.2 75.9 %copy-start.37 = (bf16[128,1024]{1,0:T(8,128)(2,1)S(1)}, bf16[128,1024]{1,0:T(8,128)(2,1)}, u32[]{:S(2)}) copy-start(bf16[128,1024]{1,0:T(8,128)(2,1)} %param.12) | copy-start | bytes 786436
  7.2 75.9 %all-gather.9.cloned.1.call-start = ((), (), s32[]{:S(2)}) async-start(), calls=%async_computation.7 | async-start | bytes 4718592 | tf_op jit(solution)/shard_map/all_gather | solution.py:123
  7.9 149.0 %all-gather.11.cloned.1.call-start = ((), (), s32[]{:S(2)}) async-start(), calls=%async_computation.8 | async-start | bytes 4718592 | tf_op jit(solution)/shard_map/all_gather | solution.py:124
  8.7 247.2 %all-gather.13.cloned.1.call-start = ((), (), s32[]{:S(2)}) async-start(), calls=%async_computation.9 | async-start | bytes 7077888 | tf_op jit(solution)/shard_map/all_gather | solution.py:125
  9.4 300.1 %all-gather.17.cloned.1.call-start = ((), (), s32[]{:S(2)}) async-start(), calls=%async_computation.11 | async-start | bytes 2359296 | tf_op jit(solution)/shard_map/all_gather | solution.py:177
  12.9 144.0 %copy-start.25 = (bf16[128,512]{1,0:T(8,128)(2,1)}, bf16[128,512]{1,0:T(8,128)(2,1)S(1)}, u32[]{:S(2)}) copy-start(bf16[128,512]{1,0:T(8,128)(2,1)S(1)} %get-tuple-element.73) | copy-start | bytes 393220
  13.0 144.0 %copy-start.27 = (bf16[128,512]{1,0:T(8,128)(2,1)}, bf16[128,512]{1,0:T(8,128)(2,1)S(1)}, u32[]{:S(2)}) copy-start(bf16[128,512]{1,0:T(8,128)(2,1)S(1)} %get-tuple-element.74) | copy-start | bytes 393220
  87.2 72.6 %copy-start.50 = (f32[128]{0:T(128)}, f32[128]{0:T(128)S(1)}, u32[]{:S(2)}) copy-start(f32[128]{0:T(128)S(1)} %get-tuple-element.78) | copy-start | bytes 1540
  87.3 323.9 %copy-start.4 = (f32[128,1024]{1,0:T(8,128)}, f32[128,1024]{1,0:T(8,128)S(1)}, u32[]{:S(2)}) copy-start(f32[128,1024]{1,0:T(8,128)S(1)} %get-tuple-element.79) | copy-start | bytes 1572868
  87.3 72.6 %copy-start.43 = (f32[128]{0:T(128)}, f32[128]{0:T(128)S(1)}, u32[]{:S(2)}) copy-start(f32[128]{0:T(128)S(1)} %fusion.75) | copy-start | bytes 1540
  260.5 99.7 %all-gather.15.cloned.1.call-start = ((), (), s32[]{:S(2)}) async-start(), calls=%async_computation.10 | async-start | bytes 2359296 | tf_op jit(solution)/shard_map/all_gather | solution.py:176
  265.0 95.2 %copy-start.21 = (bf16[128,16,32]{0,2,1:T(8,128)(2,1)}, bf16[128,16,32]{0,2,1:T(8,128)(2,1)S(1)}, u32[]{:S(2)}) copy-start(bf16[128,16,32]{0,2,1:T(8,128)(2,1)S(1)} %get-tuple-element.62) | copy-start | bytes 393220
  265.0 95.2 %copy-start.23 = (bf16[128,16,32]{0,2,1:T(8,128)(2,1)}, bf16[128,16,32]{0,2,1:T(8,128)(2,1)S(1)}, u32[]{:S(2)}) copy-start(bf16[128,16,32]{0,2,1:T(8,128)(2,1)S(1)} %get-tuple-element.63) | copy-start | bytes 393220
  265.8 145.3 %all-gather.19.cloned.1.call-start = ((), (), s32[]{:S(2)}) async-start(), calls=%async_computation.12 | async-start | bytes 2359296 | tf_op jit(solution)/shard_map/all_gather | solution.py:126
  266.4 268.9 %all-gather.21.cloned.1.call-start = ((), (), s32[]{:S(2)}) async-start(), calls=%async_computation.13 | async-start | bytes 9437184 | tf_op jit(solution)/shard_map/all_gather | solution.py:127
  267.1 393.4 %all-gather.23.cloned.1.call-start = ((), (), s32[]{:S(2)}) async-start(), calls=%async_computation.14 | async-start | bytes 9437184 | tf_op jit(solution)/shard_map/all_gather | solution.py:128
  267.9 579.6 %reduce-scatter.8.cloned.1.call-start = ((), (), s32[]{:S(2)}) async-start(), calls=%async_computation.15 | async-start | bytes 9437184 | tf_op jit(solution)/shard_map/reduce_scatter | solution.py:259
  413.9 127.3 %copy-start.10 = (bf16[128,1024]{1,0:T(8,128)(2,1)}, bf16[128,1024]{1,0:T(8,128)(2,1)S(1)}, u32[]{:S(2)}) copy-start(bf16[128,1024]{1,0:T(8,128)(2,1)S(1)} %multiply_convert_fusion.3) | copy-start | bytes 786436
  413.9 246.6 %copy-start.29 = (bf16[128,1024]{1,0:T(8,128)(2,1)S(1)}, bf16[128,1024]{1,0:T(8,128)(2,1)}, u32[]{:S(2)}) copy-start(bf16[128,1024]{1,0:T(8,128)(2,1)} %param.21) | copy-start | bytes 786436
  660.6 11.0 copy-start.2
  687.1 5.8 copy-start.22
  687.1 5.8 copy-start.24
  699.1 240.9 %reduce-scatter.16.cloned.1.call-start = ((), (), s32[]{:S(2)}) async-start(), calls=%async_computation.19 | async-start | bytes 4718592 | tf_op jit(solution)/shard_map/reduce_scatter | solution.py:288
  701.9 522.8 %reduce-scatter.18.cloned.1.call-start = ((), (), s32[]{:S(2)}) async-start(), calls=%async_computation.20 | async-start | bytes 18874368 | tf_op jit(solution)/shard_map/reduce_scatter | solution.py:289
  712.8 797.8 %reduce-scatter.20.cloned.1.call-start = ((), (), s32[]{:S(2)}) async-start(), calls=%async_computation.21 | async-start | bytes 18874368 | tf_op jit(solution)/shard_map/reduce_scatter | solution.py:290
  723.9 125.8 %copy-start.40 = (f32[128,32]{0,1:T(8,128)S(1)}, f32[128,32]{0,1:T(8,128)}, u32[]{:S(2)}) copy-start(f32[128,32]{0,1:T(8,128)} %get-tuple-element.75) | copy-start | bytes 49156
  723.9 938.2 %reduce-scatter.12.cloned.1.call-start = ((), (), s32[]{:S(2)}) async-start(), calls=%async_computation.17 | async-start | bytes 9437184 | tf_op jit(solution)/shard_map/reduce_scatter | solution.py:286
  849.7 6.7 copy-start.12
  862.1 952.0 %reduce-scatter.10.cloned.1.call-start = ((), (), s32[]{:S(2)}) async-start(), calls=%async_computation.16 | async-start | bytes 9437184 | tf_op jit(solution)/shard_map/reduce_scatter | solution.py:285
  868.8 1154.9 %reduce-scatter.14.cloned.1.call-start = ((), (), s32[]{:S(2)}) async-start(), calls=%async_computation.18 | async-start | bytes 14155776 | tf_op jit(solution)/shard_map/reduce_scatter | solution.py:287
  876.3 1238.2 %all-reduce.3.cloned.1.call-start = ((), (), s32[]{:S(2)}) async-start(), calls=%async_computation.22 | async-start | bytes 8388608 | tf_op jit(solution)/shard_map/psum | solution.py:293
  (36 other events, 98.8 us)
Sparse Core Ops, SparseCore 0:
  10.2 72.8 all-gather.8
  85.2 71.7 all-gather.10
  159.1 96.6 all-gather.12
  260.6 48.9 all-gather.16
  312.0 48.1 all-gather.14
  362.2 48.8 all-gather.18
  413.2 122.0 all-gather.20
  537.4 123.1 all-gather.22
  699.2 148.2 reduce-scatter.7
  851.4 88.4 reduce-scatter.15
  943.7 281.0 reduce-scatter.17
  1228.9 281.6 reduce-scatter.19
  1514.2 147.8 reduce-scatter.11
  1666.1 147.9 reduce-scatter.9
  1817.5 206.0 reduce-scatter.13
  2027.4 87.1 all-reduce.2
where the time goes:
time: 2140 us; the launch traced here: 2130 us
  waiting for transfers between devices  1940 us (91%)
  matrix products  104 us (5%)
  other arithmetic  46.8 us (2%)
    reduce_scatter x1, waiting for transfers between devices, body(): lax.psum_scatter(grad_down, 'seq', scatter_dimension=0, tiled=True)  283 us
    reduce_scatter x1, waiting for transfers between devices, body(): lax.psum_scatter(grad_up, 'seq', scatter_dimension=0, tiled=True)  283 us
    reduce_scatter x1, waiting for transfers between devices, body(): lax.psum_scatter(grad_qkv, 'seq', scatter_dimension=0, tiled=True)  207 us
    reduce_scatter x1, waiting for transfers between devices, body(): lax.psum_scatter(grad_skip_w, 'seq', scatter_dimension=0, tiled=True)  150 us
    reduce_scatter x1, waiting for transfers between devices, body(): lax.psum_scatter(grad_cond, 'seq', scatter_dimension=0, tiled=True)  149 us
    all_gather x1, waiting for transfers between devices, body(): lax.all_gather(up_weight, 'seq', axis=0, tiled=True)  121 us
    all_gather x1, waiting for transfers between devices, body(): lax.all_gather(down_weight, 'seq', axis=0, tiled=True)  119 us
    reduce_scatter x1, waiting for transfers between devices, body(): lax.psum_scatter(terms.reshape(key_total, 2 * model_width), 'seq', scatte...  119 us
  transfers between devices with their start and end apart: 16, of which 16 were waited for; matrix products, arithmetic and copies ran while one was open for 5% of the time, Pallas kernels for 0%

commit v1 on v0

--- a/solution.py
+++ b/solution.py
@@ -3,6 +3,8 @@
 import jax
 import jax.numpy as jnp
 from jax import lax
+from jax.experimental import pallas as pl
+from jax.experimental.pallas import tpu as pltpu
 from jax.sharding import PartitionSpec as P
 
 HEADS = 16
@@ -91,7 +93,13 @@
     return (probs.astype(jnp.bfloat16), d_scores)
 
 
-def body(
+def scatter_first(after, grad):
+    return lax.optimization_barrier(
+        (after, lax.psum_scatter(grad, "seq", scatter_dimension=0, tiled=True))
+    )
+
+
+def plain_body(
     hidden_in,
     skips,
     lengths,
@@ -197,16 +205,16 @@
     )
     w_skip, w_cond, w_qkv, w_out, w_up, w_down = regathered
     d_act = contract(cotangent, w_down, 1, 1)
-    grad_down = contract(act, cotangent, 0, 0)
+    d_act, shard_down = scatter_first(d_act, contract(act, cotangent, 0, 0))
     unused, gelu_back = jax.vjp(lambda inner: jax.nn.gelu(inner, approximate=False), pre)
     d_pre = gelu_back(d_act)[0].astype(jnp.bfloat16)
-    grad_up = contract(normed_two, d_pre, 0, 0)
+    d_pre, shard_up = scatter_first(d_pre, contract(normed_two, d_pre, 0, 0))
     d_normed_two = contract(d_pre, w_up, 1, 1)
     unused, norm_back_two = jax.vjp(scale_norm, h_one, cond_ffn)
     d_h_norm, d_cond_ffn = norm_back_two(d_normed_two)
     d_h_one = cotangent.astype(jnp.float32) + d_h_norm
     d_h_low = d_h_one.astype(jnp.bfloat16)
-    grad_out = contract(attended, d_h_low, 0, 0)
+    d_h_low, shard_out = scatter_first(d_h_low, contract(attended, d_h_low, 0, 0))
     d_attended = contract(d_h_low, w_out, 1, 1).astype(jnp.bfloat16)
     row_delta = jnp.sum(
         (d_attended.astype(jnp.float32) * attended_full).reshape(tok_rows, head_count, head_size),
@@ -245,7 +253,7 @@
         d_value = jnp.einsum(
             "qhk,qhd->khd", probs_low, do_heads, preferred_element_type=jnp.float32
         ).reshape(block_size, model_width)
-        return (d_query, jnp.concatenate([d_key, d_value], axis=1))
+        return (d_query, (d_key, d_value))
 
     d_query, terms = lax.scan(
         body_scan_step,
@@ -256,11 +264,10 @@
             block_size * jnp.arange(number, dtype=jnp.int32),
         ),
     )
-    key_grads = lax.psum_scatter(
-        terms.reshape(key_total, 2 * model_width), "seq", scatter_dimension=0, tiled=True
-    )
-    d_key = key_grads[:, :model_width]
-    d_value = key_grads[:, model_width:]
+    value_terms, d_key = scatter_first(terms[1], terms[0].reshape(key_total, model_width))
+    d_value = lax.psum_scatter(
+        value_terms.reshape(key_total, model_width), "seq", scatter_dimension=0, tiled=True
+    )
     d_qkv = jnp.concatenate(
         [
             rotate(d_query.reshape(tok_rows, model_width), positions, head_count, -1.0),
@@ -269,13 +276,13 @@
         ],
         axis=1,
     ).astype(jnp.bfloat16)
-    grad_qkv = contract(normed, d_qkv, 0, 0)
+    d_qkv, shard_qkv = scatter_first(d_qkv, contract(normed, d_qkv, 0, 0))
     d_normed = contract(d_qkv, w_qkv, 1, 1)
     unused, norm_back_one = jax.vjp(scale_norm, h_zero, cond_attn)
     d_h_first, d_cond_attn = norm_back_one(d_normed)
     d_h_zero = (d_h_one + d_h_first).astype(jnp.bfloat16)
     d_cond = jnp.concatenate([d_cond_attn, d_cond_ffn], axis=1).astype(jnp.bfloat16)
-    grad_cond = contract(emb, d_cond, 0, 0)
+    d_cond, shard_cond = scatter_first(d_cond, contract(emb, d_cond, 0, 0))
     grad_skip_w = jnp.concatenate(
         [contract(hidden_in, d_h_zero, 0, 0), contract(skips, d_h_zero, 0, 0)], axis=0
     )
@@ -283,11 +290,11 @@
     skip_grad = contract(d_h_zero, w_skip[model_width:], 1, 1).astype(jnp.bfloat16)
     shards = (
         lax.psum_scatter(grad_skip_w, "seq", scatter_dimension=0, tiled=True),
-        lax.psum_scatter(grad_cond, "seq", scatter_dimension=0, tiled=True),
-        lax.psum_scatter(grad_qkv, "seq", scatter_dimension=0, tiled=True),
-        lax.psum_scatter(grad_out, "seq", scatter_dimension=0, tiled=True),
-        lax.psum_scatter(grad_up, "seq", scatter_dimension=0, tiled=True),
-        lax.psum_scatter(grad_down, "seq", scatter_dimension=0, tiled=True),
+        shard_cond,
+        shard_qkv,
+        shard_out,
+        shard_up,
+        shard_down,
     )
     summed = (
         lax.psum(shards[0].astype(jnp.bfloat16), "grp").astype(jnp.float32),
@@ -307,6 +314,686 @@
         summed[3],
         summed[4],
         summed[5],
+    )
+
+
+ORDER = (0, 2, 1, 3)
+BF16 = jnp.bfloat16
+F32 = jnp.float32
+ANY = pl.BlockSpec(memory_space=pl.ANY)
+VMEM = pl.BlockSpec(memory_space=pltpu.VMEM)
+SMEM = pl.BlockSpec(memory_space=pltpu.SMEM)
+
+
+def swapped(axis, mask, size):
+    return [(index, index ^ mask) for index in range(size)]
+
+
+def from_seq(array, mask):
+    return lax.ppermute(array, "seq", swapped("seq", mask, 8))
+
+
+def from_grp(array, mask):
+    return lax.ppermute(array, "grp", swapped("grp", mask, 4))
+
+
+def run_copies(pairs, sems):
+    copies = [pltpu.make_async_copy(src, dst, sems.at[i]) for i, (src, dst) in enumerate(pairs)]
+    for copy in copies:
+        copy.start()
+    for copy in copies:
+        copy.wait()
+
+
+def call(kernel, out_shapes, in_specs, scratch, args, flops=0, vmem_mib=48):
+    moved = sum(a.size * a.dtype.itemsize for a in args)
+    moved += sum(o.size * o.dtype.itemsize for o in out_shapes)
+    return pl.pallas_call(
+        kernel,
+        out_shape=tuple(out_shapes),
+        in_specs=in_specs,
+        out_specs=(VMEM,) * len(out_shapes),
+        scratch_shapes=scratch,
+        compiler_params=pltpu.CompilerParams(vmem_limit_bytes=vmem_mib * 1024 * 1024),
+        cost_estimate=pl.CostEstimate(flops=flops, bytes_accessed=moved, transcendentals=0),
+    )(*args)
+
+
+def sds(shape, dtype):
+    return jax.ShapeDtypeStruct(shape, dtype)
+
+
+def aligned(index, size):
+    return pl.ds(pl.multiple_of(index * size, size), size)
+
+
+def nt(left, right):
+    return lax.dot_general(left, right, (((1,), (1,)), ((), ())), preferred_element_type=F32)
+
+
+def tn(left, right):
+    return lax.dot_general(left, right, (((0,), (0,)), ((), ())), preferred_element_type=F32)
+
+
+def nn(left, right):
+    return jnp.dot(left, right, preferred_element_type=F32)
+
+
+def slot_rows(ids, pieces, dst, rows, lanes=None):
+    out = []
+    for r, piece in enumerate(pieces):
+        src = piece if lanes is None else piece.at[:, pl.ds(*lanes)]
+        out.append((src, dst.at[aligned(ids[0] ^ r, rows), :]))
+    return out
+
+
+def h_zero_kernel(ids, *refs):
+    inputs, weights = refs[:4], refs[4:12]
+    out, held, wide, sems = refs[12:]
+    tok = inputs[0].shape[0]
+    pairs = [(x, held.at[pl.ds(f * tok, tok), :]) for f, x in enumerate(inputs)]
+    run_copies(pairs + slot_rows(ids, weights, wide, weights[0].shape[0]), sems)
+    out[...] = nn(held[...], wide[...]).astype(BF16)
+
+
+def qkv_kernel(ids, *refs):
+    pieces, scale, weights = refs[:4], refs[4], refs[5:13]
+    normed_out, hidden_out, packed, held, wide, sems = refs[13:]
+    tok = packed.shape[1]
+    cols = pieces[0].shape[1]
+    pairs = []
+    for q in range(4):
+        for f in range(4):
+            pairs.append(
+                (
+                    pieces[q].at[pl.ds(ORDER[ORDER[f] ^ q] * tok, tok), :],
+                    held.at[pl.ds(f * tok, tok), aligned(ids[1] ^ q, cols)],
+                )
+            )
+    run_copies(pairs + slot_rows(ids, weights, wide, weights[0].shape[0]), sems)
+    for f in range(4):
+        rows = pl.ds(f * tok, tok)
+        hidden = held[rows, :].astype(F32)
+        inverse = lax.rsqrt(jnp.mean(hidden * hidden, axis=1, keepdims=True) + EPS)
+        normed = (hidden * inverse * scale[rows, :]).astype(BF16)
+        normed_out[rows, :] = normed
+        if f < 2:
+            hidden_out[rows, :] = held[rows, :]
+        qkv = nn(normed, wide[...]).astype(BF16)
+        group = ids[1] ^ ORDER[f]
+        for pair in range(2):
+            for part in range(3):
+                packed[2 * group + pair, :, pl.ds(part * 128, 128)] = qkv[
+                    :, (2 * part + pair) * 128 : (2 * part + pair + 1) * 128
+                ]
+
+
+def turn(vectors, cosine, sine):
+    lane = lax.broadcasted_iota(jnp.int32, vectors.shape, 1)
+    first = (lane & 63) < 32
+    other = jnp.where(first, pltpu.roll(vectors, 96, 1), pltpu.roll(vectors, 32, 1))
+    return vectors * cosine + other * sine
+
+
+CHUNK = 256
+
+
+def rotated(qkv, cosine, sine):
+    total = qkv.shape[0] * qkv.shape[1]
+    queries = qkv[:, :, 0:128].reshape(total, 128).astype(F32)
+    keys = qkv[:, :, 128:256].reshape(total, 128).astype(F32)
+    low_q = (turn(queries, cosine[...], sine[...])).astype(BF16) * jnp.asarray(0.125, BF16)
+    low_k = turn(keys, cosine[...], sine[...]).astype(BF16)
+    return low_q, low_k
+
+
+def attend_kernel(qkv, cosine, sine, owner_col, owner_row, out, log_out):
+    total = owner_col.shape[0]
+    tok = qkv.shape[1]
+    queries, keys = rotated(qkv, cosine, sine)
+    values = qkv[:, :, 256:384].reshape(total, 128)
+    for chunk in range(total // CHUNK):
+        rows = slice(chunk * CHUNK, (chunk + 1) * CHUNK)
+        same = owner_col[...] == owner_row[:, rows]
+        both = []
+        for head in range(2):
+            lanes = slice(64 * head, 64 * head + 64)
+            scores = jnp.where(same, nt(keys[:, lanes], queries[rows, lanes]), -1e30)
+            top = jnp.max(scores, axis=0, keepdims=True)
+            weights = jnp.exp(scores - top)
+            total_w = jnp.sum(weights, axis=0, keepdims=True)
+            log_out[head : head + 1, rows] = top + jnp.log(total_w)
+            mixed = tn(values[:, lanes], weights.astype(BF16)) * (1.0 / total_w)
+            both.append(mixed.T)
+        joined = jnp.concatenate(both, axis=1).astype(BF16)
+        for block in range(CHUNK // tok):
+            out[chunk * (CHUNK // tok) + block] = joined[block * tok : (block + 1) * tok]
+
+
+def attend_back_kernel(
+    qkv, d_att, cosine, sine, owner_col, owner_row, log_total, out, d_keys, d_values
+):
+    total = owner_col.shape[0]
+    tok = qkv.shape[1]
+    queries, keys = rotated(qkv, cosine, sine)
+    values = qkv[:, :, 256:384].reshape(total, 128)
+    back = d_att[...].reshape(total, 128)
+    keys_t = [keys[:, 64 * head : 64 * head + 64].astype(F32).T.astype(BF16) for head in range(2)]
+    for chunk in range(total // CHUNK):
+        rows = slice(chunk * CHUNK, (chunk + 1) * CHUNK)
+        same = owner_col[...] == owner_row[:, rows]
+        d_queries, k_terms, v_terms = [], [], []
+        for head in range(2):
+            lanes = slice(64 * head, 64 * head + 64)
+            scores = nt(keys[:, lanes], queries[rows, lanes])
+            probs = jnp.where(same, jnp.exp(scores - log_total[head : head + 1, rows]), 0.0)
+            d_probs = nt(values[:, lanes], back[rows, lanes])
+            delta = jnp.sum(probs * d_probs, axis=0, keepdims=True)
+            d_scores = (probs * (d_probs - delta)).astype(BF16)
+            v_terms.append(nn(probs.astype(BF16), back[rows, lanes]))
+            k_terms.append(nn(d_scores, queries[rows, lanes]))
+            d_queries.append(nn(keys_t[head], d_scores).T * 0.125)
+        k_new = jnp.concatenate(k_terms, axis=1)
+        v_new = jnp.concatenate(v_terms, axis=1)
+        if chunk == 0:
+            d_keys[...] = k_new
+            d_values[...] = v_new
+        else:
+            d_keys[...] += k_new
+            d_values[...] += v_new
+        d_q = jnp.concatenate(d_queries, axis=1)
+        d_q = turn(d_q, cosine[rows, :], -sine[rows, :]).astype(BF16)
+        for block in range(CHUNK // tok):
+            out[chunk * (CHUNK // tok) + block, :, 0:128] = d_q[block * tok : (block + 1) * tok]
+    d_k = turn(d_keys[...], cosine[...], -sine[...]).astype(BF16)
+    out[:, :, 128:256] = d_k.reshape(total // tok, tok, 128)
+    out[:, :, 256:384] = d_values[...].astype(BF16).reshape(total // tok, tok, 128)
+
+
+def attended_pairs(ids, blocks, dst, tok, parts):
+    pairs = []
+    for f in range(4):
+        for pair in range(2):
+            for part in range(parts):
+                pairs.append(
+                    (
+                        blocks.at[2 * (ids[1] ^ ORDER[f]) + pair, :, pl.ds(part * 128, 128)],
+                        dst.at[pl.ds(f * tok, tok), pl.ds((2 * part + pair) * 128, 128)],
+                    )
+                )
+    return pairs
+
+
+def out_rows(ids, weight, dst):
+    return [
+        (weight.at[aligned(ids[1], 128), :], dst.at[pl.ds(0, 128), :]),
+        (weight.at[aligned(ids[1] + 4, 128), :], dst.at[pl.ds(128, 128), :]),
+    ]
+
+
+def project_kernel(ids, blocks, weight, keep, send, attended, wide, sems):
+    tok = blocks.shape[1]
+    run_copies(attended_pairs(ids, blocks, attended, tok, 1) + out_rows(ids, weight, wide), sems)
+    keep[...] = nn(attended[0 : 2 * tok, :], wide[...])
+    send[...] = nn(attended[2 * tok :, :], wide[...]).astype(BF16)
+
+
+def residual_kernel(hidden, part, other, scale, h_one_out, normed_out):
+    tok = hidden.shape[0] // 2
+    for f in range(2):
+        rows, swap = pl.ds(f * tok, tok), pl.ds((1 - f) * tok, tok)
+        h_one = hidden[rows, :].astype(F32) + part[rows, :].astype(F32) + other[swap, :].astype(F32)
+        inverse = lax.rsqrt(jnp.mean(h_one * h_one, axis=1, keepdims=True) + EPS)
+        h_one_out[rows, :] = h_one
+        normed_out[rows, :] = (h_one * inverse * scale[rows, :]).astype(BF16)
+
+
+def gelu_parts(pre):
+    half = 0.5 * (1.0 + lax.erf(pre * (2.0**-0.5)))
+    slope = half + pre * jnp.exp(-0.5 * pre * pre) * ((2.0 * math.pi) ** -0.5)
+    return pre * half, slope
+
+
+def feed_kernel(ids, *refs):
+    normed, normed_c, cot = refs[0], refs[1], refs[2:6]
+    weights = refs[6:14]
+    act_out, d_pre_out, keep, send, up, down, held, cots, sems = refs[14:]
+    tok = cot[0].shape[0]
+    rows = weights[0].shape[0]
+    hidden = up.shape[1]
+    pairs = [(normed, held.at[pl.ds(0, 2 * tok), :]), (normed_c, held.at[pl.ds(2 * tok, 2 * tok), :])]
+    pairs += [(g, cots.at[pl.ds(f * tok, tok), :]) for f, g in enumerate(cot)]
+    pairs += slot_rows(ids, weights, up, rows, (0, hidden))
+    pairs += slot_rows(ids, weights, down, rows, (hidden, down.shape[1]))
+    run_copies(pairs, sems)
+    for f in range(4):
+        block = pl.ds(f * tok, tok)
+        pre = nn(held[block, :], up[...])
+        act, slope = gelu_parts(pre)
+        act_out[block, :] = act.astype(BF16)
+        d_pre = (nt(cots[block, :], down[...]) * slope).astype(BF16)
+        d_pre_out[block, :] = d_pre
+        d_normed = nt(d_pre, up[...])
+        if f < 2:
+            keep[block, :] = d_normed
+        else:
+            send[pl.ds((f - 2) * tok, tok), :] = d_normed.astype(BF16)
+
+
+def feed_grad_kernel(ids, normed, normed_c, c0, c1, c2, c3, act, d_pre, even, odd, held, cots, sems):
+    tok = c0.shape[0]
+    pairs = [(normed, held.at[pl.ds(0, 2 * tok), :]), (normed_c, held.at[pl.ds(2 * tok, 2 * tok), :])]
+    pairs += [(g, cots.at[pl.ds(f * tok, tok), :]) for f, g in enumerate((c0, c1, c2, c3))]
+    run_copies(pairs, sems)
+    cols = act.shape[1]
+    for r in range(8):
+        block = aligned(ids[0] ^ r, 128)
+        target = (even, odd)[r % 2]
+        target[r // 2, :, 0:cols] = tn(held[:, block], d_pre[...]).astype(BF16)
+        target[r // 2, :, cols:] = tn(act[:, block], cots[...]).astype(BF16)
+
+
+def feed_out_kernel(ids, act, *refs):
+    weights = refs[:8]
+    keep, send, down, sems = refs[8:]
+    half = keep.shape[0]
+    width = down.shape[1]
+    run_copies(slot_rows(ids, weights, down, weights[0].shape[0], (act.shape[1], width)), sems)
+    keep[...] = nn(act[0:half, :], down[...])
+    send[...] = nn(act[half:, :], down[...]).astype(BF16)
+
+
+def norm_back(hidden, scale, d_normed):
+    inverse = lax.rsqrt(jnp.mean(hidden * hidden, axis=1, keepdims=True) + EPS)
+    y = hidden * inverse
+    d_y = d_normed * scale
+    d_hidden = inverse * (d_y - y * jnp.mean(d_y * y, axis=1, keepdims=True))
+    return d_hidden, d_normed * y
+
+
+def norm_back_kernel(hidden, scale, part, other, base, base_y, utt, low_out, sums_out):
+    tok = hidden.shape[0] // 2
+    for f in range(2):
+        rows, swap = pl.ds(f * tok, tok), pl.ds((1 - f) * tok, tok)
+        d_normed = part[rows, :].astype(F32) + other[swap, :].astype(F32)
+        d_hidden, d_scale = norm_back(hidden[rows, :].astype(F32), scale[rows, :], d_normed)
+        added = (base, base_y)[f][...].astype(F32) + d_hidden
+        low_out[rows, :] = added.astype(low_out.dtype)
+        if f == 0:
+            sums_out[...] = nn(utt[...], d_scale.astype(BF16))
+
+
+def d_attended_kernel(ids, d_h, d_h_c, weight, packed, wide, sems):
+    tok = packed.shape[1]
+    run_copies(out_rows(ids, weight, wide), sems)
+    for f in range(4):
+        rows = pl.ds((f % 2) * tok, tok)
+        part = nt((d_h, d_h_c)[f // 2][rows, :], wide[...]).astype(BF16)
+        group = ids[1] ^ ORDER[f]
+        for pair in range(2):
+            packed[2 * group + pair] = part[:, pair * 128 : (pair + 1) * 128]
+
+
+def qkv_back_kernel(ids, blocks, *refs):
+    weights = refs[:8]
+    keep, send, joined, wide, sems = refs[8:]
+    tok = blocks.shape[1]
+    pairs = attended_pairs(ids, blocks, joined, tok, 3)
+    run_copies(pairs + slot_rows(ids, weights, wide, weights[0].shape[0]), sems)
+    half = keep.shape[0]
+    keep[...] = nt(joined[0:half, :], wide[...])
+    send[...] = nt(joined[half:, :], wide[...]).astype(BF16)
+
+
+def qkv_grad_kernel(ids, normed, joined, d_h, d_h_c, a0, a1, a2, a3, even, odd, attended, sems):
+    tok = a0.shape[0] // 4
+    half = d_h.shape[0]
+    pairs = []
+    for q, piece in enumerate((a0, a1, a2, a3)):
+        for f in range(4):
+            for pair in range(2):
+                pairs.append(
+                    (
+                        piece.at[pl.ds(ORDER[ORDER[f] ^ q] * tok, tok), pl.ds(pair * 128, 128)],
+                        attended.at[pl.ds(f * tok, tok), aligned((ids[1] ^ q) + 4 * pair, 128)],
+                    )
+                )
+    run_copies(pairs, sems)
+    cols = joined.shape[1]
+    mine = aligned(ids[1], 256)
+    for r in range(8):
+        block = aligned(ids[0] ^ r, 128)
+        target = (even, odd)[r % 2]
+        target[r // 2, :, 0:cols] = tn(normed[:, block], joined[...]).astype(BF16)
+        target[r // 2, :, cols:] = (
+            tn(attended[0:half, block], d_h[:, mine]) + tn(attended[half:, block], d_h_c[:, mine])
+        ).astype(BF16)
+
+
+def skip_back_kernel(ids, *refs):
+    d_h, d_h_c, inputs, weights = refs[0], refs[1], refs[2:6], refs[6:14]
+    even, odd, keep, send, held, wide, sems = refs[14:]
+    tok = inputs[0].shape[0]
+    pairs = [(x, held.at[pl.ds(f * tok, tok), :]) for f, x in enumerate(inputs)]
+    run_copies(pairs + slot_rows(ids, weights, wide, weights[0].shape[0]), sems)
+    mine = aligned(ids[1], 256)
+    near, far = d_h[:, mine], d_h_c[:, mine]
+    half = 2 * tok
+    for r in range(8):
+        block = aligned(ids[0] ^ r, 256)
+        target = (even, odd)[r % 2]
+        target[r // 2] = (tn(held[0:half, block], near) + tn(held[half:, block], far)).astype(BF16)
+    keep[...] = nt(near, wide[...])
+    send[...] = nt(far, wide[...]).astype(BF16)
+
+
+def spread_kernel(ids, *refs):
+    qkv_o, out_o, up_o, down_o, skip_o = refs[12:]
+    for q in range(4):
+        part = ids[1] ^ q
+        qkv_out, feed, skip = refs[q], refs[4 + q], refs[8 + q]
+        for block in range(6):
+            qkv_o[:, aligned(4 * block + part, 128)] = qkv_out[:, pl.ds(block * 128, 128)].astype(F32)
+        out_o[:, aligned(part, 256)] = qkv_out[:, pl.ds(768, 256)].astype(F32)
+        for block in range(8):
+            up_o[:, aligned(4 * block + part, 128)] = feed[:, pl.ds(block * 128, 128)].astype(F32)
+        down_o[aligned(part, 128), :] = feed[:, pl.ds(1024, 1024)].astype(F32)
+        skip_o[:, aligned(part, 256)] = skip[...].astype(F32)
+
+
+def gather_slots(piece):
+    near = [piece] + [from_seq(piece, 2 * k) for k in range(1, 4)]
+    out = []
+    for array in near:
+        out += [array, from_seq(array, 1)]
+    return out
+
+
+def gather_groups(piece):
+    along_y = from_grp(piece, 2)
+    return [piece, along_y, from_grp(piece, 1), from_grp(along_y, 1)]
+
+
+def scatter_slots(even, odd):
+    arrived = from_seq(odd, 1)
+    parts = [
+        (even[k].astype(F32) + arrived[k].astype(F32)).astype(BF16) for k in range(4)
+    ]
+    total = parts[0].astype(F32)
+    for k in range(1, 4):
+        total = total + from_seq(parts[k], 2 * k).astype(F32)
+    return total.astype(BF16)
+
+
+def halves_sum(keep, send):
+    return (keep + from_grp(send, 1).astype(F32)).astype(BF16)
+
+
+def exchange(array, cols):
+    return lax.all_to_all(array, "seq", 0, 0, tiled=True)
+
+
+def tp_body(
+    hidden_in, skips, lengths, times, skip_weight, cond_weight, qkv_weight, out_weight,
+    up_weight, down_weight, cotangent,
+):
+    tok, width = hidden_in.shape
+    ff = up_weight.shape[1]
+    frames = 8 * tok
+    slot = lax.axis_index("seq")
+    part = lax.axis_index("grp")
+    ids = jnp.stack([slot, part]).astype(jnp.int32)
+    sem = pltpu.SemaphoreType.DMA
+
+    def columns(weight, blocks, size):
+        rows = weight.shape[0]
+        split = weight.reshape(rows, blocks, 4, size)
+        return lax.dynamic_index_in_dim(split, part, 2, keepdims=False).reshape(rows, blocks * size)
+
+    w_skip = gather_slots(columns(skip_weight, 1, 256))
+    inputs_own = jnp.concatenate([hidden_in, skips], axis=1)
+    x_y = from_grp(inputs_own, 2)
+    inputs = [inputs_own, x_y, from_grp(inputs_own, 1), from_grp(x_y, 1)]
+
+    half_width = width // 2
+    freqs = jnp.exp(-math.log(10000.0) * jnp.arange(half_width, dtype=F32) / half_width)
+    angles = times[0].astype(F32)[:, None] * freqs[None, :]
+    emb = jnp.concatenate([jnp.sin(angles), jnp.cos(angles)], axis=1).astype(BF16)
+    rows_here = cond_weight.shape[0]
+    emb_here = lax.dynamic_slice_in_dim(emb, slot * rows_here, rows_here, 1)
+    utts = emb.shape[0]
+    cond_part = matmul(emb_here, cond_weight)
+    note = jnp.zeros((1, 2 * width), F32).at[0, :utts].set(lengths[0].astype(F32))
+    told = lax.all_gather(jnp.concatenate([cond_part, note], axis=0), ("grp", "seq"), axis=0)
+    told = told.reshape(4, 8, utts + 1, 2 * width)
+    cond_all = jnp.sum(told[:, :, :utts], axis=1)
+    lengths_all = told[:, 0, utts, :utts].astype(jnp.int32)
+    ends_all = jnp.cumsum(lengths_all, axis=1)
+
+    frame_here = slot * tok + jnp.arange(tok, dtype=jnp.int32)
+
+    def scale_rows(f, cond_cols):
+        group = part ^ ORDER[f]
+        ends = lax.dynamic_index_in_dim(ends_all, group, 0, keepdims=False)
+        owner = owner_of(frame_here, ends)
+        rows = lax.dynamic_index_in_dim(cond_all, group, 0, keepdims=False)[:, cond_cols]
+        onehot = owner[:, None] == jnp.arange(utts, dtype=jnp.int32)[None, :]
+        picked = 1.0 + jnp.dot(onehot.astype(F32), rows, precision=lax.Precision.HIGHEST)
+        return picked, onehot
+
+    attn_cols, ffn_cols = slice(0, width), slice(width, 2 * width)
+    scaled = [scale_rows(f, attn_cols) for f in range(4)]
+    scale_attn = jnp.concatenate([pair[0] for pair in scaled], axis=0)
+    scale_ffn = jnp.concatenate([scale_rows(f, ffn_cols)[0] for f in range(2)], axis=0)
+    utt_rows = scaled[0][1].astype(BF16).T
+
+    my_ends = lax.dynamic_index_in_dim(ends_all, slot // 2, 0, keepdims=False)
+    my_lengths = lax.dynamic_index_in_dim(lengths_all, slot // 2, 0, keepdims=False)
+    all_frames = jnp.arange(frames, dtype=jnp.int32)
+    owner_all = owner_of(all_frames, my_ends)
+    own_hot = owner_all[:, None] == jnp.arange(utts, dtype=jnp.int32)[None, :]
+    begins = jnp.sum(jnp.where(own_hot, (my_ends - my_lengths)[None, :], 0), axis=1)
+    positions = (all_frames - begins).astype(F32)
+    inverse = jnp.exp(-math.log(10000.0) * jnp.arange(32, dtype=F32) / 32)
+    turn_angles = positions[:, None] * inverse[None, :]
+    cos_half, sin_half = jnp.cos(turn_angles), jnp.sin(turn_angles)
+    cosine = jnp.concatenate([cos_half] * 4, axis=1)
+    sine = jnp.concatenate([-sin_half, sin_half] * 2, axis=1)
+    owner_col, owner_row = owner_all[:, None], owner_all[None, :]
+
+    w_qkv = gather_slots(columns(qkv_weight, 6, 128))
+    out_rows_all = lax.all_gather(out_weight, "seq", axis=0, tiled=True)
+    w_feed = gather_slots(
+        jnp.concatenate(
+            [columns(up_weight, 8, 128), lax.dynamic_slice_in_dim(down_weight, part * 128, 128, 0)],
+            axis=1,
+        )
+    )
+    cots = gather_groups(cotangent)
+
+    (h_cols,) = call(
+        h_zero_kernel,
+        [sds((4 * tok, 256), BF16)],
+        [SMEM] + [ANY] * 12,
+        [pltpu.VMEM((4 * tok, 2 * width), BF16), pltpu.VMEM((2 * width, 256), BF16), sem((12,))],
+        [ids] + inputs + w_skip,
+        flops=2 * 4 * tok * 2 * width * 256,
+    )
+    h_pieces = gather_groups(h_cols)
+    h_pieces = [h_pieces[0], h_pieces[2], h_pieces[1], h_pieces[3]]
+    normed, h_zero, packed = call(
+        qkv_kernel,
+        [sds((4 * tok, width), BF16), sds((2 * tok, width), BF16), sds((8, tok, 384), BF16)],
+        [SMEM] + [ANY] * 4 + [VMEM] + [ANY] * 8,
+        [pltpu.VMEM((4 * tok, width), BF16), pltpu.VMEM((width, 768), BF16), sem((24,))],
+        [ids] + h_pieces + [scale_attn] + w_qkv,
+        flops=2 * 4 * tok * width * 768,
+    )
+    qkv = exchange(packed, 384)
+    mixed, log_total = call(
+        attend_kernel,
+        [sds((8, tok, 128), BF16), sds((2, frames), F32)],
+        [VMEM] * 5,
+        [],
+        [qkv, cosine, sine, owner_col, owner_row],
+        flops=2 * 2 * 2 * frames * frames * 64 * 2,
+    )
+    attended_blocks = exchange(mixed, 128)
+    keep, send, attended = call(
+        project_kernel,
+        [sds((2 * tok, width), F32), sds((2 * tok, width), BF16), sds((4 * tok, 256), BF16)],
+        [SMEM, ANY, ANY],
+        [pltpu.VMEM((256, width), BF16), sem((10,))],
+        [ids, attended_blocks, out_rows_all],
+        flops=2 * 4 * tok * width * 256,
+    )
+    h_part = halves_sum(keep, send)
+    h_one, normed_two = call(
+        residual_kernel,
+        [sds((2 * tok, width), F32), sds((2 * tok, width), BF16)],
+        [VMEM] * 4,
+        [],
+        [h_zero, h_part, from_grp(h_part, 2), scale_ffn],
+    )
+    normed_two_c = from_grp(normed_two, 1)
+    quarter = ff // 4
+    feed_scratch = [
+        pltpu.VMEM((width, quarter), BF16),
+        pltpu.VMEM((quarter, width), BF16),
+        pltpu.VMEM((4 * tok, width), BF16),
+        pltpu.VMEM((4 * tok, width), BF16),
+        sem((22,)),
+    ]
+    act, d_pre, keep, send = call(
+        feed_kernel,
+        [
+            sds((4 * tok, quarter), BF16),
+            sds((4 * tok, quarter), BF16),
+            sds((2 * tok, width), F32),
+            sds((2 * tok, width), BF16),
+        ],
+        [SMEM] + [ANY] * 14,
+        feed_scratch,
+        [ids, normed_two, normed_two_c] + cots + w_feed,
+        flops=3 * 2 * 4 * tok * width * quarter,
+    )
+
+    d_part = halves_sum(keep, send)
+    d_h_one, sums_ffn = call(
+        norm_back_kernel,
+        [sds((2 * tok, width), BF16), sds((utts, width), F32)],
+        [VMEM] * 7,
+        [],
+        [h_one, scale_ffn, d_part, from_grp(d_part, 2), cots[0], cots[1], utt_rows],
+    )
+    d_h_one_c = from_grp(d_h_one, 1)
+    (d_att_packed,) = call(
+        d_attended_kernel,
+        [sds((8, tok, 128), BF16)],
+        [SMEM, VMEM, VMEM, ANY],
+        [pltpu.VMEM((256, width), BF16), sem((2,))],
+        [ids, d_h_one, d_h_one_c, out_rows_all],
+        flops=2 * 4 * tok * width * 256,
+    )
+    d_att = exchange(d_att_packed, 128)
+
+    out_keep, out_send = call(
+        feed_out_kernel,
+        [sds((2 * tok, width), F32), sds((2 * tok, width), BF16)],
+        [SMEM, VMEM] + [ANY] * 8,
+        [pltpu.VMEM((quarter, width), BF16), sem((8,))],
+        [ids, act] + w_feed,
+        flops=2 * 4 * tok * width * quarter,
+    )
+    out_part = halves_sum(out_keep, out_send)
+    block_out = (
+        h_one[:tok] + out_part[:tok].astype(F32) + from_grp(out_part[tok:], 2).astype(F32)
+    ).astype(BF16)
+    feed_even, feed_odd = call(
+        feed_grad_kernel,
+        [sds((4, 128, 2 * width), BF16)] * 2,
+        [SMEM] + [ANY] * 6 + [VMEM] * 2,
+        feed_scratch[2:4] + [sem((6,))],
+        [ids, normed_two, normed_two_c] + cots + [act, d_pre],
+        flops=2 * 2 * 4 * tok * width * quarter,
+    )
+    feed_grads = gather_groups(scatter_slots(feed_even, feed_odd))
+    att_pieces = gather_groups(attended)
+
+    (d_packed,) = call(
+        attend_back_kernel,
+        [sds((8, tok, 384), BF16)],
+        [VMEM] * 7,
+        [pltpu.VMEM((frames, 128), F32), pltpu.VMEM((frames, 128), F32)],
+        [qkv, d_att, cosine, sine, owner_col, owner_row, log_total],
+        flops=5 * 2 * 2 * frames * frames * 64 * 2,
+    )
+    d_qkv_blocks = exchange(d_packed, 384)
+    keep, send, d_qkv = call(
+        qkv_back_kernel,
+        [sds((2 * tok, width), F32), sds((2 * tok, width), BF16), sds((4 * tok, 768), BF16)],
+        [SMEM] + [ANY] * 9,
+        [pltpu.VMEM((width, 768), BF16), sem((32,))],
+        [ids, d_qkv_blocks] + w_qkv,
+        flops=2 * 4 * tok * width * 768,
+    )
+    d_part = halves_sum(keep, send)
+    d_h_zero, sums_attn = call(
+        norm_back_kernel,
+        [sds((2 * tok, width), BF16), sds((utts, width), F32)],
+        [VMEM] * 7,
+        [],
+        [h_zero, scale_attn[: 2 * tok], d_part, from_grp(d_part, 2), d_h_one[:tok], d_h_one[tok:], utt_rows],
+    )
+    qkv_even, qkv_odd = call(
+        qkv_grad_kernel,
+        [sds((4, 128, 1024), BF16)] * 2,
+        [SMEM] + [VMEM] * 4 + [ANY] * 4,
+        [pltpu.VMEM((4 * tok, width), BF16), sem((32,))],
+        [ids, normed, d_qkv, d_h_one, d_h_one_c, att_pieces[0], att_pieces[2], att_pieces[1], att_pieces[3]],
+        flops=2 * 4 * tok * width * 1024,
+    )
+    d_h_zero_c = from_grp(d_h_zero, 1)
+    skip_even, skip_odd, in_keep, in_send = call(
+        skip_back_kernel,
+        [sds((4, 256, 256), BF16)] * 2 + [sds((2 * tok, 2 * width), F32), sds((2 * tok, 2 * width), BF16)],
+        [SMEM, VMEM, VMEM] + [ANY] * 12,
+        [pltpu.VMEM((4 * tok, 2 * width), BF16), pltpu.VMEM((2 * width, 256), BF16), sem((12,))],
+        [ids, d_h_zero, d_h_zero_c] + inputs + w_skip,
+        flops=2 * 2 * 4 * tok * 2 * width * 256,
+    )
+    skip_grads = gather_groups(scatter_slots(skip_even, skip_odd))
+    qkv_grads = gather_groups(scatter_slots(qkv_even, qkv_odd))
+    in_part = halves_sum(in_keep, in_send)
+    in_both = (in_part[:tok].astype(F32) + from_grp(in_part[tok:], 2).astype(F32)).astype(BF16)
+
+    emb_sums = jnp.concatenate([sums_attn, sums_ffn], axis=1)
+    sums_all = lax.all_gather(emb_sums, ("grp", "seq"), axis=0).reshape(4, 8, utts, 2 * width)
+    sums_all = jnp.sum(sums_all, axis=1)
+    emb_all = lax.all_gather(emb_here, "grp", axis=0)
+    cond_grad = contract(
+        emb_all.reshape(4 * utts, rows_here), sums_all.reshape(4 * utts, 2 * width).astype(BF16), 0, 0
+    )
+
+    def by_mask(pieces):
+        return [pieces[0], pieces[2], pieces[1], pieces[3]]
+
+    qkv_grad, out_grad, up_grad, down_grad, skip_grad_w = call(
+        spread_kernel,
+        [
+            sds((128, 3 * width), F32),
+            sds((128, width), F32),
+            sds((128, ff), F32),
+            sds((ff // 8, width), F32),
+            sds((256, width), F32),
+        ],
+        [SMEM] + [VMEM] * 12,
+        [],
+        [ids] + by_mask(qkv_grads) + by_mask(feed_grads) + by_mask(skip_grads),
+    )
+    return (
+        block_out, in_both[:, :width], in_both[:, width:], skip_grad_w, cond_grad, qkv_grad,
+        out_grad, up_grad, down_grad,
     )
 
 
@@ -324,6 +1011,7 @@
         P("seq", None),
         P(("grp", "seq"), None),
     )
+    body = tp_body if (mesh.shape["grp"], mesh.shape["seq"]) == (4, 8) else plain_body
     return jax.shard_map(
         body,
         mesh=mesh,

time: 2140 us -> 510 us (0.24)
  waiting for transfers between devices: 1940 us -> 207 us
  starting transfers between devices: 1.39 us -> 117 us
  matrix products: 104 us -> 4.98 us
  Pallas kernels: 0 us -> 65.9 us
  local copies, waits for them, and re-layouts: 19.9 us -> 44.1 us
    reduce_scatter x7 -> x0, waiting for transfers between devices: 1250 us -> none  [the longest x1 283 us: body(): lax.psum_scatter(grad_down, 'seq', scatter_dimension=0, tiled=True)]
    all_gather x8 -> x3, waiting for transfers between devices: 604 us -> 19.9 us  [the longest x1 19.9 us: tp_body(): lax.all_gather(jnp.concatenate([cond_part, note], axis=0), ('grp', 'seq')...]
    ppermute x0 -> x67, waiting for transfers between devices: none -> 158 us  [the longest x33 117 us: from_seq(): return lax.ppermute(array, 'seq', swapped('seq', mask, 8))]
    ppermute x0 -> x67, starting transfers between devices: none -> 96.5 us  [the longest x34 64.8 us: from_grp(): return lax.ppermute(array, 'grp', swapped('grp', mask, 4))]
    psum x1 -> x0, waiting for transfers between devices: 79.9 us -> none  [body(): lax.psum(shards[0].astype(jnp.bfloat16), 'grp').astype(jnp.float32)]
    pallas_call x0 -> x16, Pallas kernels: none -> 65.9 us  [call(): pl.pallas_call(kernel, out_shape=tuple(out_shapes), in_specs=in_specs, ou...]
    dot_general x13 -> x1, matrix products: 56.8 us -> 1.31 us  [contract(): lax.dot_general(left, right, (((left_dim,), (right_dim,)), ((), ())), pre...]
    all_to_all x0 -> x3, waiting for transfers between devices: none -> 28.9 us  [exchange(): return lax.all_to_all(array, 'seq', 0, 0, tiled=True)]
  transfers between devices with their start and end apart: 16 -> 73, of which waited for: 16 -> 29; matrix products, arithmetic and copies ran while one was open for 5% -> 7% of each run, Pallas kernels for 0% -> 9%
where the time goes in v1:
time: 510 us; the launch traced here: 500 us
  waiting for transfers between devices  207 us (41%)
  starting transfers between devices  117 us (23%)
  Pallas kernels  65.9 us (13%)
  local copies, waits for them, and re-layouts  44.1 us (9%)
  other arithmetic  26.7 us (5%)
  blocking collectives  18.7 us (4%)
  between operations  15.1 us (3%)
    ppermute x33, waiting for transfers between devices, from_seq(): return lax.ppermute(array, 'seq', swapped('seq', mask, 8))  117 us
    pallas_call x16, Pallas kernels, call(): pl.pallas_call(kernel, out_shape=tuple(out_shapes), in_specs=in_specs, ou...  65.9 us
    ppermute x34, starting transfers between devices, from_grp(): return lax.ppermute(array, 'grp', swapped('grp', mask, 4))  64.8 us
    ppermute x34, waiting for transfers between devices, from_grp(): return lax.ppermute(array, 'grp', swapped('grp', mask, 4))  41 us
    unnamed x166, local copies, waits for them, and re-layouts  33 us
    ppermute x33, starting transfers between devices, from_seq(): return lax.ppermute(array, 'seq', swapped('seq', mask, 8))  31.7 us
    all_to_all x3, waiting for transfers between devices, exchange(): return lax.all_to_all(array, 'seq', 0, 0, tiled=True)  28.9 us
    all_to_all x3, starting transfers between devices, exchange(): return lax.all_to_all(array, 'seq', 0, 0, tiled=True)  20.7 us
  transfers between devices with their start and end apart: 73, of which 29 were waited for; matrix products, arithmetic and copies ran while one was open for 7% of the time, Pallas kernels for 9%

profile of v1, /device:TPU:9, one launch (start us, length us, event | category | flops | bytes accessed | tf_op | source)
XLA Modules:
  0.0 500.1 jit_solution(17652651331713547394)
XLA Ops:
  35.4 6.0 %collective-permute-done.14.refs_7_.refs_2_ = bf16[128,768]{1,0:T(8,128)(2,1)} collective-permute-done((bf16[128,768]{1,0:T(8,128)(2,1)}, bf16[128,768]{1,0:T(8,128)(2,1)}, u32[]{:S(2)}, u32[]{:S(2)}) %collective-permute-start.14) | collective-permute-done | bytes 196640 | tf_op jit(solution)/shard_map/ppermute | solution.py:333
  46.1 12.6 %collective-permute-done.18.refs_11_.refs_6_ = bf16[128,768]{1,0:T(8,128)(2,1)} collective-permute-done((bf16[128,768]{1,0:T(8,128)(2,1)}, bf16[128,768]{1,0:T(8,128)(2,1)}, u32[]{:S(2)}, u32[]{:S(2)}) %collective-permute-start.18) | collective-permute-done | bytes 196640 | tf_op jit(solution)/shard_map/ppermute | solution.py:333
  70.4 19.9 %all-gather.12.cloned.1.call-done = f32[32,9,2048]{2,1,0:T(8,128)} async-done(((f32[1,9,2048]{2,1,0:T(8,128)}), f32[32,9,2048]{2,1,0:T(8,128)}) %all-gather.12.cloned.1.call-update) | async-done | bytes 2359312 | tf_op jit(solution)/shard_map/all_gather | solution.py:767
  98.2 4.7 shard_map.179
  105.7 6.5 %all-to-all-start = ((bf16[8,128,384]{2,1,0:T(8,128)(2,1)}), bf16[8,128,384]{2,1,0:T(8,128)(2,1)}, u32[]{:S(2)}, u32[]{:S(2)}) async-start(bf16[8,128,384]{2,1,0:T(8,128)(2,1)} %copy-done.14), calls=%async_computation | async-start | bytes 1572864 | tf_op jit(solution)/shard_map/all_to_all | solution.py:733
  117.8 20.8 %all-to-all-done.qkv = bf16[8,128,384]{2,1,0:T(8,128)(2,1)} async-done(((bf16[8,128,384]{2,1,0:T(8,128)(2,1)}), bf16[8,128,384]{2,1,0:T(8,128)(2,1)}, u32[]{:S(2)}, u32[]{:S(2)}) %all-to-all-start) | async-done | bytes 786464 | tf_op jit(solution)/shard_map/all_to_all | solution.py:733
  141.8 7.1 %shard_map.180 = (bf16[8,128,128]{2,1,0:T(8,128)(2,1)S(1)}, f32[2,1024]{1,0:T(2,128)S(1)}) custom-call(bf16[8,128,384]{2,1,0:T(8,128)(2,1)} %all-to-all-done.qkv, f32[1024,128]{1,0:T(8,128)S(1)} %copy-done.16, f32[1024,128]{1,0:T(8,128)S(1)} %copy-done.18, s32[1024,1]{1,0:T(8,128)S(1)} %copy-done.26, s32[1,1024]{1,0:T(1,128)S(1)} %bitcast.94), custom_call_target="tpu_custom_call" | custom-call | flops 1073741824 | bytes 2113536 | tf_op jit(solution)/shard_map/pallas_call | solution.py:351
  150.2 8.6 %all-to-all-start.1 = ((bf16[8,128,128]{2,1,0:T(8,128)(2,1)}), bf16[8,128,128]{2,1,0:T(8,128)(2,1)S(1)}, u32[]{:S(2)}, u32[]{:S(2)}) async-start(bf16[8,128,128]{2,1,0:T(8,128)(2,1)} %copy-done.44), calls=%async_computation.1 | async-start | bytes 524288 | tf_op jit(solution)/shard_map/all_to_all | solution.py:733
  158.8 5.6 %all-to-all-done.1.blocks = bf16[8,128,128]{2,1,0:T(8,128)(2,1)S(1)} async-done(((bf16[8,128,128]{2,1,0:T(8,128)(2,1)}), bf16[8,128,128]{2,1,0:T(8,128)(2,1)S(1)}, u32[]{:S(2)}, u32[]{:S(2)}) %all-to-all-start.1) | async-done | bytes 262176 | tf_op jit(solution)/shard_map/all_to_all | solution.py:733
  184.3 8.3 %collective-permute-done.21.other = bf16[256,1024]{1,0:T(8,128)(2,1)S(1)} collective-permute-done((bf16[256,1024]{1,0:T(8,128)(2,1)S(1)}, bf16[256,1024]{1,0:T(8,128)(2,1)S(1)}, u32[]{:S(2)}, u32[]{:S(2)}) %collective-permute-start.21) | collective-permute-done | bytes 524320 | tf_op jit(solution)/shard_map/ppermute | solution.py:337
  194.3 7.8 %collective-permute-done.27.refs_8_.refs_2_ = bf16[128,2048]{1,0:T(8,128)(2,1)S(1)} collective-permute-done((bf16[128,2048]{1,0:T(8,128)(2,1)S(1)}, bf16[128,2048]{1,0:T(8,128)(2,1)S(1)}, u32[]{:S(2)}, u32[]{:S(2)}) %collective-permute-start.27) | collective-permute-done | bytes 524320 | tf_op jit(solution)/shard_map/ppermute | solution.py:333
  205.5 22.8 %collective-permute-done.31.refs_12_.refs_6_ = bf16[128,2048]{1,0:T(8,128)(2,1)S(1)} collective-permute-done((bf16[128,2048]{1,0:T(8,128)(2,1)S(1)}, bf16[128,2048]{1,0:T(8,128)(2,1)S(1)}, u32[]{:S(2)}, u32[]{:S(2)}) %collective-permute-start.31) | collective-permute-done | bytes 524320 | tf_op jit(solution)/shard_map/ppermute | solution.py:333
  232.6 7.4 %collective-permute-done.32.refs_13_.refs_7_ = bf16[128,2048]{1,0:T(8,128)(2,1)S(1)} collective-permute-done((bf16[128,2048]{1,0:T(8,128)(2,1)S(1)}, bf16[128,2048]{1,0:T(8,128)(2,1)S(1)}, u32[]{:S(2)}, u32[]{:S(2)}) %collective-permute-start.32) | collective-permute-done | bytes 524320 | tf_op jit(solution)/shard_map/ppermute | solution.py:333
  240.8 9.7 %shard_map.183 = (bf16[512,1024]{1,0:T(8,128)(2,1)}, bf16[512,1024]{1,0:T(8,128)(2,1)}, f32[256,1024]{1,0:T(8,128)}, bf16[256,1024]{1,0:T(8,128)(2,1)S(1)}) custom-call(s32[2]{0:T(128)S(1)} %pad_add_fusion.ids, bf16[256,1024]{1,0:T(8,128)(2,1)S(1)} %get-tuple-element.63.refs_0_.normed, bf16[256,1024]{1,0:T(8,128)(2,1)S(1)} %collective-permute-done.22.refs_1_.normed_c, ...), custom_call_target="tpu_custom_call" | custom-call | flops 3221225472 | bytes 9961480 | tf_op jit(solution)/shard_map/pallas_call | solution.py:351
  259.6 11.9 %collective-permute-done.36.other = bf16[256,1024]{1,0:T(8,128)(2,1)S(1)} collective-permute-done((bf16[256,1024]{1,0:T(8,128)(2,1)S(1)}, bf16[256,1024]{1,0:T(8,128)(2,1)S(1)}, u32[]{:S(2)}, u32[]{:S(2)}) %collective-permute-start.36) | collective-permute-done | bytes 524320 | tf_op jit(solution)/shard_map/ppermute | solution.py:337
  277.9 10.0 %all_to_all.20.d_att = bf16[8,128,128]{2,1,0:T(8,128)(2,1)S(1)} all-to-all(bf16[8,128,128]{2,1,0:T(8,128)(2,1)S(1)} %shard_map.186), channel_id=1, replica_groups=mesh['grp'=4,'seq'=8] {'seq'}, dimensions={0} | all-to-all | bytes 524288 | tf_op jit(solution)/shard_map/all_to_all | solution.py:733
  287.9 8.7 %shard_map.187 = bf16[8,128,384]{2,1,0:T(8,128)(2,1)S(1)} custom-call(bf16[8,128,384]{2,1,0:T(8,128)(2,1)} %all-to-all-done.qkv, bf16[8,128,128]{2,1,0:T(8,128)(2,1)S(1)} %all_to_all.20.d_att, f32[1024,128]{1,0:T(8,128)S(1)} %copy-done.17, f32[1024,128]{1,0:T(8,128)S(1)} %copy-done.19, s32[1024,1]{1,0:T(8,128)S(1)} %copy-done.27, s32[1,1024]{1,0:T(1,128)S(1)} %bitcast.95, ...), custom_call_target="tpu_custom_call" | custom-call | flops 2684354560 | bytes 2899968 | tf_op jit(solution)/shard_map/pallas_call | solution.py:351
  297.5 5.6 %all-to-all-start.3 = ((bf16[8,128,384]{2,1,0:T(8,128)(2,1)}), bf16[8,128,384]{2,1,0:T(8,128)(2,1)}, u32[]{:S(2)}, u32[]{:S(2)}) async-start(bf16[8,128,384]{2,1,0:T(8,128)(2,1)} %copy-done.15), calls=%async_computation.3 | async-start | bytes 1572864 | tf_op jit(solution)/shard_map/all_to_all | solution.py:733
  309.8 5.9 %shard_map.192 = (bf16[4,128,2048]{2,1,0:T(8,128)(2,1)}, bf16[4,128,2048]{2,1,0:T(8,128)(2,1)}) custom-call(s32[2]{0:T(128)S(1)} %pad_add_fusion.ids, bf16[256,1024]{1,0:T(8,128)(2,1)S(1)} %copy-done.50, bf16[256,1024]{1,0:T(8,128)(2,1)S(1)} %copy-done.52, bf16[128,1024]{1,0:T(8,128)(2,1)} %c0.1, ...), custom_call_target="tpu_custom_call" | custom-call | flops 2147483648 | bytes 8388616 | tf_op jit(solution)/shard_map/pallas_call | solution.py:351
  329.3 6.2 %collective-permute-done.44.a2 = bf16[512,256]{1,0:T(8,128)(2,1)} collective-permute-done((bf16[512,256]{1,0:T(8,128)(2,1)S(1)}, bf16[512,256]{1,0:T(8,128)(2,1)}, u32[]{:S(2)}, u32[]{:S(2)}) %collective-permute-start.44) | collective-permute-done | bytes 262176 | tf_op jit(solution)/shard_map/ppermute | solution.py:337
  337.8 24.5 %collective-permute-done.53 = bf16[4,128,2048]{2,1,0:T(8,128)(2,1)} collective-permute-done((bf16[4,128,2048]{2,1,0:T(8,128)(2,1)}, bf16[4,128,2048]{2,1,0:T(8,128)(2,1)}, u32[]{:S(2)}, u32[]{:S(2)}) %collective-permute-start.53) | collective-permute-done | bytes 2097184 | tf_op jit(solution)/shard_map/ppermute | solution.py:333
  386.6 6.0 %shard_map.190 = (bf16[4,256,256]{2,1,0:T(8,128)(2,1)S(1)}, bf16[4,256,256]{2,1,0:T(8,128)(2,1)S(1)}, f32[256,2048]{1,0:T(8,128)}, bf16[256,2048]{1,0:T(8,128)(2,1)}) custom-call(s32[2]{0:T(128)S(1)} %pad_add_fusion.ids, bf16[256,1024]{1,0:T(8,128)(2,1)} %get-tuple-element.73.refs_0_, bf16[256,1024]{1,0:T(8,128)(2,1)} %collective-permute-done.40.refs_1_, ...), custom_call_target="tpu_custom_call" | custom-call | flops 1073741824 | bytes 8388616 | tf_op jit(solution)/shard_map/pallas_call | solution.py:351
  394.0 10.1 %collective-permute-done.55 = bf16[128,2048]{1,0:T(8,128)(2,1)} collective-permute-done((bf16[128,2048]{1,0:T(8,128)(2,1)}, bf16[128,2048]{1,0:T(8,128)(2,1)}, u32[]{:S(2)}, u32[]{:S(2)}) %collective-permute-start.55) | collective-permute-done | bytes 524320 | tf_op jit(solution)/shard_map/ppermute | solution.py:333
  404.1 4.1 collective-permute-start.41
  408.2 7.3 %collective-permute-done.56 = bf16[128,2048]{1,0:T(8,128)(2,1)S(1)} collective-permute-done((bf16[128,2048]{1,0:T(8,128)(2,1)}, bf16[128,2048]{1,0:T(8,128)(2,1)S(1)}, u32[]{:S(2)}, u32[]{:S(2)}) %collective-permute-start.56) | collective-permute-done | bytes 524320 | tf_op jit(solution)/shard_map/ppermute | solution.py:333
  422.8 6.0 %collective-permute-done.58.refs_6_ = bf16[128,2048]{1,0:T(8,128)(2,1)S(1)} collective-permute-done((bf16[128,2048]{1,0:T(8,128)(2,1)S(1)}, bf16[128,2048]{1,0:T(8,128)(2,1)S(1)}, u32[]{:S(2)}, u32[]{:S(2)}) %collective-permute-start.58) | collective-permute-done | bytes 524320 | tf_op jit(solution)/shard_map/ppermute | solution.py:337
  435.3 12.1 %collective-permute-start.59 = (bf16[128,2048]{1,0:T(8,128)(2,1)S(1)}, bf16[128,2048]{1,0:T(8,128)(2,1)S(1)}, u32[]{:S(2)}, u32[]{:S(2)}) collective-permute-start(bf16[128,2048]{1,0:T(8,128)(2,1)S(1)} %collective-permute-done.58.refs_6_), channel_id=1, source_target_pairs={{0,8},{8,0},{16,24},{24,16},{1,9},{9,1},{17,25},{25,17},{2,10},{10... | collective-permute-start | bytes 1572872 | tf_op jit(solution)/shard_map/ppermute | solution.py:337
  455.8 4.3 collective-permute-done.62
  463.7 7.1 %collective-permute-start.50 = (bf16[128,1024]{1,0:T(8,128)(2,1)S(1)}, bf16[128,1024]{1,0:T(8,128)(2,1)S(1)}, u32[]{:S(2)}, u32[]{:S(2)}) collective-permute-start(bf16[128,1024]{1,0:T(8,128)(2,1)S(1)} %fusion.9.refs_0_), channel_id=1, source_target_pairs={{0,8},{8,0},{16,24},{24,16},{1,9},{9,1},{17,25},{25,17},{2,10},{10... | collective-permute-start | bytes 786440 | tf_op jit(solution)/shard_map/ppermute | solution.py:337
  470.8 4.1 collective-permute-start.52
  474.9 8.7 %all-gather.1 = bf16[32,128]{1,0:T(8,128)(2,1)S(1)} all-gather(bf16[8,128]{1,0:T(8,128)(2,1)S(1)} %fusion.40), channel_id=3, replica_groups=mesh['grp'=4,'seq'=8] {'grp'}, dimensions={0}, use_global_device_ids=true | all-gather | bytes 10240 | tf_op jit(solution)/shard_map/all_gather | solution.py:973
  485.2 4.1 shard_map.193
  (363 shorter events, 190.8 us)
Async XLA Ops:
  7.2 83.1 %all-gather.12.cloned.1.call-start = ((), (), s32[]{:S(2)}) async-start(), calls=%async_computation.6 | async-start | bytes 4325376 | tf_op jit(solution)/shard_map/all_gather | solution.py:767
  12.0 146.8 %all-gather.8.cloned.1.call-start = ((), (), s32[]{:S(2)}) async-start(), calls=%async_computation.4 | async-start | bytes 2359296 | tf_op jit(solution)/shard_map/all_gather | solution.py:805
  22.2 41.7 %collective-permute-start.1 = (bf16[128,2048]{1,0:T(8,128)(2,1)S(1)}, bf16[128,2048]{1,0:T(8,128)(2,1)S(1)}, u32[]{:S(2)}, u32[]{:S(2)}) collective-permute-start(bf16[128,2048]{1,0:T(8,128)(2,1)S(1)} %constant_dynamic-update-slice_fusion.refs_0_.refs_2_), channel_id=1, source_target_pairs={{0,8},{8,0},{16,24},{24,16},{1,9},{9,1},{17,25},{25,17},{2,10},{10... | collective-permute-start | bytes 1572872 | tf_op jit(solution)/shard_map/ppermute | solution.py:337
  27.8 36.5 %collective-permute-start.2 = (bf16[128,2048]{1,0:T(8,128)(2,1)S(1)}, bf16[128,2048]{1,0:T(8,128)(2,1)S(1)}, u32[]{:S(2)}, u32[]{:S(2)}) collective-permute-start(bf16[128,2048]{1,0:T(8,128)(2,1)S(1)} %collective-permute-done.refs_1_.refs_3_), channel_id=1, source_target_pairs={{0,8},{8,0},{16,24},{24,16},{1,9},{9,1},{17,25},{25,17},{2,10},{10... | collective-permute-start | bytes 1572872 | tf_op jit(solution)/shard_map/ppermute | solution.py:337
  60.3 35.3 %collective-permute-start.13 = (bf16[128,768]{1,0:T(8,128)(2,1)}, bf16[128,768]{1,0:T(8,128)(2,1)}, u32[]{:S(2)}, u32[]{:S(2)}) collective-permute-start(bf16[128,768]{1,0:T(8,128)(2,1)} %copy.72.refs_5_.refs_0_), channel_id=1, source_target_pairs={{0,1},{1,0},{2,3},{3,2},{4,5},{5,4},{6,7},{7,6},{8,9},{9,8},{10,11... | collective-permute-start | bytes 589832 | tf_op jit(solution)/shard_map/ppermute | solution.py:333
  60.7 37.5 %collective-permute-start.15 = (bf16[128,768]{1,0:T(8,128)(2,1)}, bf16[128,768]{1,0:T(8,128)(2,1)}, u32[]{:S(2)}, u32[]{:S(2)}) collective-permute-start(bf16[128,768]{1,0:T(8,128)(2,1)} %collective-permute-done.14.refs_7_.refs_2_), channel_id=1, source_target_pairs={{0,1},{1,0},{2,3},{3,2},{4,5},{5,4},{6,7},{7,6},{8,9},{9,8},{10,11... | collective-permute-start | bytes 589832 | tf_op jit(solution)/shard_map/ppermute | solution.py:333
  62.7 35.4 %collective-permute-start.17 = (bf16[128,768]{1,0:T(8,128)(2,1)}, bf16[128,768]{1,0:T(8,128)(2,1)}, u32[]{:S(2)}, u32[]{:S(2)}) collective-permute-start(bf16[128,768]{1,0:T(8,128)(2,1)} %collective-permute-done.16.refs_9_.refs_4_), channel_id=1, source_target_pairs={{0,1},{1,0},{2,3},{3,2},{4,5},{5,4},{6,7},{7,6},{8,9},{9,8},{10,11... | collective-permute-start | bytes 589832 | tf_op jit(solution)/shard_map/ppermute | solution.py:333
  63.9 34.3 %collective-permute-start.19 = (bf16[128,768]{1,0:T(8,128)(2,1)}, bf16[128,768]{1,0:T(8,128)(2,1)}, u32[]{:S(2)}, u32[]{:S(2)}) collective-permute-start(bf16[128,768]{1,0:T(8,128)(2,1)} %collective-permute-done.18.refs_11_.refs_6_), channel_id=1, source_target_pairs={{0,1},{1,0},{2,3},{3,2},{4,5},{5,4},{6,7},{7,6},{8,9},{9,8},{10,11... | collective-permute-start | bytes 589832 | tf_op jit(solution)/shard_map/ppermute | solution.py:333
  69.1 26.8 %collective-permute-start.11 = (bf16[512,256]{1,0:T(8,128)(2,1)S(1)}, bf16[512,256]{1,0:T(8,128)(2,1)}, u32[]{:S(2)}, u32[]{:S(2)}) collective-permute-start(bf16[512,256]{1,0:T(8,128)(2,1)S(1)} %shard_map.178.refs_0_), channel_id=1, source_target_pairs={{0,16},{8,24},{16,0},{24,8},{1,17},{9,25},{17,1},{25,9},{2,18},{10... | collective-permute-start | bytes 786440 | tf_op jit(solution)/shard_map/ppermute | solution.py:337
  105.7 33.0 %all-to-all-start = ((bf16[8,128,384]{2,1,0:T(8,128)(2,1)}), bf16[8,128,384]{2,1,0:T(8,128)(2,1)}, u32[]{:S(2)}, u32[]{:S(2)}) async-start(bf16[8,128,384]{2,1,0:T(8,128)(2,1)} %copy-done.14), calls=%async_computation | async-start | bytes 1572864 | tf_op jit(solution)/shard_map/all_to_all | solution.py:733
  182.1 46.2 %collective-permute-start.31 = (bf16[128,2048]{1,0:T(8,128)(2,1)S(1)}, bf16[128,2048]{1,0:T(8,128)(2,1)S(1)}, u32[]{:S(2)}, u32[]{:S(2)}) collective-permute-start(bf16[128,2048]{1,0:T(8,128)(2,1)S(1)} %pad_maximum_fusion.5.refs_6_.refs_0_), channel_id=1, source_target_pairs={{0,6},{1,7},{2,4},{3,5},{4,2},{5,3},{6,0},{7,1},{8,14},{9,15},{10,... | collective-permute-start | bytes 1572872 | tf_op jit(solution)/shard_map/ppermute | solution.py:333
  183.8 46.9 %collective-permute-start.26 = (bf16[128,2048]{1,0:T(8,128)(2,1)S(1)}, bf16[128,2048]{1,0:T(8,128)(2,1)S(1)}, u32[]{:S(2)}, u32[]{:S(2)}) collective-permute-start(bf16[128,2048]{1,0:T(8,128)(2,1)S(1)} %pad_maximum_fusion.5.refs_6_.refs_0_), channel_id=1, source_target_pairs={{0,1},{1,0},{2,3},{3,2},{4,5},{5,4},{6,7},{7,6},{8,9},{9,8},{10,11... | collective-permute-start | bytes 1572872 | tf_op jit(solution)/shard_map/ppermute | solution.py:333
  192.6 36.5 %collective-permute-start.24 = (bf16[128,1024]{1,0:T(8,128)(2,1)}, bf16[128,1024]{1,0:T(8,128)(2,1)S(1)}, u32[]{:S(2)}, u32[]{:S(2)}) collective-permute-start(bf16[128,1024]{1,0:T(8,128)(2,1)} %c0.1), channel_id=1, source_target_pairs={{0,8},{8,0},{16,24},{24,16},{1,9},{9,1},{17,25},{25,17},{2,10},{10... | collective-permute-start | bytes 786440 | tf_op jit(solution)/shard_map/ppermute | solution.py:337
  202.1 30.6 %collective-permute-start.28 = (bf16[128,2048]{1,0:T(8,128)(2,1)S(1)}, bf16[128,2048]{1,0:T(8,128)(2,1)S(1)}, u32[]{:S(2)}, u32[]{:S(2)}) collective-permute-start(bf16[128,2048]{1,0:T(8,128)(2,1)S(1)} %collective-permute-done.27.refs_8_.refs_2_), channel_id=1, source_target_pairs={{0,1},{1,0},{2,3},{3,2},{4,5},{5,4},{6,7},{7,6},{8,9},{9,8},{10,11... | collective-permute-start | bytes 1572872 | tf_op jit(solution)/shard_map/ppermute | solution.py:333
  204.9 27.8 %collective-permute-start.30 = (bf16[128,2048]{1,0:T(8,128)(2,1)S(1)}, bf16[128,2048]{1,0:T(8,128)(2,1)S(1)}, u32[]{:S(2)}, u32[]{:S(2)}) collective-permute-start(bf16[128,2048]{1,0:T(8,128)(2,1)S(1)} %collective-permute-done.29.refs_10_.refs_4_), channel_id=1, source_target_pairs={{0,1},{1,0},{2,3},{3,2},{4,5},{5,4},{6,7},{7,6},{8,9},{9,8},{10,11... | collective-permute-start | bytes 1572872 | tf_op jit(solution)/shard_map/ppermute | solution.py:333
  303.1 187.2 %all-gather.10.cloned.1.call-start = ((), (), s32[]{:S(2)}) async-start(), calls=%async_computation.5 | async-start | bytes 2162688 | tf_op jit(solution)/shard_map/all_gather | solution.py:971
  315.6 46.7 %collective-permute-start.53 = (bf16[4,128,2048]{2,1,0:T(8,128)(2,1)}, bf16[4,128,2048]{2,1,0:T(8,128)(2,1)}, u32[]{:S(2)}, u32[]{:S(2)}) collective-permute-start(bf16[4,128,2048]{2,1,0:T(8,128)(2,1)} %get-tuple-element.83), channel_id=1, source_target_pairs={{0,1},{1,0},{2,3},{3,2},{4,5},{5,4},{6,7},{7,6},{8,9},{9,8},{10,11... | collective-permute-start | bytes 6291464 | tf_op jit(solution)/shard_map/ppermute | solution.py:333
  328.9 45.0 %collective-permute-start.43 = (bf16[512,256]{1,0:T(8,128)(2,1)S(1)}, bf16[512,256]{1,0:T(8,128)(2,1)}, u32[]{:S(2)}, u32[]{:S(2)}) collective-permute-start(bf16[512,256]{1,0:T(8,128)(2,1)S(1)} %copy-done.54), channel_id=1, source_target_pairs={{0,8},{8,0},{16,24},{24,16},{1,9},{9,1},{17,25},{25,17},{2,10},{10... | collective-permute-start | bytes 786440 | tf_op jit(solution)/shard_map/ppermute | solution.py:337
  335.5 38.5 %collective-permute-start.45 = (bf16[512,256]{1,0:T(8,128)(2,1)}, bf16[512,256]{1,0:T(8,128)(2,1)}, u32[]{:S(2)}, u32[]{:S(2)}) collective-permute-start(bf16[512,256]{1,0:T(8,128)(2,1)} %collective-permute-done.44.a2), channel_id=1, source_target_pairs={{0,8},{8,0},{16,24},{24,16},{1,9},{9,1},{17,25},{25,17},{2,10},{10... | collective-permute-start | bytes 786440 | tf_op jit(solution)/shard_map/ppermute | solution.py:337
  336.5 33.7 %collective-permute-start.39 = (bf16[256,1024]{1,0:T(8,128)(2,1)S(1)}, bf16[256,1024]{1,0:T(8,128)(2,1)S(1)}, u32[]{:S(2)}, u32[]{:S(2)}) collective-permute-start(bf16[256,1024]{1,0:T(8,128)(2,1)S(1)} %add_convert_fusion.6.part), channel_id=1, source_target_pairs={{0,16},{8,24},{16,0},{24,8},{1,17},{9,25},{17,1},{25,9},{2,18},{10... | collective-permute-start | bytes 1572872 | tf_op jit(solution)/shard_map/ppermute | solution.py:337
  365.3 27.4 %collective-permute-start.54 = (bf16[128,2048]{1,0:T(8,128)(2,1)}, bf16[128,2048]{1,0:T(8,128)(2,1)}, u32[]{:S(2)}, u32[]{:S(2)}) collective-permute-start(bf16[128,2048]{1,0:T(8,128)(2,1)} %get-tuple-element.97), channel_id=1, source_target_pairs={{0,2},{1,3},{2,0},{3,1},{4,6},{5,7},{6,4},{7,5},{8,10},{9,11},{10,... | collective-permute-start | bytes 1572872 | tf_op jit(solution)/shard_map/ppermute | solution.py:333
  366.2 37.9 %collective-permute-start.55 = (bf16[128,2048]{1,0:T(8,128)(2,1)}, bf16[128,2048]{1,0:T(8,128)(2,1)}, u32[]{:S(2)}, u32[]{:S(2)}) collective-permute-start(bf16[128,2048]{1,0:T(8,128)(2,1)} %get-tuple-element.99), channel_id=1, source_target_pairs={{0,4},{1,5},{2,6},{3,7},{4,0},{5,1},{6,2},{7,3},{8,12},{9,13},{10,... | collective-permute-start | bytes 1572872 | tf_op jit(solution)/shard_map/ppermute | solution.py:333
  373.9 41.6 %collective-permute-start.56 = (bf16[128,2048]{1,0:T(8,128)(2,1)}, bf16[128,2048]{1,0:T(8,128)(2,1)S(1)}, u32[]{:S(2)}, u32[]{:S(2)}) collective-permute-start(bf16[128,2048]{1,0:T(8,128)(2,1)} %get-tuple-element.98), channel_id=1, source_target_pairs={{0,6},{1,7},{2,4},{3,5},{4,2},{5,3},{6,0},{7,1},{8,14},{9,15},{10,... | collective-permute-start | bytes 1572872 | tf_op jit(solution)/shard_map/ppermute | solution.py:333
  382.2 36.6 %collective-permute-start.46 = (bf16[4,128,1024]{2,1,0:T(8,128)(2,1)S(1)}, bf16[4,128,1024]{2,1,0:T(8,128)(2,1)S(1)}, u32[]{:S(2)}, u32[]{:S(2)}) collective-permute-start(bf16[4,128,1024]{2,1,0:T(8,128)(2,1)S(1)} %get-tuple-element.80), channel_id=1, source_target_pairs={{0,1},{1,0},{2,3},{3,2},{4,5},{5,4},{6,7},{7,6},{8,9},{9,8},{10,11... | collective-permute-start | bytes 3145736 | tf_op jit(solution)/shard_map/ppermute | solution.py:333
  386.2 33.0 %collective-permute-start.33 = (bf16[256,1024]{1,0:T(8,128)(2,1)S(1)}, bf16[256,1024]{1,0:T(8,128)(2,1)S(1)}, u32[]{:S(2)}, u32[]{:S(2)}) collective-permute-start(bf16[256,1024]{1,0:T(8,128)(2,1)S(1)} %get-tuple-element.66), channel_id=1, source_target_pairs={{0,8},{8,0},{16,24},{24,16},{1,9},{9,1},{17,25},{25,17},{2,10},{10... | collective-permute-start | bytes 1572872 | tf_op jit(solution)/shard_map/ppermute | solution.py:337
  392.6 29.9 %collective-permute-start.60 = (bf16[4,256,256]{2,1,0:T(8,128)(2,1)S(1)}, bf16[4,256,256]{2,1,0:T(8,128)(2,1)S(1)}, u32[]{:S(2)}, u32[]{:S(2)}) collective-permute-start(bf16[4,256,256]{2,1,0:T(8,128)(2,1)S(1)} %get-tuple-element.85), channel_id=1, source_target_pairs={{0,1},{1,0},{2,3},{3,2},{4,5},{5,4},{6,7},{7,6},{8,9},{9,8},{10,11... | collective-permute-start | bytes 1572872 | tf_op jit(solution)/shard_map/ppermute | solution.py:333
  404.1 50.8 %collective-permute-start.41 = (bf16[256,2048]{1,0:T(8,128)(2,1)}, bf16[256,2048]{1,0:T(8,128)(2,1)S(1)}, u32[]{:S(2)}, u32[]{:S(2)}) collective-permute-start(bf16[256,2048]{1,0:T(8,128)(2,1)} %get-tuple-element.75), channel_id=1, source_target_pairs={{0,8},{8,0},{16,24},{24,16},{1,9},{9,1},{17,25},{25,17},{2,10},{10... | collective-permute-start | bytes 3145736 | tf_op jit(solution)/shard_map/ppermute | solution.py:337
  422.5 27.7 %collective-permute-start.49 = (bf16[128,1024]{1,0:T(8,128)(2,1)S(1)}, bf16[128,1024]{1,0:T(8,128)(2,1)S(1)}, u32[]{:S(2)}, u32[]{:S(2)}) collective-permute-start(bf16[128,1024]{1,0:T(8,128)(2,1)S(1)} %get-tuple-element.101), channel_id=1, source_target_pairs={{0,6},{1,7},{2,4},{3,5},{4,2},{5,3},{6,0},{7,1},{8,14},{9,15},{10,... | collective-permute-start | bytes 786440 | tf_op jit(solution)/shard_map/ppermute | solution.py:333
  428.8 33.7 %collective-permute-start.34 = (bf16[128,1024]{1,0:T(8,128)(2,1)S(1)}, bf16[128,1024]{1,0:T(8,128)(2,1)S(1)}, u32[]{:S(2)}, u32[]{:S(2)}) collective-permute-start(bf16[128,1024]{1,0:T(8,128)(2,1)S(1)} %slice.191), channel_id=1, source_target_pairs={{0,16},{8,24},{16,0},{24,8},{1,17},{9,25},{17,1},{25,9},{2,18},{10... | collective-permute-start | bytes 786440 | tf_op jit(solution)/shard_map/ppermute | solution.py:337
  430.1 33.6 %collective-permute-start.57 = (bf16[128,2048]{1,0:T(8,128)(2,1)S(1)}, bf16[128,2048]{1,0:T(8,128)(2,1)S(1)}, u32[]{:S(2)}, u32[]{:S(2)}) collective-permute-start(bf16[128,2048]{1,0:T(8,128)(2,1)S(1)} %fusion.2.refs_4_), channel_id=1, source_target_pairs={{0,8},{8,0},{16,24},{24,16},{1,9},{9,1},{17,25},{25,17},{2,10},{10... | collective-permute-start | bytes 1572872 | tf_op jit(solution)/shard_map/ppermute | solution.py:337
  435.3 48.3 %collective-permute-start.59 = (bf16[128,2048]{1,0:T(8,128)(2,1)S(1)}, bf16[128,2048]{1,0:T(8,128)(2,1)S(1)}, u32[]{:S(2)}, u32[]{:S(2)}) collective-permute-start(bf16[128,2048]{1,0:T(8,128)(2,1)S(1)} %collective-permute-done.58.refs_6_), channel_id=1, source_target_pairs={{0,8},{8,0},{16,24},{24,16},{1,9},{9,1},{17,25},{25,17},{2,10},{10... | collective-permute-start | bytes 1572872 | tf_op jit(solution)/shard_map/ppermute | solution.py:337
  462.0 27.3 %collective-permute-start.42 = (bf16[128,2048]{1,0:T(8,128)(2,1)S(1)}, bf16[128,2048]{1,0:T(8,128)(2,1)S(1)}, u32[]{:S(2)}, u32[]{:S(2)}) collective-permute-start(bf16[128,2048]{1,0:T(8,128)(2,1)S(1)} %slice.193), channel_id=1, source_target_pairs={{0,16},{8,24},{16,0},{24,8},{1,17},{9,25},{17,1},{25,9},{2,18},{10... | collective-permute-start | bytes 1572872 | tf_op jit(solution)/shard_map/ppermute | solution.py:337
  (122 other events, 1323.4 us)
Sparse Core Ops, SparseCore 0:
  12.1 78.2 all-gather.11
  92.5 55.6 all-gather.7
  374.0 80.1 all-gather.9

commit v2 on v1

--- a/solution.py
+++ b/solution.py
@@ -1,3 +1,4 @@
+import functools
 import math
 
 import jax
@@ -319,9 +320,11 @@
 
 ORDER = (0, 2, 1, 3)
 BF16 = jnp.bfloat16
+VMEM_MIB = 63
 F32 = jnp.float32
 ANY = pl.BlockSpec(memory_space=pl.ANY)
 VMEM = pl.BlockSpec(memory_space=pltpu.VMEM)
+HBM = pl.BlockSpec(memory_space=pltpu.HBM)
 SMEM = pl.BlockSpec(memory_space=pltpu.SMEM)
 
 
@@ -345,18 +348,25 @@
         copy.wait()
 
 
-def call(kernel, out_shapes, in_specs, scratch, args, flops=0, vmem_mib=48):
+def call(kernel, out_shapes, in_specs, scratch, args, deps=(), out_spec=VMEM, cost_us=0.0):
     moved = sum(a.size * a.dtype.itemsize for a in args)
     moved += sum(o.size * o.dtype.itemsize for o in out_shapes)
+    given, extra = len(args), len(deps)
+
+    def with_deps(*refs):
+        kernel(*refs[:given], *refs[given + extra :])
+
     return pl.pallas_call(
-        kernel,
+        with_deps,
         out_shape=tuple(out_shapes),
-        in_specs=in_specs,
-        out_specs=(VMEM,) * len(out_shapes),
+        in_specs=list(in_specs) + [ANY] * extra,
+        out_specs=(out_spec,) * len(out_shapes),
         scratch_shapes=scratch,
-        compiler_params=pltpu.CompilerParams(vmem_limit_bytes=vmem_mib * 1024 * 1024),
-        cost_estimate=pl.CostEstimate(flops=flops, bytes_accessed=moved, transcendentals=0),
-    )(*args)
+        compiler_params=pltpu.CompilerParams(vmem_limit_bytes=VMEM_MIB * 1024 * 1024),
+        cost_estimate=pl.CostEstimate(
+            flops=int(cost_us * 1.15e9), bytes_accessed=0, transcendentals=0
+        ),
+    )(*args, *deps)
 
 
 def sds(shape, dtype):
@@ -379,29 +389,33 @@
     return jnp.dot(left, right, preferred_element_type=F32)
 
 
-def slot_rows(ids, pieces, dst, rows, lanes=None):
-    out = []
-    for r, piece in enumerate(pieces):
-        src = piece if lanes is None else piece.at[:, pl.ds(*lanes)]
-        out.append((src, dst.at[aligned(ids[0] ^ r, rows), :]))
-    return out
-
-
-def h_zero_kernel(ids, *refs):
-    inputs, weights = refs[:4], refs[4:12]
-    out, held, wide, sems = refs[12:]
-    tok = inputs[0].shape[0]
-    pairs = [(x, held.at[pl.ds(f * tok, tok), :]) for f, x in enumerate(inputs)]
-    run_copies(pairs + slot_rows(ids, weights, wide, weights[0].shape[0]), sems)
-    out[...] = nn(held[...], wide[...]).astype(BF16)
+def frame_blocks(ids, blocks, dst):
+    tok = blocks.shape[1]
+    return [(blocks.at[ids[1] ^ ORDER[f]], dst.at[pl.ds(f * tok, tok), :]) for f in range(4)]
+
+
+def h_zero_kernel(ids, inputs, near, far, notes, out, whole, held, wide, shares, sems):
+    rows = wide.shape[0] // 8
+    frames = held.shape[0]
+    pairs = frame_blocks(ids, inputs, held)
+    for r in range(8):
+        piece = (near, far)[r % 2].at[pl.ds((r // 2) * rows, rows), :]
+        pairs.append((piece, wide.at[aligned(ids[0] ^ r, rows), :]))
+    for k, pieces in enumerate((near, far)):
+        pairs.append((pieces.at[pl.ds(4 * rows, 64), :], shares.at[k]))
+    run_copies(pairs, sems)
+    out[0:frames, :] = nn(held[...], wide[...]).astype(BF16)
+    out[frames : frames + 64, :] = (shares[0].astype(F32) + shares[1].astype(F32)).astype(BF16)
+    out[frames + 64 :, :] = notes[...]
+    whole[...] = wide[...]
 
 
 def qkv_kernel(ids, *refs):
-    pieces, scale, weights = refs[:4], refs[4], refs[5:13]
-    normed_out, hidden_out, packed, held, wide, sems = refs[13:]
+    pieces, weight = refs[:4], refs[4]
+    normed_out, hidden_out, packed, told, held, raw, sems = refs[5:]
     tok = packed.shape[1]
     cols = pieces[0].shape[1]
-    pairs = []
+    pairs = [(pieces[ORDER[f]].at[pl.ds(4 * tok, 80), :], raw.at[f]) for f in range(4)]
     for q in range(4):
         for f in range(4):
             pairs.append(
@@ -410,16 +424,23 @@
                     held.at[pl.ds(f * tok, tok), aligned(ids[1] ^ q, cols)],
                 )
             )
-    run_copies(pairs + slot_rows(ids, weights, wide, weights[0].shape[0]), sems)
+    run_copies(pairs, sems)
+    for f in range(4):
+        rows = raw[f].astype(F32)
+        told[f, 0:8, :] = unpacked_rows(rows[0:64])
+        counts = jnp.concatenate(
+            [32.0 * rows[64:65] + rows[65:66], 32.0 * rows[66:67] + rows[67:68], jnp.zeros((6, cols), F32)], axis=0
+        )
+        told[f, 8:16, :] = jnp.concatenate([counts, jnp.zeros((8, told.shape[2] - cols), F32)], axis=1)
     for f in range(4):
         rows = pl.ds(f * tok, tok)
         hidden = held[rows, :].astype(F32)
         inverse = lax.rsqrt(jnp.mean(hidden * hidden, axis=1, keepdims=True) + EPS)
-        normed = (hidden * inverse * scale[rows, :]).astype(BF16)
+        normed = (hidden * inverse * scale_of(ids, told.at[f], tok, 0, hidden.shape[1])).astype(BF16)
         normed_out[rows, :] = normed
         if f < 2:
             hidden_out[rows, :] = held[rows, :]
-        qkv = nn(normed, wide[...]).astype(BF16)
+        qkv = nn(normed, weight[...]).astype(BF16)
         group = ids[1] ^ ORDER[f]
         for pair in range(2):
             for part in range(3):
@@ -447,14 +468,29 @@
     return low_q, low_k
 
 
-def attend_kernel(qkv, cosine, sine, owner_col, owner_row, out, log_out):
-    total = owner_col.shape[0]
+def owners_of(ids, told, total):
+    utts = told.shape[1] // 2
+    group = ids[1] ^ (ids[0] >> 1)
+    lens = jnp.zeros((2 * utts, utts), F32)
+    for f in range(4):
+        lens = lens + jnp.where(group == ORDER[f], told[f, :, 0:utts], 0.0)
+    _, end, _, end_col = utt_bounds(lens, utts)
+    down = lax.broadcasted_iota(jnp.int32, (total, utts), 0).astype(F32)
+    across = lax.broadcasted_iota(jnp.int32, (utts, total), 1).astype(F32)
+    col = jnp.sum(jnp.where(down >= end, 1.0, 0.0), axis=1, keepdims=True)
+    row = jnp.sum(jnp.where(across >= end_col, 1.0, 0.0), axis=0, keepdims=True)
+    return col, row
+
+
+def attend_kernel(ids, qkv, cosine, sine, told, out, log_out, owner_row):
+    total = cosine.shape[0]
+    owner_col, owner_row[...] = owners_of(ids, told, total)
     tok = qkv.shape[1]
     queries, keys = rotated(qkv, cosine, sine)
     values = qkv[:, :, 256:384].reshape(total, 128)
     for chunk in range(total // CHUNK):
         rows = slice(chunk * CHUNK, (chunk + 1) * CHUNK)
-        same = owner_col[...] == owner_row[:, rows]
+        same = owner_col == owner_row[:, rows]
         both = []
         for head in range(2):
             lanes = slice(64 * head, 64 * head + 64)
@@ -471,9 +507,10 @@
 
 
 def attend_back_kernel(
-    qkv, d_att, cosine, sine, owner_col, owner_row, log_total, out, d_keys, d_values
+    ids, qkv, d_att, cosine, sine, log_total, told, out, d_keys, d_values, owner_row
 ):
-    total = owner_col.shape[0]
+    total = cosine.shape[0]
+    owner_col, owner_row[...] = owners_of(ids, told, total)
     tok = qkv.shape[1]
     queries, keys = rotated(qkv, cosine, sine)
     values = qkv[:, :, 256:384].reshape(total, 128)
@@ -481,7 +518,7 @@
     keys_t = [keys[:, 64 * head : 64 * head + 64].astype(F32).T.astype(BF16) for head in range(2)]
     for chunk in range(total // CHUNK):
         rows = slice(chunk * CHUNK, (chunk + 1) * CHUNK)
-        same = owner_col[...] == owner_row[:, rows]
+        same = owner_col == owner_row[:, rows]
         d_queries, k_terms, v_terms = [], [], []
         for head in range(2):
             lanes = slice(64 * head, 64 * head + 64)
@@ -524,83 +561,205 @@
     return pairs
 
 
-def out_rows(ids, weight, dst):
-    return [
-        (weight.at[aligned(ids[1], 128), :], dst.at[pl.ds(0, 128), :]),
-        (weight.at[aligned(ids[1] + 4, 128), :], dst.at[pl.ds(128, 128), :]),
-    ]
-
-
-def project_kernel(ids, blocks, weight, keep, send, attended, wide, sems):
+def packed_rows(wide):
+    return jnp.concatenate([wide[:, k : k + 256] for k in range(0, wide.shape[1], 256)], axis=0)
+
+
+def unpacked_rows(rows):
+    return jnp.concatenate([rows[k : k + 8] for k in range(0, rows.shape[0], 8)], axis=1)
+
+
+def cut_skip_kernel(ids, weight, emb, cond_weight, piece):
+    rows = weight.shape[0]
+    piece[0:rows, :] = weight[:, aligned(ids[1], piece.shape[1])]
+    piece[rows:, :] = packed_rows(nn(emb[...], cond_weight[...])).astype(BF16)
+
+
+def gather_kernel(p0, p1, p2, p3, out):
+    rows = (out.shape[0] - 64) // 4
+    total = jnp.zeros((64, out.shape[1]), F32)
+    for k, piece in enumerate((p0, p1, p2, p3)):
+        out[k * rows : (k + 1) * rows, :] = piece[0:rows, :]
+        total = total + piece[rows:, :].astype(F32)
+    out[4 * rows :, :] = total.astype(BF16)
+
+
+def join_kernel(left, right, joined):
+    width = left.shape[1]
+    for k in range(joined.shape[0]):
+        joined[k, :, 0:width] = left[...]
+        joined[k, :, width:] = right[...]
+
+
+def near_kernel(even, odd, *outs):
+    for k, out in enumerate(outs):
+        out[...] = (even[k].astype(F32) + odd[k].astype(F32)).astype(BF16)
+
+
+def add_kernel(left, right, out, held, sem):
+    held[...] = (left[...].astype(F32) + right[...].astype(F32)).astype(out.dtype)
+    copy = pltpu.make_async_copy(held, out, sem)
+    copy.start()
+    copy.wait()
+
+
+def add_twice_kernel(left, right, out, again):
+    total = (left[...].astype(F32) + right[...].astype(F32)).astype(out.dtype)
+    out[...] = total
+    again[...] = total
+
+
+def add_three_kernel(first, second, third, out):
+    total = first[...].astype(F32) + second[...].astype(F32) + third[...].astype(F32)
+    out[...] = total.astype(out.dtype)
+
+
+def pick_kernel(ids, own, near, far, farther, out):
+    z, y = ids[0] >> 1, ids[1] >> 1
+    rows = own.shape[0]
+    low = z >> 1
+    source = (z & 1) == y
+    first, second = aligned(low, rows), aligned(1 - low, rows)
+
+    @pl.when(source)
+    def _():
+        out[first, :] = own[...]
+        out[second, :] = far[...]
+
+    @pl.when(jnp.logical_not(source))
+    def _():
+        out[first, :] = near[...]
+        out[second, :] = farther[...]
+
+
+def copy_kernel(source, out):
+    out[...] = source[...]
+
+
+def stack_kernel(*refs):
+    out = refs[-1]
+    for k, ref in enumerate(refs[:-1]):
+        out[k] = ref[...]
+
+
+def cut_qkv_kernel(ids, qkv, piece):
+    for block in range(piece.shape[1] // 128):
+        piece[:, pl.ds(block * 128, 128)] = qkv[:, aligned(4 * block + ids[1], 128)]
+
+
+def cut_feed_kernel(ids, up, down, piece, sem):
+    fetch = pltpu.make_async_copy(down.at[aligned(ids[1], 128), :], piece.at[:, up.shape[1] // 4 :], sem)
+    fetch.start()
+    for block in range(up.shape[1] // 512):
+        piece[:, pl.ds(block * 128, 128)] = up[:, aligned(4 * block + ids[1], 128)]
+    fetch.wait()
+
+
+def utt_bounds(told, utts):
+    row = lax.broadcasted_iota(jnp.int32, (utts, utts), 0)
+    col = lax.broadcasted_iota(jnp.int32, (utts, utts), 1)
+    lens = told[utts : utts + 1, 0:utts]
+    spread = jnp.broadcast_to(lens, (utts, utts))
+    lens_col = jnp.sum(jnp.where(row == col, spread, 0.0), axis=1, keepdims=True)
+    ends = jnp.sum(jnp.where(row <= col, lens_col, 0.0), axis=0, keepdims=True)
+    ends_col = jnp.sum(jnp.where(col <= row, spread, 0.0), axis=1, keepdims=True)
+    return ends - lens, ends, ends_col - lens_col, ends_col
+
+
+def scale_of(ids, told, tok, first_col, width):
+    utts = told.shape[0] // 2
+    begin, end, _, _ = utt_bounds(told, utts)
+    frame = (ids[0] * tok + lax.broadcasted_iota(jnp.int32, (tok, utts), 0)).astype(F32)
+    onehot = jnp.where((frame >= begin) & (frame < end), 1.0, 0.0).astype(BF16)
+    cond = told[0:utts, first_col : first_col + width]
+    high = cond.astype(BF16)
+    rest = cond - high.astype(F32)
+    low = rest.astype(BF16)
+    return 1.0 + (nn(onehot, high) + nn(onehot, low))
+
+
+def utt_picks(ids, told, tok):
+    utts = told.shape[0] // 2
+    _, _, begin, end = utt_bounds(told, utts)
+    frame = (ids[0] * tok + lax.broadcasted_iota(jnp.int32, (utts, tok), 1)).astype(F32)
+    return jnp.where((frame >= begin) & (frame < end), 1.0, 0.0).astype(BF16)
+
+
+def project_kernel(ids, blocks, picked, over, keep, send, attended, weight, sems):
     tok = blocks.shape[1]
-    run_copies(attended_pairs(ids, blocks, attended, tok, 1) + out_rows(ids, weight, wide), sems)
-    keep[...] = nn(attended[0 : 2 * tok, :], wide[...])
-    send[...] = nn(attended[2 * tok :, :], wide[...]).astype(BF16)
-
-
-def residual_kernel(hidden, part, other, scale, h_one_out, normed_out):
+    mine = (ids[0] & 1) == (ids[1] & 1)
+
+    @pl.when(mine)
+    def _():
+        run_copies([(picked, weight)], sems.at[pl.ds(8, 1)])
+
+    @pl.when(jnp.logical_not(mine))
+    def _():
+        run_copies([(over, weight)], sems.at[pl.ds(8, 1)])
+
+    run_copies(attended_pairs(ids, blocks, attended, tok, 1), sems)
+    keep[...] = nn(attended[0 : 2 * tok, :], weight[...])
+    send[...] = nn(attended[2 * tok :, :], weight[...]).astype(BF16)
+
+
+def residual_kernel(ids, hidden, part, other, told, h_one_out, normed_out):
     tok = hidden.shape[0] // 2
     for f in range(2):
         rows, swap = pl.ds(f * tok, tok), pl.ds((1 - f) * tok, tok)
         h_one = hidden[rows, :].astype(F32) + part[rows, :].astype(F32) + other[swap, :].astype(F32)
         inverse = lax.rsqrt(jnp.mean(h_one * h_one, axis=1, keepdims=True) + EPS)
         h_one_out[rows, :] = h_one
-        normed_out[rows, :] = (h_one * inverse * scale[rows, :]).astype(BF16)
+        scale = scale_of(ids, told.at[f], tok, h_one.shape[1], h_one.shape[1])
+        normed_out[rows, :] = (h_one * inverse * scale).astype(BF16)
 
 
 def gelu_parts(pre):
-    half = 0.5 * (1.0 + lax.erf(pre * (2.0**-0.5)))
-    slope = half + pre * jnp.exp(-0.5 * pre * pre) * ((2.0 * math.pi) ** -0.5)
-    return pre * half, slope
+    size = jnp.abs(pre)
+    decay = jnp.exp(-0.5 * pre * pre)
+    t = 1.0 / (1.0 + (0.3275911 * 2.0**-0.5) * size)
+    series = t * (0.254829592 + t * (-0.284496736 + t * (1.421413741 + t * (-1.453152027 + t * 1.061405429))))
+    tail = 0.5 * series * decay
+    half = jnp.where(pre < 0.0, tail, 1.0 - tail)
+    return pre * half, half + pre * decay * ((2.0 * math.pi) ** -0.5)
 
 
 def feed_kernel(ids, *refs):
-    normed, normed_c, cot = refs[0], refs[1], refs[2:6]
-    weights = refs[6:14]
-    act_out, d_pre_out, keep, send, up, down, held, cots, sems = refs[14:]
-    tok = cot[0].shape[0]
-    rows = weights[0].shape[0]
-    hidden = up.shape[1]
-    pairs = [(normed, held.at[pl.ds(0, 2 * tok), :]), (normed_c, held.at[pl.ds(2 * tok, 2 * tok), :])]
-    pairs += [(g, cots.at[pl.ds(f * tok, tok), :]) for f, g in enumerate(cot)]
-    pairs += slot_rows(ids, weights, up, rows, (0, hidden))
-    pairs += slot_rows(ids, weights, down, rows, (hidden, down.shape[1]))
-    run_copies(pairs, sems)
+    normed, normed_c, cots, weight = refs[0], refs[1], refs[2:6], refs[6]
+    act_out, d_pre_out, keep, send = refs[7:]
+    tok = cots[0].shape[0]
+    hidden = act_out.shape[1]
     for f in range(4):
         block = pl.ds(f * tok, tok)
-        pre = nn(held[block, :], up[...])
+        rows = pl.ds((f % 2) * tok, tok)
+        pre = nn((normed, normed_c)[f // 2][rows, :], weight[:, 0:hidden])
         act, slope = gelu_parts(pre)
         act_out[block, :] = act.astype(BF16)
-        d_pre = (nt(cots[block, :], down[...]) * slope).astype(BF16)
+        d_pre = (nt(cots[f][...], weight[:, hidden:]) * slope).astype(BF16)
         d_pre_out[block, :] = d_pre
-        d_normed = nt(d_pre, up[...])
+        d_normed = nt(d_pre, weight[:, 0:hidden])
         if f < 2:
             keep[block, :] = d_normed
         else:
-            send[pl.ds((f - 2) * tok, tok), :] = d_normed.astype(BF16)
-
-
-def feed_grad_kernel(ids, normed, normed_c, c0, c1, c2, c3, act, d_pre, even, odd, held, cots, sems):
+            send[rows, :] = d_normed.astype(BF16)
+
+
+def feed_grad_kernel(normed, normed_c, c0, c1, c2, c3, act, d_pre, out, held, cots, sems):
     tok = c0.shape[0]
     pairs = [(normed, held.at[pl.ds(0, 2 * tok), :]), (normed_c, held.at[pl.ds(2 * tok, 2 * tok), :])]
-    pairs += [(g, cots.at[pl.ds(f * tok, tok), :]) for f, g in enumerate((c0, c1, c2, c3))]
+    pairs += [(cot, cots.at[pl.ds(f * tok, tok), :]) for f, cot in enumerate((c0, c1, c2, c3))]
     run_copies(pairs, sems)
     cols = act.shape[1]
     for r in range(8):
-        block = aligned(ids[0] ^ r, 128)
-        target = (even, odd)[r % 2]
-        target[r // 2, :, 0:cols] = tn(held[:, block], d_pre[...]).astype(BF16)
-        target[r // 2, :, cols:] = tn(act[:, block], cots[...]).astype(BF16)
-
-
-def feed_out_kernel(ids, act, *refs):
-    weights = refs[:8]
-    keep, send, down, sems = refs[8:]
+        block = pl.ds(r * 128, 128)
+        out[block, 0:cols] = tn(held[:, block], d_pre[...]).astype(BF16)
+        out[block, cols:] = tn(act[:, block], cots[...]).astype(BF16)
+
+
+def feed_out_kernel(act, weight, keep, send):
     half = keep.shape[0]
-    width = down.shape[1]
-    run_copies(slot_rows(ids, weights, down, weights[0].shape[0], (act.shape[1], width)), sems)
-    keep[...] = nn(act[0:half, :], down[...])
-    send[...] = nn(act[half:, :], down[...]).astype(BF16)
+    hidden = act.shape[1]
+    keep[...] = nn(act[0:half, :], weight[:, hidden:])
+    send[...] = nn(act[half:, :], weight[:, hidden:]).astype(BF16)
 
 
 def norm_back(hidden, scale, d_normed):
@@ -611,41 +770,39 @@
     return d_hidden, d_normed * y
 
 
-def norm_back_kernel(hidden, scale, part, other, base, base_y, utt, low_out, sums_out):
+def norm_back_kernel(first_col, ids, hidden, part, other, base, base_y, told, low_out, sums_out):
     tok = hidden.shape[0] // 2
+    width = hidden.shape[1]
     for f in range(2):
         rows, swap = pl.ds(f * tok, tok), pl.ds((1 - f) * tok, tok)
         d_normed = part[rows, :].astype(F32) + other[swap, :].astype(F32)
-        d_hidden, d_scale = norm_back(hidden[rows, :].astype(F32), scale[rows, :], d_normed)
+        scale = scale_of(ids, told.at[f], tok, first_col, width)
+        d_hidden, d_scale = norm_back(hidden[rows, :].astype(F32), scale, d_normed)
         added = (base, base_y)[f][...].astype(F32) + d_hidden
         low_out[rows, :] = added.astype(low_out.dtype)
         if f == 0:
-            sums_out[...] = nn(utt[...], d_scale.astype(BF16))
-
-
-def d_attended_kernel(ids, d_h, d_h_c, weight, packed, wide, sems):
+            sums_out[...] = nn(utt_picks(ids, told.at[0], tok), d_scale.astype(BF16))
+
+
+def d_attended_kernel(ids, d_h, d_h_c, weight, packed):
     tok = packed.shape[1]
-    run_copies(out_rows(ids, weight, wide), sems)
     for f in range(4):
         rows = pl.ds((f % 2) * tok, tok)
-        part = nt((d_h, d_h_c)[f // 2][rows, :], wide[...]).astype(BF16)
+        part = nt((d_h, d_h_c)[f // 2][rows, :], weight[...]).astype(BF16)
         group = ids[1] ^ ORDER[f]
         for pair in range(2):
             packed[2 * group + pair] = part[:, pair * 128 : (pair + 1) * 128]
 
 
-def qkv_back_kernel(ids, blocks, *refs):
-    weights = refs[:8]
-    keep, send, joined, wide, sems = refs[8:]
+def qkv_back_kernel(ids, blocks, weight, keep, send, joined, sems):
     tok = blocks.shape[1]
-    pairs = attended_pairs(ids, blocks, joined, tok, 3)
-    run_copies(pairs + slot_rows(ids, weights, wide, weights[0].shape[0]), sems)
+    run_copies(attended_pairs(ids, blocks, joined, tok, 3), sems)
     half = keep.shape[0]
-    keep[...] = nt(joined[0:half, :], wide[...])
-    send[...] = nt(joined[half:, :], wide[...]).astype(BF16)
-
-
-def qkv_grad_kernel(ids, normed, joined, d_h, d_h_c, a0, a1, a2, a3, even, odd, attended, sems):
+    send[...] = nt(joined[half:, :], weight[...]).astype(BF16)
+    keep[...] = nt(joined[0:half, :], weight[...])
+
+
+def qkv_grad_kernel(ids, normed, joined, d_h, d_h_c, a0, a2, a1, a3, even, odd, attended, sems):
     tok = a0.shape[0] // 4
     half = d_h.shape[0]
     pairs = []
@@ -661,7 +818,7 @@
     run_copies(pairs, sems)
     cols = joined.shape[1]
     mine = aligned(ids[1], 256)
-    for r in range(8):
+    for r in (1, 3, 5, 7, 0, 2, 4, 6):
         block = aligned(ids[0] ^ r, 128)
         target = (even, odd)[r % 2]
         target[r // 2, :, 0:cols] = tn(normed[:, block], joined[...]).astype(BF16)
@@ -670,43 +827,86 @@
         ).astype(BF16)
 
 
-def skip_back_kernel(ids, *refs):
-    d_h, d_h_c, inputs, weights = refs[0], refs[1], refs[2:6], refs[6:14]
-    even, odd, keep, send, held, wide, sems = refs[14:]
-    tok = inputs[0].shape[0]
-    pairs = [(x, held.at[pl.ds(f * tok, tok), :]) for f, x in enumerate(inputs)]
-    run_copies(pairs + slot_rows(ids, weights, wide, weights[0].shape[0]), sems)
+def skip_back_kernel(ids, d_h, d_h_c, inputs, sums_attn, sums_ffn, even, odd, sums, held, sems):
+    tok = inputs.shape[1]
+    run_copies(frame_blocks(ids, inputs, held), sems)
     mine = aligned(ids[1], 256)
     near, far = d_h[:, mine], d_h_c[:, mine]
     half = 2 * tok
-    for r in range(8):
+    for r in (1, 3, 5, 7, 0, 2, 4, 6):
         block = aligned(ids[0] ^ r, 256)
-        target = (even, odd)[r % 2]
-        target[r // 2] = (tn(held[0:half, block], near) + tn(held[half:, block], far)).astype(BF16)
-    keep[...] = nt(near, wide[...])
-    send[...] = nt(far, wide[...]).astype(BF16)
-
-
-def spread_kernel(ids, *refs):
-    qkv_o, out_o, up_o, down_o, skip_o = refs[12:]
+        grad = (tn(held[0:half, block], near) + tn(held[half:, block], far)).astype(BF16)
+        if r % 2:
+            odd[(r // 2) * 256 : (r // 2) * 256 + 256, :] = grad
+        else:
+            even[r // 2] = grad
+    low = packed_rows(jnp.concatenate([sums_attn[...], sums_ffn[...]], axis=1)).astype(BF16)
+    odd[1024:, :] = low
+    sums[...] = low
+
+
+def skip_near_kernel(even, sums, arrived, *outs):
+    both = (sums[...].astype(F32) + arrived[1024:, :].astype(F32)).astype(BF16)
+    for k, out in enumerate(outs):
+        out[0:256, :] = (even[k].astype(F32) + arrived[k * 256 : (k + 1) * 256, :].astype(F32)).astype(BF16)
+        out[256:, :] = both
+
+
+def in_back_kernel(ids, d_h, near, far, in_out, skip_out):
+    tok, width = in_out.shape
+    total = jnp.zeros((tok, 2 * width), F32)
+    for q in range(4):
+        weight = (near, far)[q % 2].at[q // 2]
+        total = total + nt(d_h[0:tok, aligned(ids[1] ^ q, 256)], weight[...])
+    in_out[...] = total[:, 0:width].astype(BF16)
+    skip_out[...] = total[:, width:].astype(BF16)
+
+
+def spread_feed_kernel(ids, near, far, up_o, down_o):
+    hidden = near.shape[2] - down_o.shape[1]
     for q in range(4):
         part = ids[1] ^ q
-        qkv_out, feed, skip = refs[q], refs[4 + q], refs[8 + q]
+        feed = (near, far)[q % 2].at[q // 2]
+        for block in range(hidden // 128):
+            up_o[:, aligned(4 * block + part, 128)] = feed[:, pl.ds(block * 128, 128)].astype(F32)
+        down_o[aligned(part, 128), :] = feed[:, hidden:].astype(F32)
+
+
+def last_kernel(p0, p1, p2, p3, q0, q1, q2, q3, out):
+    qkv = q0[...].astype(F32) + q1[...].astype(F32) + q2[...].astype(F32) + q3[...].astype(F32)
+    skip = p0[...].astype(F32) + p1[...].astype(F32) + p2[...].astype(F32) + p3[...].astype(F32)
+    out[:, 0:1024] = qkv.astype(BF16)
+    out[:, 1024:1280] = skip[0:128].astype(BF16)
+    out[:, 1280:1536] = skip[128:256].astype(BF16)
+    out[0:64, 1536:1792] = skip[256:].astype(BF16)
+    out[64:, 1536:1792] = jnp.zeros((64, 256), BF16)
+
+
+def spread_kernel(ids, g0, g1, g2, g3, emb, qkv_o, out_o, skip_o, cond_o):
+    rows = qkv_o.shape[0]
+    utts = emb.shape[0] // 4
+    for q in range(4):
+        part = ids[1] ^ q
+        piece = (g0, g2, g1, g3)[q]
         for block in range(6):
-            qkv_o[:, aligned(4 * block + part, 128)] = qkv_out[:, pl.ds(block * 128, 128)].astype(F32)
-        out_o[:, aligned(part, 256)] = qkv_out[:, pl.ds(768, 256)].astype(F32)
-        for block in range(8):
-            up_o[:, aligned(4 * block + part, 128)] = feed[:, pl.ds(block * 128, 128)].astype(F32)
-        down_o[aligned(part, 128), :] = feed[:, pl.ds(1024, 1024)].astype(F32)
-        skip_o[:, aligned(part, 256)] = skip[...].astype(F32)
-
-
-def gather_slots(piece):
-    near = [piece] + [from_seq(piece, 2 * k) for k in range(1, 4)]
-    out = []
-    for array in near:
-        out += [array, from_seq(array, 1)]
-    return out
+            qkv_o[:, aligned(4 * block + part, 128)] = piece[0:rows, pl.ds(block * 128, 128)].astype(F32)
+        out_o[:, aligned(part, 256)] = piece[0:rows, pl.ds(768, 256)].astype(F32)
+        skip_o[0:rows, aligned(part, 256)] = piece[0:rows, pl.ds(1024, 256)].astype(F32)
+        skip_o[rows:, aligned(part, 256)] = piece[0:rows, pl.ds(1280, 256)].astype(F32)
+    total = jnp.zeros(cond_o.shape, F32)
+    for f in range(4):
+        sums = unpacked_rows((g0, g1, g2, g3)[f][0:64, 1536:1792].astype(F32)).astype(BF16)
+        total = total + tn(emb[f * utts : (f + 1) * utts, :], sums)
+    cond_o[...] = total
+
+
+def stack(arrays, deps=()):
+    shape = (len(arrays),) + arrays[0].shape
+    return call(stack_kernel, [sds(shape, arrays[0].dtype)], [VMEM] * len(arrays), [], list(arrays), deps=deps)[0]
+
+
+def around(piece):
+    return [piece, from_grp(piece, 2), from_grp(piece, 1), from_grp(piece, 3)]
 
 
 def gather_groups(piece):
@@ -714,23 +914,61 @@
     return [piece, along_y, from_grp(piece, 1), from_grp(along_y, 1)]
 
 
-def scatter_slots(even, odd):
+def gather_pairs(piece, deps=()):
+    near = stack([piece, from_grp(piece, 2)], deps)
+    return near, from_grp(near, 1)
+
+
+def scatter_near(even, odd, deps):
     arrived = from_seq(odd, 1)
-    parts = [
-        (even[k].astype(F32) + arrived[k].astype(F32)).astype(BF16) for k in range(4)
-    ]
-    total = parts[0].astype(F32)
-    for k in range(1, 4):
-        total = total + from_seq(parts[k], 2 * k).astype(F32)
-    return total.astype(BF16)
+    return call(near_kernel, [sds(even.shape[1:], BF16)] * 4, [VMEM] * 2, [], [even, arrived], deps=deps)
+
+
+def by_mask(pieces):
+    return [pieces[0], pieces[2], pieces[1], pieces[3]]
 
 
 def halves_sum(keep, send):
-    return (keep + from_grp(send, 1).astype(F32)).astype(BF16)
+    kept, sent = call(
+        add_twice_kernel, [sds(keep.shape, BF16)] * 2, [VMEM] * 2, [], [keep, from_grp(send, 1)]
+    )
+    return kept, from_grp(sent, 2)
+
+
+def add_two(left, right, deps=()):
+    return call(
+        add_kernel,
+        [sds(left.shape, BF16)],
+        [VMEM] * 2,
+        [pltpu.VMEM(left.shape, BF16), pltpu.SemaphoreType.DMA],
+        [left, right],
+        deps=deps,
+        out_spec=HBM,
+    )[0]
 
 
 def exchange(array, cols):
     return lax.all_to_all(array, "seq", 0, 0, tiled=True)
+
+
+def out_moves(mask, keep):
+    pairs = []
+    for t in range(4):
+        for slot in range(8):
+            if keep(slot, t):
+                pairs.append((t * 8 + slot, t * 8 + (slot ^ mask)))
+    return pairs
+
+
+def out_along_z(piece):
+    def holds(slot, t):
+        return (slot & 1) == (t & 1) and ((slot >> 1) & 1) == (t >> 1)
+
+    return [lax.ppermute(piece, ("grp", "seq"), out_moves(2 * k, holds)) for k in range(1, 4)]
+
+
+def out_along_x(rows):
+    return lax.ppermute(rows, ("grp", "seq"), out_moves(1, lambda slot, t: (slot & 1) == (t & 1)))
 
 
 def tp_body(
@@ -745,125 +983,135 @@
     ids = jnp.stack([slot, part]).astype(jnp.int32)
     sem = pltpu.SemaphoreType.DMA
 
-    def columns(weight, blocks, size):
-        rows = weight.shape[0]
-        split = weight.reshape(rows, blocks, 4, size)
-        return lax.dynamic_index_in_dim(split, part, 2, keepdims=False).reshape(rows, blocks * size)
-
-    w_skip = gather_slots(columns(skip_weight, 1, 256))
-    inputs_own = jnp.concatenate([hidden_in, skips], axis=1)
-    x_y = from_grp(inputs_own, 2)
-    inputs = [inputs_own, x_y, from_grp(inputs_own, 1), from_grp(x_y, 1)]
-
     half_width = width // 2
-    freqs = jnp.exp(-math.log(10000.0) * jnp.arange(half_width, dtype=F32) / half_width)
-    angles = times[0].astype(F32)[:, None] * freqs[None, :]
-    emb = jnp.concatenate([jnp.sin(angles), jnp.cos(angles)], axis=1).astype(BF16)
     rows_here = cond_weight.shape[0]
-    emb_here = lax.dynamic_slice_in_dim(emb, slot * rows_here, rows_here, 1)
-    utts = emb.shape[0]
-    cond_part = matmul(emb_here, cond_weight)
-    note = jnp.zeros((1, 2 * width), F32).at[0, :utts].set(lengths[0].astype(F32))
-    told = lax.all_gather(jnp.concatenate([cond_part, note], axis=0), ("grp", "seq"), axis=0)
-    told = told.reshape(4, 8, utts + 1, 2 * width)
-    cond_all = jnp.sum(told[:, :, :utts], axis=1)
-    lengths_all = told[:, 0, utts, :utts].astype(jnp.int32)
-    ends_all = jnp.cumsum(lengths_all, axis=1)
-
-    frame_here = slot * tok + jnp.arange(tok, dtype=jnp.int32)
-
-    def scale_rows(f, cond_cols):
-        group = part ^ ORDER[f]
-        ends = lax.dynamic_index_in_dim(ends_all, group, 0, keepdims=False)
-        owner = owner_of(frame_here, ends)
-        rows = lax.dynamic_index_in_dim(cond_all, group, 0, keepdims=False)[:, cond_cols]
-        onehot = owner[:, None] == jnp.arange(utts, dtype=jnp.int32)[None, :]
-        picked = 1.0 + jnp.dot(onehot.astype(F32), rows, precision=lax.Precision.HIGHEST)
-        return picked, onehot
-
-    attn_cols, ffn_cols = slice(0, width), slice(width, 2 * width)
-    scaled = [scale_rows(f, attn_cols) for f in range(4)]
-    scale_attn = jnp.concatenate([pair[0] for pair in scaled], axis=0)
-    scale_ffn = jnp.concatenate([scale_rows(f, ffn_cols)[0] for f in range(2)], axis=0)
-    utt_rows = scaled[0][1].astype(BF16).T
-
-    my_ends = lax.dynamic_index_in_dim(ends_all, slot // 2, 0, keepdims=False)
-    my_lengths = lax.dynamic_index_in_dim(lengths_all, slot // 2, 0, keepdims=False)
-    all_frames = jnp.arange(frames, dtype=jnp.int32)
-    owner_all = owner_of(all_frames, my_ends)
-    own_hot = owner_all[:, None] == jnp.arange(utts, dtype=jnp.int32)[None, :]
-    begins = jnp.sum(jnp.where(own_hot, (my_ends - my_lengths)[None, :], 0), axis=1)
-    positions = (all_frames - begins).astype(F32)
+    utts = times.shape[1]
+
+    def embed_here(time_rows):
+        column = (slot * rows_here + jnp.arange(rows_here, dtype=jnp.int32)) % half_width
+        freqs = jnp.exp(-math.log(10000.0) * column.astype(F32) / half_width)
+        angles = time_rows[:, None] * freqs[None, :]
+        return jnp.where(slot * rows_here < half_width, jnp.sin(angles), jnp.cos(angles)).astype(BF16)
+
+    skip_rows = skip_weight.shape[0]
+    (skip_piece,) = call(
+        cut_skip_kernel,
+        [sds((skip_rows + 64, 256), BF16)],
+        [SMEM] + [VMEM] * 3,
+        [],
+        [ids, skip_weight, embed_here(times[0].astype(F32)), cond_weight],
+    )
+    (skip_same,) = call(
+        gather_kernel,
+        [sds((4 * skip_rows + 64, 256), BF16)],
+        [VMEM] * 4,
+        [],
+        [skip_piece] + [from_seq(skip_piece, 2 * k) for k in range(1, 4)],
+    )
+    skip_other = from_seq(skip_same, 1)
+    (joined,) = call(
+        join_kernel, [sds((4, tok, 2 * width), BF16)], [VMEM] * 2, [], [hidden_in, skips], deps=[skip_piece]
+    )
+    inputs = lax.all_to_all(joined, "grp", 0, 0, tiled=True)
+    (qkv_piece,) = call(cut_qkv_kernel, [sds((128, 768), BF16)], [SMEM, VMEM], [], [ids, qkv_weight], deps=[joined])
+    w_qkv = lax.all_gather(qkv_piece, "seq", axis=0, tiled=True)
+    (feed_piece,) = call(
+        cut_feed_kernel,
+        [sds((128, ff // 4 + width), BF16)],
+        [SMEM, VMEM, ANY],
+        [sem],
+        [ids, up_weight, down_weight],
+        deps=[qkv_piece],
+    )
+    w_feed = lax.all_gather(feed_piece, "seq", axis=0, tiled=True)
+
+    counts = jnp.stack([lengths[0] >> 5, lengths[0] & 31, times[0] >> 5, times[0] & 31])
+    notes = jnp.zeros((16, 256), BF16).at[0:4, 0:utts].set(counts.astype(BF16))
+
+    (out_piece,) = call(copy_kernel, [sds(out_weight.shape, BF16)], [VMEM], [], [out_weight], deps=[skip_same])
+    out_came = out_along_z(out_piece)
+
     inverse = jnp.exp(-math.log(10000.0) * jnp.arange(32, dtype=F32) / 32)
-    turn_angles = positions[:, None] * inverse[None, :]
+    turn_angles = jnp.arange(frames, dtype=F32)[:, None] * inverse[None, :]
     cos_half, sin_half = jnp.cos(turn_angles), jnp.sin(turn_angles)
     cosine = jnp.concatenate([cos_half] * 4, axis=1)
     sine = jnp.concatenate([-sin_half, sin_half] * 2, axis=1)
-    owner_col, owner_row = owner_all[:, None], owner_all[None, :]
-
-    w_qkv = gather_slots(columns(qkv_weight, 6, 128))
-    out_rows_all = lax.all_gather(out_weight, "seq", axis=0, tiled=True)
-    w_feed = gather_slots(
-        jnp.concatenate(
-            [columns(up_weight, 8, 128), lax.dynamic_slice_in_dim(down_weight, part * 128, 128, 0)],
-            axis=1,
-        )
-    )
-    cots = gather_groups(cotangent)
-
-    (h_cols,) = call(
+
+    h_cols, w_skip = call(
         h_zero_kernel,
-        [sds((4 * tok, 256), BF16)],
-        [SMEM] + [ANY] * 12,
-        [pltpu.VMEM((4 * tok, 2 * width), BF16), pltpu.VMEM((2 * width, 256), BF16), sem((12,))],
-        [ids] + inputs + w_skip,
-        flops=2 * 4 * tok * 2 * width * 256,
+        [sds((4 * tok + 80, 256), BF16), sds((2 * width, 256), BF16)],
+        [SMEM] + [ANY] * 3 + [VMEM],
+        [
+            pltpu.VMEM((4 * tok, 2 * width), BF16),
+            pltpu.VMEM((2 * width, 256), BF16),
+            pltpu.VMEM((2, 64, 256), BF16),
+            sem((14,)),
+        ],
+        [ids, inputs, skip_same, skip_other, notes],
+        deps=out_came,
+        cost_us=100.0,
     )
     h_pieces = gather_groups(h_cols)
     h_pieces = [h_pieces[0], h_pieces[2], h_pieces[1], h_pieces[3]]
-    normed, h_zero, packed = call(
+    normed, h_zero, packed, told = call(
         qkv_kernel,
-        [sds((4 * tok, width), BF16), sds((2 * tok, width), BF16), sds((8, tok, 384), BF16)],
-        [SMEM] + [ANY] * 4 + [VMEM] + [ANY] * 8,
-        [pltpu.VMEM((4 * tok, width), BF16), pltpu.VMEM((width, 768), BF16), sem((24,))],
-        [ids] + h_pieces + [scale_attn] + w_qkv,
-        flops=2 * 4 * tok * width * 768,
-    )
+        [
+            sds((4 * tok, width), BF16),
+            sds((2 * tok, width), BF16),
+            sds((8, tok, 384), BF16),
+            sds((4, 2 * utts, 2 * width), F32),
+        ],
+        [SMEM] + [ANY] * 4 + [VMEM],
+        [pltpu.VMEM((4 * tok, width), BF16), pltpu.VMEM((4, 80, 256), BF16), sem((20,))],
+        [ids] + h_pieces + [w_qkv],
+    )
+    emb_all = embed_here(told[:, utts + 1, :utts].reshape(4 * utts))
     qkv = exchange(packed, 384)
+    (out_picked,) = call(
+        pick_kernel, [sds((2 * tok, width), BF16)], [SMEM] + [VMEM] * 4, [], [ids, out_piece] + out_came
+    )
+    out_over = out_along_x(out_picked)
+    (w_skip,) = call(copy_kernel, [sds(w_skip.shape, BF16)], [VMEM], [], [w_skip], deps=[packed])
+    skip_y = from_grp(w_skip, 2)
     mixed, log_total = call(
         attend_kernel,
         [sds((8, tok, 128), BF16), sds((2, frames), F32)],
-        [VMEM] * 5,
-        [],
-        [qkv, cosine, sine, owner_col, owner_row],
-        flops=2 * 2 * 2 * frames * frames * 64 * 2,
+        [SMEM] + [VMEM] * 4,
+        [pltpu.VMEM((1, frames), F32)],
+        [ids, qkv, cosine, sine, told],
+        deps=[emb_all, out_over, skip_y],
     )
     attended_blocks = exchange(mixed, 128)
-    keep, send, attended = call(
+    (cot_piece,) = call(
+        copy_kernel, [sds((tok, width), BF16)], [VMEM], [], [cotangent], deps=[mixed]
+    )
+    cots = around(cot_piece)
+    keep, send, attended, w_out = call(
         project_kernel,
-        [sds((2 * tok, width), F32), sds((2 * tok, width), BF16), sds((4 * tok, 256), BF16)],
-        [SMEM, ANY, ANY],
-        [pltpu.VMEM((256, width), BF16), sem((10,))],
-        [ids, attended_blocks, out_rows_all],
-        flops=2 * 4 * tok * width * 256,
-    )
-    h_part = halves_sum(keep, send)
+        [
+            sds((2 * tok, width), F32),
+            sds((2 * tok, width), BF16),
+            sds((4 * tok, 256), BF16),
+            sds((2 * tok, width), BF16),
+        ],
+        [SMEM, ANY, ANY, ANY],
+        [sem((9,))],
+        [ids, attended_blocks, out_picked, out_over],
+        deps=cots[1:],
+    )
+    h_part, h_part_y = halves_sum(keep, send)
+    skip_near = stack([w_skip, skip_y], [h_part])
+    skip_far = from_grp(skip_near, 1)
     h_one, normed_two = call(
         residual_kernel,
         [sds((2 * tok, width), F32), sds((2 * tok, width), BF16)],
-        [VMEM] * 4,
+        [SMEM] + [VMEM] * 4,
         [],
-        [h_zero, h_part, from_grp(h_part, 2), scale_ffn],
+        [ids, h_zero, h_part, h_part_y, told],
+        deps=[skip_near],
     )
     normed_two_c = from_grp(normed_two, 1)
     quarter = ff // 4
-    feed_scratch = [
-        pltpu.VMEM((width, quarter), BF16),
-        pltpu.VMEM((quarter, width), BF16),
-        pltpu.VMEM((4 * tok, width), BF16),
-        pltpu.VMEM((4 * tok, width), BF16),
-        sem((22,)),
-    ]
     act, d_pre, keep, send = call(
         feed_kernel,
         [
@@ -872,127 +1120,151 @@
             sds((2 * tok, width), F32),
             sds((2 * tok, width), BF16),
         ],
-        [SMEM] + [ANY] * 14,
-        feed_scratch,
-        [ids, normed_two, normed_two_c] + cots + w_feed,
-        flops=3 * 2 * 4 * tok * width * quarter,
-    )
-
-    d_part = halves_sum(keep, send)
+        [SMEM] + [VMEM] * 7,
+        [],
+        [ids, normed_two, normed_two_c, *cots, w_feed],
+    )
+
+    d_part, d_part_y = halves_sum(keep, send)
+    (feed_terms,) = call(
+        feed_grad_kernel,
+        [sds((width, quarter + width), BF16)],
+        [ANY] * 6 + [VMEM] * 2,
+        [pltpu.VMEM((4 * tok, width), BF16), pltpu.VMEM((4 * tok, width), BF16), sem((6,))],
+        [normed_two, normed_two_c, *cots, act, d_pre],
+        deps=[d_part],
+    )
+    out_keep, out_send = call(
+        feed_out_kernel,
+        [sds((2 * tok, width), F32), sds((2 * tok, width), BF16)],
+        [VMEM, VMEM],
+        [],
+        [act, w_feed],
+        deps=[feed_terms],
+    )
     d_h_one, sums_ffn = call(
-        norm_back_kernel,
+        functools.partial(norm_back_kernel, width),
         [sds((2 * tok, width), BF16), sds((utts, width), F32)],
-        [VMEM] * 7,
+        [SMEM] + [VMEM] * 6,
         [],
-        [h_one, scale_ffn, d_part, from_grp(d_part, 2), cots[0], cots[1], utt_rows],
+        [ids, h_one, d_part, d_part_y, cots[0], cots[1], told],
+        deps=[out_send],
+        cost_us=100.0,
     )
     d_h_one_c = from_grp(d_h_one, 1)
     (d_att_packed,) = call(
         d_attended_kernel,
         [sds((8, tok, 128), BF16)],
-        [SMEM, VMEM, VMEM, ANY],
-        [pltpu.VMEM((256, width), BF16), sem((2,))],
-        [ids, d_h_one, d_h_one_c, out_rows_all],
-        flops=2 * 4 * tok * width * 256,
+        [SMEM, VMEM, VMEM, VMEM],
+        [],
+        [ids, d_h_one, d_h_one_c, w_out],
     )
     d_att = exchange(d_att_packed, 128)
 
-    out_keep, out_send = call(
-        feed_out_kernel,
-        [sds((2 * tok, width), F32), sds((2 * tok, width), BF16)],
-        [SMEM, VMEM] + [ANY] * 8,
-        [pltpu.VMEM((quarter, width), BF16), sem((8,))],
-        [ids, act] + w_feed,
-        flops=2 * 4 * tok * width * quarter,
-    )
-    out_part = halves_sum(out_keep, out_send)
-    block_out = (
-        h_one[:tok] + out_part[:tok].astype(F32) + from_grp(out_part[tok:], 2).astype(F32)
-    ).astype(BF16)
-    feed_even, feed_odd = call(
-        feed_grad_kernel,
-        [sds((4, 128, 2 * width), BF16)] * 2,
-        [SMEM] + [ANY] * 6 + [VMEM] * 2,
-        feed_scratch[2:4] + [sem((6,))],
-        [ids, normed_two, normed_two_c] + cots + [act, d_pre],
-        flops=2 * 2 * 4 * tok * width * quarter,
-    )
-    feed_grads = gather_groups(scatter_slots(feed_even, feed_odd))
-    att_pieces = gather_groups(attended)
-
+    out_part = add_two(out_keep, from_grp(out_send, 1), [d_att_packed])
+    feed_own = lax.psum_scatter(feed_terms, "seq", scatter_dimension=0, tiled=True)
+    att_pieces = around(attended)
     (d_packed,) = call(
         attend_back_kernel,
         [sds((8, tok, 384), BF16)],
-        [VMEM] * 7,
-        [pltpu.VMEM((frames, 128), F32), pltpu.VMEM((frames, 128), F32)],
-        [qkv, d_att, cosine, sine, owner_col, owner_row, log_total],
-        flops=5 * 2 * 2 * frames * frames * 64 * 2,
+        [SMEM] + [VMEM] * 6,
+        [pltpu.VMEM((frames, 128), F32), pltpu.VMEM((frames, 128), F32), pltpu.VMEM((1, frames), F32)],
+        [ids, qkv, d_att, cosine, sine, log_total, told],
+        deps=[out_part] + att_pieces[1:],
     )
     d_qkv_blocks = exchange(d_packed, 384)
+    (block_out,) = call(
+        add_three_kernel,
+        [sds((tok, width), BF16)],
+        [VMEM] * 3,
+        [],
+        [h_one[:tok], out_part[:tok], from_grp(out_part[tok:], 2)],
+        deps=[d_packed],
+    )
     keep, send, d_qkv = call(
         qkv_back_kernel,
         [sds((2 * tok, width), F32), sds((2 * tok, width), BF16), sds((4 * tok, 768), BF16)],
-        [SMEM] + [ANY] * 9,
-        [pltpu.VMEM((width, 768), BF16), sem((32,))],
-        [ids, d_qkv_blocks] + w_qkv,
-        flops=2 * 4 * tok * width * 768,
-    )
-    d_part = halves_sum(keep, send)
-    d_h_zero, sums_attn = call(
-        norm_back_kernel,
-        [sds((2 * tok, width), BF16), sds((utts, width), F32)],
-        [VMEM] * 7,
-        [],
-        [h_zero, scale_attn[: 2 * tok], d_part, from_grp(d_part, 2), d_h_one[:tok], d_h_one[tok:], utt_rows],
-    )
+        [SMEM, ANY, VMEM],
+        [sem((24,))],
+        [ids, d_qkv_blocks, w_qkv],
+        deps=[block_out],
+    )
+    d_part, d_part_y = halves_sum(keep, send)
     qkv_even, qkv_odd = call(
         qkv_grad_kernel,
         [sds((4, 128, 1024), BF16)] * 2,
         [SMEM] + [VMEM] * 4 + [ANY] * 4,
         [pltpu.VMEM((4 * tok, width), BF16), sem((32,))],
-        [ids, normed, d_qkv, d_h_one, d_h_one_c, att_pieces[0], att_pieces[2], att_pieces[1], att_pieces[3]],
-        flops=2 * 4 * tok * width * 1024,
+        [ids, normed, d_qkv, d_h_one, d_h_one_c] + att_pieces,
+        deps=[d_part],
+    )
+    d_h_zero, sums_attn = call(
+        functools.partial(norm_back_kernel, 0),
+        [sds((2 * tok, width), BF16), sds((utts, width), F32)],
+        [SMEM] + [VMEM] * 6,
+        [],
+        [ids, h_zero, d_part, d_part_y, d_h_one[:tok], d_h_one[tok:], told],
+        deps=[qkv_odd],
     )
     d_h_zero_c = from_grp(d_h_zero, 1)
-    skip_even, skip_odd, in_keep, in_send = call(
+    skip_even, skip_odd, skip_sums = call(
         skip_back_kernel,
-        [sds((4, 256, 256), BF16)] * 2 + [sds((2 * tok, 2 * width), F32), sds((2 * tok, 2 * width), BF16)],
-        [SMEM, VMEM, VMEM] + [ANY] * 12,
-        [pltpu.VMEM((4 * tok, 2 * width), BF16), pltpu.VMEM((2 * width, 256), BF16), sem((12,))],
-        [ids, d_h_zero, d_h_zero_c] + inputs + w_skip,
-        flops=2 * 2 * 4 * tok * 2 * width * 256,
-    )
-    skip_grads = gather_groups(scatter_slots(skip_even, skip_odd))
-    qkv_grads = gather_groups(scatter_slots(qkv_even, qkv_odd))
-    in_part = halves_sum(in_keep, in_send)
-    in_both = (in_part[:tok].astype(F32) + from_grp(in_part[tok:], 2).astype(F32)).astype(BF16)
-
-    emb_sums = jnp.concatenate([sums_attn, sums_ffn], axis=1)
-    sums_all = lax.all_gather(emb_sums, ("grp", "seq"), axis=0).reshape(4, 8, utts, 2 * width)
-    sums_all = jnp.sum(sums_all, axis=1)
-    emb_all = lax.all_gather(emb_here, "grp", axis=0)
-    cond_grad = contract(
-        emb_all.reshape(4 * utts, rows_here), sums_all.reshape(4 * utts, 2 * width).astype(BF16), 0, 0
-    )
-
-    def by_mask(pieces):
-        return [pieces[0], pieces[2], pieces[1], pieces[3]]
-
-    qkv_grad, out_grad, up_grad, down_grad, skip_grad_w = call(
+        [sds((4, 256, 256), BF16), sds((1024 + 64, 256), BF16), sds((64, 256), BF16)],
+        [SMEM, VMEM, VMEM, ANY, VMEM, VMEM],
+        [pltpu.VMEM((4 * tok, 2 * width), BF16), sem((4,))],
+        [ids, d_h_zero, d_h_zero_c, inputs, sums_attn, sums_ffn],
+    )
+    qkv_near = scatter_near(qkv_even, qkv_odd, [skip_odd])
+    qkv_came = [from_seq(qkv_near[k], 2 * k) for k in range(1, 4)]
+    last_near = call(
+        skip_near_kernel,
+        [sds((256 + 64, 256), BF16)] * 4,
+        [VMEM] * 3,
+        [],
+        [skip_even, skip_sums, from_seq(skip_odd, 1)],
+        deps=[qkv_near[0]],
+    )
+    last_came = [from_seq(last_near[k], 2 * k) for k in range(1, 4)]
+    in_grad, skip_grad = call(
+        in_back_kernel,
+        [sds((tok, width), BF16)] * 2,
+        [SMEM] + [VMEM] * 3,
+        [],
+        [ids, d_h_zero, skip_near, skip_far],
+        deps=qkv_came + [last_near[0]],
+    )
+    (last_own,) = call(
+        last_kernel,
+        [sds((128, 1792), BF16)],
+        [VMEM] * 8,
+        [],
+        [last_near[0]] + last_came + [qkv_near[0]] + qkv_came,
+        deps=[in_grad],
+    )
+    last_all = gather_groups(last_own)
+    feed_near, feed_far = gather_pairs(feed_own, [last_own])
+    up_grad, down_grad = call(
+        spread_feed_kernel,
+        [sds((128, ff), F32), sds((ff // 8, width), F32)],
+        [SMEM] + [VMEM] * 2,
+        [],
+        [ids, feed_near, feed_far],
+    )
+    qkv_grad, out_grad, skip_grad_w, cond_grad = call(
         spread_kernel,
         [
             sds((128, 3 * width), F32),
             sds((128, width), F32),
-            sds((128, ff), F32),
-            sds((ff // 8, width), F32),
             sds((256, width), F32),
+            sds((rows_here, 2 * width), F32),
         ],
-        [SMEM] + [VMEM] * 12,
+        [SMEM] + [VMEM] * 5,
         [],
-        [ids] + by_mask(qkv_grads) + by_mask(feed_grads) + by_mask(skip_grads),
+        [ids] + last_all + [emb_all],
+        deps=[up_grad],
     )
     return (
-        block_out, in_both[:, :width], in_both[:, width:], skip_grad_w, cond_grad, qkv_grad,
+        block_out, in_grad, skip_grad, skip_grad_w, cond_grad, qkv_grad,
         out_grad, up_grad, down_grad,
     )
 

time: 510 us -> 417 us (0.82)
  Pallas kernels: 65.9 us -> 141 us
  waiting for transfers between devices: 207 us -> 152 us
  starting transfers between devices: 117 us -> 80.9 us
  local copies, waits for them, and re-layouts: 44.1 us -> 14.7 us
  other arithmetic: 26.7 us -> 7.24 us
  blocking collectives: 18.7 us -> 0 us
    pallas_call x16 -> x37, Pallas kernels: 65.9 us -> 141 us  [call(): pl.pallas_call(with_deps, out_shape=tuple(out_shapes), in_specs=list(in_s...]
    ppermute x33 -> x12, waiting for transfers between devices: 117 us -> 62.9 us  [from_seq(): return lax.ppermute(array, 'seq', swapped('seq', mask, 8))]
    ppermute x34 -> x27, waiting for transfers between devices: 41 us -> 73.1 us  [from_grp(): return lax.ppermute(array, 'grp', swapped('grp', mask, 4))]
    ppermute x34 -> x27, starting transfers between devices: 64.8 us -> 33.7 us  [from_grp(): return lax.ppermute(array, 'grp', swapped('grp', mask, 4))]
    ppermute x33 -> x12, starting transfers between devices: 31.7 us -> 9.66 us  [from_seq(): return lax.ppermute(array, 'seq', swapped('seq', mask, 8))]
    unnamed x166 -> x72, local copies, waits for them, and re-layouts: 33 us -> 11.5 us
    all_gather x3 -> x2, waiting for transfers between devices: 19.9 us -> 0.01 us  [the longest x1 0.01 us: tp_body(): w_qkv = lax.all_gather(qkv_piece, 'seq', axis=0, tiled=True)]
    all_to_all x3 -> x4, waiting for transfers between devices: 28.9 us -> 9.69 us  [exchange(): return lax.all_to_all(array, 'seq', 0, 0, tiled=True)]
  transfers between devices with their start and end apart: 73 -> 51, of which waited for: 29 -> 29; matrix products, arithmetic and copies ran while one was open for 7% -> 2% of each run, Pallas kernels for 9% -> 28%
where the time goes in v2:
time: 417 us; the launch traced here: 411 us
  waiting for transfers between devices  152 us (36%)
  Pallas kernels  141 us (34%)
  starting transfers between devices  80.9 us (19%)
  local copies, waits for them, and re-layouts  14.7 us (4%)
  between operations  14.4 us (3%)
  other arithmetic  7.24 us (2%)
    pallas_call x37, Pallas kernels, call(): pl.pallas_call(with_deps, out_shape=tuple(out_shapes), in_specs=list(in_s...  141 us
    ppermute x27, waiting for transfers between devices, from_grp(): return lax.ppermute(array, 'grp', swapped('grp', mask, 4))  73.1 us
    ppermute x12, waiting for transfers between devices, from_seq(): return lax.ppermute(array, 'seq', swapped('seq', mask, 8))  62.9 us
    ppermute x27, starting transfers between devices, from_grp(): return lax.ppermute(array, 'grp', swapped('grp', mask, 4))  33.7 us
    all_to_all x4, starting transfers between devices, exchange(): return lax.all_to_all(array, 'seq', 0, 0, tiled=True)  28.3 us
    unnamed x72, local copies, waits for them, and re-layouts  11.5 us
    all_to_all x4, waiting for transfers between devices, exchange(): return lax.all_to_all(array, 'seq', 0, 0, tiled=True)  9.69 us
    ppermute x12, starting transfers between devices, from_seq(): return lax.ppermute(array, 'seq', swapped('seq', mask, 8))  9.66 us
  transfers between devices with their start and end apart: 51, of which 29 were waited for; matrix products, arithmetic and copies ran while one was open for 2% of the time, Pallas kernels for 28%

profile of v2, /device:TPU:9, one launch (start us, length us, event | category | flops | bytes accessed | tf_op | source)
XLA Modules:
  0.0 410.8 jit_solution(17050203203234987286)
XLA Ops:
  15.8 5.2 %all-to-all-start = ((bf16[4,128,2048]{2,1,0:T(8,128)(2,1)}), bf16[4,128,2048]{2,1,0:T(8,128)(2,1)}, u32[]{:S(2)}, u32[]{:S(2)}) async-start(bf16[4,128,2048]{2,1,0:T(8,128)(2,1)} %shard_map.179.refs_2_), calls=%async_computation | async-start | bytes 4194304 | tf_op jit(solution)/shard_map/all_to_all | solution.py:1015
  27.9 5.3 %collective-permute-done.1.refs_2_ = bf16[320,256]{1,0:T(8,128)(2,1)S(1)} collective-permute-done((bf16[320,256]{1,0:T(8,128)(2,1)S(1)}, bf16[320,256]{1,0:T(8,128)(2,1)S(1)}, u32[]{:S(2)}, u32[]{:S(2)}) %collective-permute-start.1) | collective-permute-done | bytes 163872 | tf_op jit(solution)/shard_map/ppermute | solution.py:336
  33.2 10.6 %collective-permute-done.2.refs_3_ = bf16[320,256]{1,0:T(8,128)(2,1)S(1)} collective-permute-done((bf16[320,256]{1,0:T(8,128)(2,1)S(1)}, bf16[320,256]{1,0:T(8,128)(2,1)S(1)}, u32[]{:S(2)}, u32[]{:S(2)}) %collective-permute-start.2) | collective-permute-done | bytes 163872 | tf_op jit(solution)/shard_map/ppermute | solution.py:336
  55.4 10.7 %collective-permute-done.3.refs_3_ = bf16[1088,256]{1,0:T(8,128)(2,1)} collective-permute-done((bf16[1088,256]{1,0:T(8,128)(2,1)}, bf16[1088,256]{1,0:T(8,128)(2,1)}, u32[]{:S(2)}, u32[]{:S(2)}) %collective-permute-start.3) | collective-permute-done | bytes 557088 | tf_op jit(solution)/shard_map/ppermute | solution.py:336
  66.1 4.4 %shard_map.182 = (bf16[592,256]{1,0:T(8,128)(2,1)}, bf16[2048,256]{1,0:T(8,128)(2,1)}) custom-call(s32[2]{0:T(128)} %pad_add_fusion.refs_0_, bf16[4,128,2048]{2,1,0:T(8,128)(2,1)} %all-to-all-done.refs_1_.refs_3_, bf16[1088,256]{1,0:T(8,128)(2,1)} %shard_map.180.refs_1_.refs_2_, bf16[1088,256]{1,0:T(8,128)(2,1)} %collective-permute-done.3.refs_3_, ...), custom_call_target="tpu_custom_call" | custom-call | flops 115000000512 | tf_op jit(solution)/shard_map/pallas_call | solution.py:359
  77.1 5.9 %collective-permute-start.9 = (bf16[592,256]{1,0:T(8,128)(2,1)S(1)}, bf16[592,256]{1,0:T(8,128)(2,1)S(1)}, u32[]{:S(2)}, u32[]{:S(2)}) collective-permute-start(bf16[592,256]{1,0:T(8,128)(2,1)S(1)} %collective-permute-done.8.refs_3_), channel_id=1, source_target_pairs={{0,8},{8,0},{16,24},{24,16},{1,9},{9,1},{17,25},{25,17},{2,10},{10... | collective-permute-start | bytes 909320 | tf_op jit(solution)/shard_map/ppermute | solution.py:340
  84.9 6.4 %shard_map.184 = (bf16[512,1024]{1,0:T(8,128)(2,1)}, bf16[256,1024]{1,0:T(8,128)(2,1)}, bf16[8,128,384]{2,1,0:T(8,128)(2,1)}, f32[4,16,2048]{2,1,0:T(8,128)}) custom-call(s32[2]{0:T(128)} %pad_add_fusion.refs_0_, bf16[592,256]{1,0:T(8,128)(2,1)} %get-tuple-element.75.refs_1_, bf16[592,256]{1,0:T(8,128)(2,1)} %copy-done.24, bf16[592,256]{1,0:T(8,128)(2,1)} %copy-done.23, ...), custom_call_target="tpu_custom_call" | custom-call | tf_op jit(solution)/shard_map/pallas_call | solution.py:359
  91.3 8.7 %all-to-all-start.1 = ((bf16[8,128,384]{2,1,0:T(8,128)(2,1)}), bf16[8,128,384]{2,1,0:T(8,128)(2,1)S(1)}, u32[]{:S(2)}, u32[]{:S(2)}) async-start(bf16[8,128,384]{2,1,0:T(8,128)(2,1)} %get-tuple-element.77.refs_1_), calls=%async_computation.1 | async-start | bytes 1572864 | tf_op jit(solution)/shard_map/all_to_all | solution.py:951
  113.3 6.4 %collective-permute-done.10.refs_6_.refs_3_ = bf16[256,1024]{1,0:T(8,128)(2,1)S(1)} collective-permute-done((bf16[256,1024]{1,0:T(8,128)(2,1)}, bf16[256,1024]{1,0:T(8,128)(2,1)S(1)}, u32[]{:S(2)}, u32[]{:S(2)}) %collective-permute-start.10) | collective-permute-done | bytes 524320 | tf_op jit(solution)/shard_map/ppermute | solution.py:971
  119.7 7.5 %collective-permute-done.11.refs_7_.refs_1_ = bf16[2048,256]{1,0:T(8,128)(2,1)} collective-permute-done((bf16[2048,256]{1,0:T(8,128)(2,1)}, bf16[2048,256]{1,0:T(8,128)(2,1)}, u32[]{:S(2)}, u32[]{:S(2)}) %collective-permute-start.11) | collective-permute-done | bytes 1048608 | tf_op jit(solution)/shard_map/ppermute | solution.py:340
  131.0 8.6 %shard_map.187 = (bf16[8,128,128]{2,1,0:T(8,128)(2,1)}, f32[2,1024]{1,0:T(2,128)}) custom-call(s32[2]{0:T(128)} %pad_add_fusion.refs_0_, bf16[8,128,384]{2,1,0:T(8,128)(2,1)} %copy-done, f32[1024,128]{1,0:T(8,128)} %get-tuple-element.143.refs_2_.refs_3_, f32[1024,128]{1,0:T(8,128)} %get-tuple-element.144.refs_3_.refs_4_, ...), custom_call_target="tpu_custom_call" | custom-call | tf_op jit(solution)/shard_map/pallas_call | solution.py:359
  139.6 7.8 %all-to-all-start.2 = ((bf16[8,128,128]{2,1,0:T(8,128)(2,1)}), bf16[8,128,128]{2,1,0:T(8,128)(2,1)}, u32[]{:S(2)}, u32[]{:S(2)}) async-start(bf16[8,128,128]{2,1,0:T(8,128)(2,1)} %get-tuple-element.80.refs_1_), calls=%async_computation.2 | async-start | bytes 524288 | tf_op jit(solution)/shard_map/all_to_all | solution.py:951
  156.2 6.9 %collective-permute-done.14.refs_6_.refs_5_ = bf16[128,1024]{1,0:T(8,128)(2,1)S(1)} collective-permute-done((bf16[128,1024]{1,0:T(8,128)(2,1)}, bf16[128,1024]{1,0:T(8,128)(2,1)S(1)}, u32[]{:S(2)}, u32[]{:S(2)}) %collective-permute-start.14) | collective-permute-done | bytes 262176 | tf_op jit(solution)/shard_map/ppermute | solution.py:340
  177.2 9.8 %collective-permute-done.16.refs_3_ = bf16[256,1024]{1,0:T(8,128)(2,1)S(1)} collective-permute-done((bf16[256,1024]{1,0:T(8,128)(2,1)}, bf16[256,1024]{1,0:T(8,128)(2,1)S(1)}, u32[]{:S(2)}, u32[]{:S(2)}) %collective-permute-start.16) | collective-permute-done | bytes 524320 | tf_op jit(solution)/shard_map/ppermute | solution.py:340
  194.4 11.2 %shard_map.194 = (bf16[512,1024]{1,0:T(8,128)(2,1)}, bf16[512,1024]{1,0:T(8,128)(2,1)}, f32[256,1024]{1,0:T(8,128)}, bf16[256,1024]{1,0:T(8,128)(2,1)}) custom-call(s32[2]{0:T(128)} %pad_add_fusion.refs_0_, bf16[256,1024]{1,0:T(8,128)(2,1)} %get-tuple-element.86.refs_1_.refs_0_, bf16[256,1024]{1,0:T(8,128)(2,1)} %copy-done.8, ...), custom_call_target="tpu_custom_call" | custom-call | tf_op jit(solution)/shard_map/pallas_call | solution.py:359
  211.8 7.5 %shard_map.196.refs_2_ = bf16[1024,2048]{1,0:T(8,128)(2,1)} custom-call(bf16[256,1024]{1,0:T(8,128)(2,1)} %get-tuple-element.86.refs_1_.refs_0_, bf16[256,1024]{1,0:T(8,128)(2,1)} %copy-done.8, bf16[128,1024]{1,0:T(8,128)(2,1)} %shard_map.188.refs_3_.refs_2_.refs_4_, bf16[128,1024]{1,0:T(8,128)(2,1)} %copy-done.4, bf16[128,1024]{1,0:T(8,128)(2,1)} %copy-done.5, ...), custom_call_target="tpu_custom_call" | custom-call | tf_op jit(solution)/shard_map/pallas_call | solution.py:359
  219.3 4.6 %shard_map.197 = (f32[256,1024]{1,0:T(8,128)}, bf16[256,1024]{1,0:T(8,128)(2,1)}) custom-call(bf16[512,1024]{1,0:T(8,128)(2,1)} %get-tuple-element.87.refs_6_.refs_0_, bf16[1024,2048]{1,0:T(8,128)(2,1)} %all-gather.5.cloned.1.call-done.refs_7_.refs_1_, bf16[1024,2048]{1,0:T(8,128)(2,1)} %shard_map.196.refs_2_), custom_call_target="tpu_custom_call" | custom-call | tf_op jit(solution)/shard_map/pallas_call | solution.py:359
  236.1 5.6 %all-to-all-start.3 = ((bf16[8,128,128]{2,1,0:T(8,128)(2,1)}), bf16[8,128,128]{2,1,0:T(8,128)(2,1)}, u32[]{:S(2)}, u32[]{:S(2)}) async-start(bf16[8,128,128]{2,1,0:T(8,128)(2,1)} %shard_map.199.refs_2_), calls=%async_computation.3 | async-start | bytes 524288 | tf_op jit(solution)/shard_map/all_to_all | solution.py:951
  248.9 7.1 %collective-permute-done.25.refs_10_.refs_8_ = bf16[512,256]{1,0:T(8,128)(2,1)S(1)} collective-permute-done((bf16[512,256]{1,0:T(8,128)(2,1)}, bf16[512,256]{1,0:T(8,128)(2,1)S(1)}, u32[]{:S(2)}, u32[]{:S(2)}) %collective-permute-start.25) | collective-permute-done | bytes 262176 | tf_op jit(solution)/shard_map/ppermute | solution.py:340
  256.7 10.7 %shard_map.201.refs_3_ = bf16[8,128,384]{2,1,0:T(8,128)(2,1)} custom-call(s32[2]{0:T(128)} %pad_add_fusion.refs_0_, bf16[8,128,384]{2,1,0:T(8,128)(2,1)} %copy-done, bf16[8,128,128]{2,1,0:T(8,128)(2,1)} %all-to-all-done.3.refs_2_, f32[1024,128]{1,0:T(8,128)} %get-tuple-element.143.refs_2_.refs_3_, f32[1024,128]{1,0:T(8,128)} %get-tuple-element.144.refs_3_.refs_4_, ...), custom_call_target="tpu_custom_call" | custom-call | tf_op jit(solution)/shard_map/pallas_call | solution.py:359
  267.4 6.2 %all-to-all-start.4 = ((bf16[8,128,384]{2,1,0:T(8,128)(2,1)}), bf16[8,128,384]{2,1,0:T(8,128)(2,1)}, u32[]{:S(2)}, u32[]{:S(2)}) async-start(bf16[8,128,384]{2,1,0:T(8,128)(2,1)} %shard_map.201.refs_3_), calls=%async_computation.4 | async-start | bytes 1572864 | tf_op jit(solution)/shard_map/all_to_all | solution.py:951
  275.9 4.8 %collective-permute-done.22.refs_2_ = bf16[128,1024]{1,0:T(8,128)(2,1)S(1)} collective-permute-done((bf16[128,1024]{1,0:T(8,128)(2,1)S(1)}, bf16[128,1024]{1,0:T(8,128)(2,1)S(1)}, u32[]{:S(2)}, u32[]{:S(2)}) %collective-permute-start.22) | collective-permute-done | bytes 262176 | tf_op jit(solution)/shard_map/ppermute | solution.py:340
  283.3 6.9 %all-to-all-done.4.refs_1_ = bf16[8,128,384]{2,1,0:T(8,128)(2,1)} async-done(((bf16[8,128,384]{2,1,0:T(8,128)(2,1)}), bf16[8,128,384]{2,1,0:T(8,128)(2,1)}, u32[]{:S(2)}, u32[]{:S(2)}) %all-to-all-start.4) | async-done | bytes 786464 | tf_op jit(solution)/shard_map/all_to_all | solution.py:951
  290.2 4.8 %shard_map.203 = (f32[256,1024]{1,0:T(8,128)}, bf16[256,1024]{1,0:T(8,128)(2,1)}, bf16[512,768]{1,0:T(8,128)(2,1)}) custom-call(s32[2]{0:T(128)} %pad_add_fusion.refs_0_, bf16[8,128,384]{2,1,0:T(8,128)(2,1)} %all-to-all-done.4.refs_1_, bf16[1024,768]{1,0:T(8,128)(2,1)} %all-gather.3.cloned.1.call-done.refs_5_.refs_2_, bf16[128,1024]{1,0:T(8,128)(2,1)} %shard_map.202.refs_3_), custom_call_target="tpu_custom_call" | custom-call | tf_op jit(solution)/shard_map/pallas_call | solution.py:359
  303.9 5.9 %shard_map.205 = (bf16[4,128,1024]{2,1,0:T(8,128)(2,1)}, bf16[4,128,1024]{2,1,0:T(8,128)(2,1)}) custom-call(s32[2]{0:T(128)} %pad_add_fusion.refs_0_, bf16[512,1024]{1,0:T(8,128)(2,1)} %get-tuple-element.103.refs_1_, bf16[512,768]{1,0:T(8,128)(2,1)} %get-tuple-element.104.refs_2_, bf16[256,1024]{1,0:T(8,128)(2,1)} %get-tuple-element.95.refs_1_.refs_3_, ...), custom_call_target="tpu_custom_call" | custom-call | tf_op jit(solution)/shard_map/pallas_call | solution.py:359
  310.7 5.9 %collective-permute-done.27.refs_3_ = bf16[256,1024]{1,0:T(8,128)(2,1)} collective-permute-done((bf16[256,1024]{1,0:T(8,128)(2,1)}, bf16[256,1024]{1,0:T(8,128)(2,1)}, u32[]{:S(2)}, u32[]{:S(2)}) %collective-permute-start.27) | collective-permute-done | bytes 524320 | tf_op jit(solution)/shard_map/ppermute | solution.py:340
  323.7 4.5 %shard_map.207 = (bf16[4,256,256]{2,1,0:T(8,128)(2,1)}, bf16[1088,256]{1,0:T(8,128)(2,1)}, bf16[64,256]{1,0:T(8,128)(2,1)}) custom-call(s32[2]{0:T(128)} %pad_add_fusion.refs_0_, bf16[256,1024]{1,0:T(8,128)(2,1)} %get-tuple-element.106.refs_1_, bf16[256,1024]{1,0:T(8,128)(2,1)} %copy-done.21, bf16[4,128,2048]{2,1,0:T(8,128)(2,1)} %all-to-all-done.refs_1_.refs_3_, ...), custom_call_target="tpu_custom_call" | custom-call | tf_op jit(solution)/shard_map/pallas_call | solution.py:359
  329.1 5.2 %collective-permute-done.29.refs_1_ = bf16[4,128,1024]{2,1,0:T(8,128)(2,1)} collective-permute-done((bf16[4,128,1024]{2,1,0:T(8,128)(2,1)}, bf16[4,128,1024]{2,1,0:T(8,128)(2,1)}, u32[]{:S(2)}, u32[]{:S(2)}) %collective-permute-start.29) | collective-permute-done | bytes 1048608 | tf_op jit(solution)/shard_map/ppermute | solution.py:336
  338.3 7.9 %collective-permute-done.34.refs_2_ = bf16[1088,256]{1,0:T(8,128)(2,1)} collective-permute-done((bf16[1088,256]{1,0:T(8,128)(2,1)}, bf16[1088,256]{1,0:T(8,128)(2,1)}, u32[]{:S(2)}, u32[]{:S(2)}) %collective-permute-start.34) | collective-permute-done | bytes 557088 | tf_op jit(solution)/shard_map/ppermute | solution.py:336
  352.3 17.1 %collective-permute-done.33.refs_6_.refs_7_ = bf16[128,1024]{1,0:T(8,128)(2,1)S(1)} collective-permute-done((bf16[128,1024]{1,0:T(8,128)(2,1)}, bf16[128,1024]{1,0:T(8,128)(2,1)S(1)}, u32[]{:S(2)}, u32[]{:S(2)}) %collective-permute-start.33) | collective-permute-done | bytes 262176 | tf_op jit(solution)/shard_map/ppermute | solution.py:336
  370.1 4.6 %shard_map.210 = (bf16[128,1024]{1,0:T(8,128)(2,1)}, bf16[128,1024]{1,0:T(8,128)(2,1)}) custom-call(s32[2]{0:T(128)} %pad_add_fusion.refs_0_, bf16[256,1024]{1,0:T(8,128)(2,1)} %get-tuple-element.106.refs_1_, bf16[2,2048,256]{2,1,0:T(8,128)(2,1)} %shard_map.191.refs_5_.refs_2_, bf16[2,2048,256]{2,1,0:T(8,128)(2,1)} %collective-permute-done.28.refs_3_, ...), custom_call_target="tpu_custom_call" | custom-call | tf_op jit(solution)/shard_map/pallas_call | solution.py:359
  383.7 11.3 %collective-permute-done.38.refs_2_ = bf16[128,1792]{1,0:T(8,128)(2,1)S(1)} collective-permute-done((bf16[128,1792]{1,0:T(8,128)(2,1)S(1)}, bf16[128,1792]{1,0:T(8,128)(2,1)S(1)}, u32[]{:S(2)}, u32[]{:S(2)}) %collective-permute-start.38) | collective-permute-done | bytes 458784 | tf_op jit(solution)/shard_map/ppermute | solution.py:340
  (196 shorter events, 160.7 us)
Async XLA Ops:
  7.2 77.0 %all-gather.3.cloned.1.call-start = ((), (), s32[]{:S(2)}) async-start(), calls=%async_computation.6 | async-start | bytes 1769472 | tf_op jit(solution)/shard_map/all_gather | solution.py:1017
  15.8 50.4 %all-to-all-start = ((bf16[4,128,2048]{2,1,0:T(8,128)(2,1)}), bf16[4,128,2048]{2,1,0:T(8,128)(2,1)}, u32[]{:S(2)}, u32[]{:S(2)}) async-start(bf16[4,128,2048]{2,1,0:T(8,128)(2,1)} %shard_map.179.refs_2_), calls=%async_computation | async-start | bytes 4194304 | tf_op jit(solution)/shard_map/all_to_all | solution.py:1015
  21.0 172.6 %all-gather.5.cloned.1.call-start = ((), (), s32[]{:S(2)}) async-start(), calls=%async_computation.7 | async-start | bytes 4718592 | tf_op jit(solution)/shard_map/all_gather | solution.py:1026
  21.0 12.2 %collective-permute-start.1 = (bf16[320,256]{1,0:T(8,128)(2,1)S(1)}, bf16[320,256]{1,0:T(8,128)(2,1)S(1)}, u32[]{:S(2)}, u32[]{:S(2)}) collective-permute-start(bf16[320,256]{1,0:T(8,128)(2,1)S(1)} %copy-done.10), channel_id=1, source_target_pairs={{0,4},{1,5},{2,6},{3,7},{4,0},{5,1},{6,2},{7,3},{8,12},{9,13},{10,... | collective-permute-start | bytes 491528 | tf_op jit(solution)/shard_map/ppermute | solution.py:336
  23.5 20.4 %collective-permute-start.2 = (bf16[320,256]{1,0:T(8,128)(2,1)S(1)}, bf16[320,256]{1,0:T(8,128)(2,1)S(1)}, u32[]{:S(2)}, u32[]{:S(2)}) collective-permute-start(bf16[320,256]{1,0:T(8,128)(2,1)S(1)} %copy-done.10), channel_id=1, source_target_pairs={{0,6},{1,7},{2,4},{3,5},{4,2},{5,3},{6,0},{7,1},{8,14},{9,15},{10,... | collective-permute-start | bytes 491528 | tf_op jit(solution)/shard_map/ppermute | solution.py:336
  46.5 19.6 %collective-permute-start.3 = (bf16[1088,256]{1,0:T(8,128)(2,1)}, bf16[1088,256]{1,0:T(8,128)(2,1)}, u32[]{:S(2)}, u32[]{:S(2)}) collective-permute-start(bf16[1088,256]{1,0:T(8,128)(2,1)} %shard_map.180.refs_1_.refs_2_), channel_id=1, source_target_pairs={{0,1},{1,0},{2,3},{3,2},{4,5},{5,4},{6,7},{7,6},{8,9},{9,8},{10,11... | collective-permute-start | bytes 1671176 | tf_op jit(solution)/shard_map/ppermute | solution.py:336
  91.3 38.7 %all-to-all-start.1 = ((bf16[8,128,384]{2,1,0:T(8,128)(2,1)}), bf16[8,128,384]{2,1,0:T(8,128)(2,1)S(1)}, u32[]{:S(2)}, u32[]{:S(2)}) async-start(bf16[8,128,384]{2,1,0:T(8,128)(2,1)} %get-tuple-element.77.refs_1_), calls=%async_computation.1 | async-start | bytes 1572864 | tf_op jit(solution)/shard_map/all_to_all | solution.py:951
  102.3 24.9 %collective-permute-start.11 = (bf16[2048,256]{1,0:T(8,128)(2,1)}, bf16[2048,256]{1,0:T(8,128)(2,1)}, u32[]{:S(2)}, u32[]{:S(2)}) collective-permute-start(bf16[2048,256]{1,0:T(8,128)(2,1)} %shard_map.186.refs_0_), channel_id=1, source_target_pairs={{0,16},{8,24},{16,0},{24,8},{1,17},{9,25},{17,1},{25,9},{2,18},{10... | collective-permute-start | bytes 3145736 | tf_op jit(solution)/shard_map/ppermute | solution.py:340
  106.1 13.6 %collective-permute-start.10 = (bf16[256,1024]{1,0:T(8,128)(2,1)}, bf16[256,1024]{1,0:T(8,128)(2,1)S(1)}, u32[]{:S(2)}, u32[]{:S(2)}) collective-permute-start(bf16[256,1024]{1,0:T(8,128)(2,1)} %shard_map.185.refs_2_), channel_id=1, source_target_pairs={{0,1},{2,3},{4,5},{6,7},{9,8},{11,10},{13,12},{15,14},{16,17},{18,... | collective-permute-start | bytes 1572872 | tf_op jit(solution)/shard_map/ppermute | solution.py:971
  139.6 23.5 %all-to-all-start.2 = ((bf16[8,128,128]{2,1,0:T(8,128)(2,1)}), bf16[8,128,128]{2,1,0:T(8,128)(2,1)}, u32[]{:S(2)}, u32[]{:S(2)}) async-start(bf16[8,128,128]{2,1,0:T(8,128)(2,1)} %get-tuple-element.80.refs_1_), calls=%async_computation.2 | async-start | bytes 524288 | tf_op jit(solution)/shard_map/all_to_all | solution.py:951
  147.4 180.9 %reduce-scatter.2.cloned.1.call-start = ((), (), s32[]{:S(2)}) async-start(), calls=%async_computation.8 | async-start | bytes 4718592 | tf_op jit(solution)/shard_map/reduce_scatter | solution.py:1165
  152.0 11.1 %collective-permute-start.14 = (bf16[128,1024]{1,0:T(8,128)(2,1)}, bf16[128,1024]{1,0:T(8,128)(2,1)S(1)}, u32[]{:S(2)}, u32[]{:S(2)}) collective-permute-start(bf16[128,1024]{1,0:T(8,128)(2,1)} %shard_map.188.refs_3_.refs_2_.refs_4_), channel_id=1, source_target_pairs={{0,24},{8,16},{16,8},{24,0},{1,25},{9,17},{17,9},{25,1},{2,26},{10... | collective-permute-start | bytes 786440 | tf_op jit(solution)/shard_map/ppermute | solution.py:340
  173.4 13.6 %collective-permute-start.16 = (bf16[256,1024]{1,0:T(8,128)(2,1)}, bf16[256,1024]{1,0:T(8,128)(2,1)S(1)}, u32[]{:S(2)}, u32[]{:S(2)}) collective-permute-start(bf16[256,1024]{1,0:T(8,128)(2,1)} %get-tuple-element.84), channel_id=1, source_target_pairs={{0,16},{8,24},{16,0},{24,8},{1,17},{9,25},{17,1},{25,9},{2,18},{10... | collective-permute-start | bytes 1572872 | tf_op jit(solution)/shard_map/ppermute | solution.py:340
  211.0 13.3 %collective-permute-start.20 = (bf16[256,1024]{1,0:T(8,128)(2,1)}, bf16[256,1024]{1,0:T(8,128)(2,1)S(1)}, u32[]{:S(2)}, u32[]{:S(2)}) collective-permute-start(bf16[256,1024]{1,0:T(8,128)(2,1)} %get-tuple-element.94), channel_id=1, source_target_pairs={{0,16},{8,24},{16,0},{24,8},{1,17},{9,25},{17,1},{25,9},{2,18},{10... | collective-permute-start | bytes 1572872 | tf_op jit(solution)/shard_map/ppermute | solution.py:340
  230.0 14.3 %collective-permute-start.19 = (bf16[256,1024]{1,0:T(8,128)(2,1)}, bf16[256,1024]{1,0:T(8,128)(2,1)}, u32[]{:S(2)}, u32[]{:S(2)}) collective-permute-start(bf16[256,1024]{1,0:T(8,128)(2,1)} %get-tuple-element.93.refs_7_), channel_id=1, source_target_pairs={{0,8},{8,0},{16,24},{24,16},{1,9},{9,1},{17,25},{25,17},{2,10},{10... | collective-permute-start | bytes 1572872 | tf_op jit(solution)/shard_map/ppermute | solution.py:340
  236.1 19.8 %all-to-all-start.3 = ((bf16[8,128,128]{2,1,0:T(8,128)(2,1)}), bf16[8,128,128]{2,1,0:T(8,128)(2,1)}, u32[]{:S(2)}, u32[]{:S(2)}) async-start(bf16[8,128,128]{2,1,0:T(8,128)(2,1)} %shard_map.199.refs_2_), calls=%async_computation.3 | async-start | bytes 524288 | tf_op jit(solution)/shard_map/all_to_all | solution.py:951
  243.6 12.3 %collective-permute-start.25 = (bf16[512,256]{1,0:T(8,128)(2,1)}, bf16[512,256]{1,0:T(8,128)(2,1)S(1)}, u32[]{:S(2)}, u32[]{:S(2)}) collective-permute-start(bf16[512,256]{1,0:T(8,128)(2,1)} %get-tuple-element.98.refs_5_), channel_id=1, source_target_pairs={{0,24},{8,16},{16,8},{24,0},{1,25},{9,17},{17,9},{25,1},{2,26},{10... | collective-permute-start | bytes 786440 | tf_op jit(solution)/shard_map/ppermute | solution.py:340
  267.4 22.8 %all-to-all-start.4 = ((bf16[8,128,384]{2,1,0:T(8,128)(2,1)}), bf16[8,128,384]{2,1,0:T(8,128)(2,1)}, u32[]{:S(2)}, u32[]{:S(2)}) async-start(bf16[8,128,384]{2,1,0:T(8,128)(2,1)} %shard_map.201.refs_3_), calls=%async_computation.4 | async-start | bytes 1572864 | tf_op jit(solution)/shard_map/all_to_all | solution.py:951
  298.1 50.2 %collective-permute-start.28 = (bf16[2,2048,256]{2,1,0:T(8,128)(2,1)}, bf16[2,2048,256]{2,1,0:T(8,128)(2,1)}, u32[]{:S(2)}, u32[]{:S(2)}) collective-permute-start(bf16[2,2048,256]{2,1,0:T(8,128)(2,1)} %shard_map.191.refs_5_.refs_2_), channel_id=1, source_target_pairs={{0,8},{8,0},{16,24},{24,16},{1,9},{9,1},{17,25},{25,17},{2,10},{10... | collective-permute-start | bytes 6291464 | tf_op jit(solution)/shard_map/ppermute | solution.py:340
  303.1 13.5 %collective-permute-start.27 = (bf16[256,1024]{1,0:T(8,128)(2,1)}, bf16[256,1024]{1,0:T(8,128)(2,1)}, u32[]{:S(2)}, u32[]{:S(2)}) collective-permute-start(bf16[256,1024]{1,0:T(8,128)(2,1)} %get-tuple-element.102), channel_id=1, source_target_pairs={{0,16},{8,24},{16,0},{24,8},{1,17},{9,25},{17,1},{25,9},{2,18},{10... | collective-permute-start | bytes 1572872 | tf_op jit(solution)/shard_map/ppermute | solution.py:340
  309.8 24.5 %collective-permute-start.29 = (bf16[4,128,1024]{2,1,0:T(8,128)(2,1)}, bf16[4,128,1024]{2,1,0:T(8,128)(2,1)}, u32[]{:S(2)}, u32[]{:S(2)}) collective-permute-start(bf16[4,128,1024]{2,1,0:T(8,128)(2,1)} %get-tuple-element.105.refs_7_), channel_id=1, source_target_pairs={{0,1},{1,0},{2,3},{3,2},{4,5},{5,4},{6,7},{7,6},{8,9},{9,8},{10,11... | collective-permute-start | bytes 3145736 | tf_op jit(solution)/shard_map/ppermute | solution.py:336
  328.1 18.1 %collective-permute-start.34 = (bf16[1088,256]{1,0:T(8,128)(2,1)}, bf16[1088,256]{1,0:T(8,128)(2,1)}, u32[]{:S(2)}, u32[]{:S(2)}) collective-permute-start(bf16[1088,256]{1,0:T(8,128)(2,1)} %get-tuple-element.110.refs_2_), channel_id=1, source_target_pairs={{0,1},{1,0},{2,3},{3,2},{4,5},{5,4},{6,7},{7,6},{8,9},{9,8},{10,11... | collective-permute-start | bytes 1671176 | tf_op jit(solution)/shard_map/ppermute | solution.py:336
  328.3 50.7 %collective-permute-start.41 = (bf16[128,2048]{1,0:T(8,128)(2,1)}, bf16[128,2048]{1,0:T(8,128)(2,1)}, u32[]{:S(2)}, u32[]{:S(2)}) collective-permute-start(bf16[128,2048]{1,0:T(8,128)(2,1)} %reduce-scatter.2.cloned.1.call-done.refs_0_), channel_id=1, source_target_pairs={{0,16},{8,24},{16,0},{24,8},{1,17},{9,25},{17,1},{25,9},{2,18},{10... | collective-permute-start | bytes 1572872 | tf_op jit(solution)/shard_map/ppermute | solution.py:340
  336.8 14.1 %collective-permute-start.31 = (bf16[128,1024]{1,0:T(8,128)(2,1)}, bf16[128,1024]{1,0:T(8,128)(2,1)S(1)}, u32[]{:S(2)}, u32[]{:S(2)}) collective-permute-start(bf16[128,1024]{1,0:T(8,128)(2,1)} %get-tuple-element.111), channel_id=1, source_target_pairs={{0,2},{1,3},{2,0},{3,1},{4,6},{5,7},{6,4},{7,5},{8,10},{9,11},{10,... | collective-permute-start | bytes 786440 | tf_op jit(solution)/shard_map/ppermute | solution.py:336
  338.3 13.7 %collective-permute-start.32 = (bf16[128,1024]{1,0:T(8,128)(2,1)}, bf16[128,1024]{1,0:T(8,128)(2,1)S(1)}, u32[]{:S(2)}, u32[]{:S(2)}) collective-permute-start(bf16[128,1024]{1,0:T(8,128)(2,1)} %get-tuple-element.112), channel_id=1, source_target_pairs={{0,4},{1,5},{2,6},{3,7},{4,0},{5,1},{6,2},{7,3},{8,12},{9,13},{10,... | collective-permute-start | bytes 786440 | tf_op jit(solution)/shard_map/ppermute | solution.py:336
  346.2 23.1 %collective-permute-start.33 = (bf16[128,1024]{1,0:T(8,128)(2,1)}, bf16[128,1024]{1,0:T(8,128)(2,1)S(1)}, u32[]{:S(2)}, u32[]{:S(2)}) collective-permute-start(bf16[128,1024]{1,0:T(8,128)(2,1)} %get-tuple-element.113), channel_id=1, source_target_pairs={{0,6},{1,7},{2,4},{3,5},{4,2},{5,3},{6,0},{7,1},{8,14},{9,15},{10,... | collective-permute-start | bytes 786440 | tf_op jit(solution)/shard_map/ppermute | solution.py:336
  348.4 26.3 %collective-permute-start.35 = (bf16[320,256]{1,0:T(8,128)(2,1)}, bf16[320,256]{1,0:T(8,128)(2,1)S(1)}, u32[]{:S(2)}, u32[]{:S(2)}) collective-permute-start(bf16[320,256]{1,0:T(8,128)(2,1)} %get-tuple-element.120), channel_id=1, source_target_pairs={{0,2},{1,3},{2,0},{3,1},{4,6},{5,7},{6,4},{7,5},{8,10},{9,11},{10,... | collective-permute-start | bytes 491528 | tf_op jit(solution)/shard_map/ppermute | solution.py:336
  350.9 23.7 %collective-permute-start.36 = (bf16[320,256]{1,0:T(8,128)(2,1)}, bf16[320,256]{1,0:T(8,128)(2,1)}, u32[]{:S(2)}, u32[]{:S(2)}) collective-permute-start(bf16[320,256]{1,0:T(8,128)(2,1)} %get-tuple-element.121), channel_id=1, source_target_pairs={{0,4},{1,5},{2,6},{3,7},{4,0},{5,1},{6,2},{7,3},{8,12},{9,13},{10,... | collective-permute-start | bytes 491528 | tf_op jit(solution)/shard_map/ppermute | solution.py:336
  352.0 24.5 %collective-permute-start.37 = (bf16[320,256]{1,0:T(8,128)(2,1)}, bf16[320,256]{1,0:T(8,128)(2,1)}, u32[]{:S(2)}, u32[]{:S(2)}) collective-permute-start(bf16[320,256]{1,0:T(8,128)(2,1)} %get-tuple-element.122), channel_id=1, source_target_pairs={{0,6},{1,7},{2,4},{3,5},{4,2},{5,3},{6,0},{7,1},{8,14},{9,15},{10,... | collective-permute-start | bytes 491528 | tf_op jit(solution)/shard_map/ppermute | solution.py:336
  381.2 14.5 %collective-permute-start.42 = (bf16[2,128,2048]{2,1,0:T(8,128)(2,1)}, bf16[2,128,2048]{2,1,0:T(8,128)(2,1)}, u32[]{:S(2)}, u32[]{:S(2)}) collective-permute-start(bf16[2,128,2048]{2,1,0:T(8,128)(2,1)} %shard_map.212.refs_1_), channel_id=1, source_target_pairs={{0,8},{8,0},{16,24},{24,16},{1,9},{9,1},{17,25},{25,17},{2,10},{10... | collective-permute-start | bytes 3145736 | tf_op jit(solution)/shard_map/ppermute | solution.py:340
  382.8 12.2 %collective-permute-start.38 = (bf16[128,1792]{1,0:T(8,128)(2,1)S(1)}, bf16[128,1792]{1,0:T(8,128)(2,1)S(1)}, u32[]{:S(2)}, u32[]{:S(2)}) collective-permute-start(bf16[128,1792]{1,0:T(8,128)(2,1)S(1)} %copy-done.3), channel_id=1, source_target_pairs={{0,16},{8,24},{16,0},{24,8},{1,17},{9,25},{17,1},{25,9},{2,18},{10... | collective-permute-start | bytes 1376264 | tf_op jit(solution)/shard_map/ppermute | solution.py:340
  383.4 16.3 %collective-permute-start.39 = (bf16[128,1792]{1,0:T(8,128)(2,1)S(1)}, bf16[128,1792]{1,0:T(8,128)(2,1)}, u32[]{:S(2)}, u32[]{:S(2)}) collective-permute-start(bf16[128,1792]{1,0:T(8,128)(2,1)S(1)} %copy-done.3), channel_id=1, source_target_pairs={{0,8},{8,0},{16,24},{24,16},{1,9},{9,1},{17,25},{25,17},{2,10},{10... | collective-permute-start | bytes 1376264 | tf_op jit(solution)/shard_map/ppermute | solution.py:340
  (55 other events, 302.4 us)
Sparse Core Ops, SparseCore 0:
  15.9 57.4 all-gather.2
  75.5 86.4 all-gather.4
  219.4 100.4 reduce-scatter.1

commit v3 on v2

--- a/solution.py
+++ b/solution.py
@@ -320,7 +320,7 @@
 
 ORDER = (0, 2, 1, 3)
 BF16 = jnp.bfloat16
-VMEM_MIB = 63
+VMEM_MIB = 44
 F32 = jnp.float32
 ANY = pl.BlockSpec(memory_space=pl.ANY)
 VMEM = pl.BlockSpec(memory_space=pltpu.VMEM)
@@ -371,6 +371,9 @@
 
 def sds(shape, dtype):
     return jax.ShapeDtypeStruct(shape, dtype)
+
+
+MARK = sds((8, 128), F32)
 
 
 def aligned(index, size):
@@ -482,8 +485,9 @@
     return col, row
 
 
-def attend_kernel(ids, qkv, cosine, sine, told, out, log_out, owner_row):
-    total = cosine.shape[0]
+def attend_kernel(ids, qkv, turns, told, out, log_out, owner_row):
+    total = turns.shape[0]
+    cosine, sine = turns.at[:, 0:128], turns.at[:, 128:256]
     owner_col, owner_row[...] = owners_of(ids, told, total)
     tok = qkv.shape[1]
     queries, keys = rotated(qkv, cosine, sine)
@@ -507,9 +511,10 @@
 
 
 def attend_back_kernel(
-    ids, qkv, d_att, cosine, sine, log_total, told, out, d_keys, d_values, owner_row
+    ids, qkv, d_att, turns, log_total, told, out, d_keys, d_values, owner_row
 ):
-    total = cosine.shape[0]
+    total = turns.shape[0]
+    cosine, sine = turns.at[:, 0:128], turns.at[:, 128:256]
     owner_col, owner_row[...] = owners_of(ids, told, total)
     tok = qkv.shape[1]
     queries, keys = rotated(qkv, cosine, sine)
@@ -596,11 +601,9 @@
         out[...] = (even[k].astype(F32) + odd[k].astype(F32)).astype(BF16)
 
 
-def add_kernel(left, right, out, held, sem):
-    held[...] = (left[...].astype(F32) + right[...].astype(F32)).astype(out.dtype)
-    copy = pltpu.make_async_copy(held, out, sem)
-    copy.start()
-    copy.wait()
+def add_kernel(left, right, out, mark):
+    out[...] = (left[...].astype(F32) + right[...].astype(F32)).astype(out.dtype)
+    mark[...] = jnp.zeros_like(mark)
 
 
 def add_twice_kernel(left, right, out, again):
@@ -612,6 +615,20 @@
 def add_three_kernel(first, second, third, out):
     total = first[...].astype(F32) + second[...].astype(F32) + third[...].astype(F32)
     out[...] = total.astype(out.dtype)
+
+
+def choose_kernel(ids, own, other, out, mark):
+    mine = (ids[0] & 1) == (ids[1] & 1)
+
+    @pl.when(mine)
+    def _():
+        out[...] = own[...]
+
+    @pl.when(jnp.logical_not(mine))
+    def _():
+        out[...] = other[...]
+
+    mark[...] = jnp.zeros_like(mark)
 
 
 def pick_kernel(ids, own, near, far, farther, out):
@@ -637,9 +654,10 @@
 
 
 def stack_kernel(*refs):
-    out = refs[-1]
-    for k, ref in enumerate(refs[:-1]):
+    out, mark = refs[-2:]
+    for k, ref in enumerate(refs[:-2]):
         out[k] = ref[...]
+    mark[...] = jnp.zeros_like(mark)
 
 
 def cut_qkv_kernel(ids, qkv, piece):
@@ -685,21 +703,11 @@
     return jnp.where((frame >= begin) & (frame < end), 1.0, 0.0).astype(BF16)
 
 
-def project_kernel(ids, blocks, picked, over, keep, send, attended, weight, sems):
+def project_kernel(ids, blocks, weight, keep, send, attended, sems):
     tok = blocks.shape[1]
-    mine = (ids[0] & 1) == (ids[1] & 1)
-
-    @pl.when(mine)
-    def _():
-        run_copies([(picked, weight)], sems.at[pl.ds(8, 1)])
-
-    @pl.when(jnp.logical_not(mine))
-    def _():
-        run_copies([(over, weight)], sems.at[pl.ds(8, 1)])
-
     run_copies(attended_pairs(ids, blocks, attended, tok, 1), sems)
+    send[...] = nn(attended[2 * tok :, :], weight[...]).astype(BF16)
     keep[...] = nn(attended[0 : 2 * tok, :], weight[...])
-    send[...] = nn(attended[2 * tok :, :], weight[...]).astype(BF16)
 
 
 def residual_kernel(ids, hidden, part, other, told, h_one_out, normed_out):
@@ -724,9 +732,9 @@
 
 
 def feed_kernel(ids, *refs):
-    normed, normed_c, cots, weight = refs[0], refs[1], refs[2:6], refs[6]
-    act_out, d_pre_out, keep, send = refs[7:]
-    tok = cots[0].shape[0]
+    normed, normed_c, cots, weight = refs[:4]
+    act_out, d_pre_out, keep, send = refs[4:]
+    tok = cots.shape[1]
     hidden = act_out.shape[1]
     for f in range(4):
         block = pl.ds(f * tok, tok)
@@ -734,7 +742,7 @@
         pre = nn((normed, normed_c)[f // 2][rows, :], weight[:, 0:hidden])
         act, slope = gelu_parts(pre)
         act_out[block, :] = act.astype(BF16)
-        d_pre = (nt(cots[f][...], weight[:, hidden:]) * slope).astype(BF16)
+        d_pre = (nt(cots[f], weight[:, hidden:]) * slope).astype(BF16)
         d_pre_out[block, :] = d_pre
         d_normed = nt(d_pre, weight[:, 0:hidden])
         if f < 2:
@@ -743,16 +751,15 @@
             send[rows, :] = d_normed.astype(BF16)
 
 
-def feed_grad_kernel(normed, normed_c, c0, c1, c2, c3, act, d_pre, out, held, cots, sems):
-    tok = c0.shape[0]
-    pairs = [(normed, held.at[pl.ds(0, 2 * tok), :]), (normed_c, held.at[pl.ds(2 * tok, 2 * tok), :])]
-    pairs += [(cot, cots.at[pl.ds(f * tok, tok), :]) for f, cot in enumerate((c0, c1, c2, c3))]
-    run_copies(pairs, sems)
+def feed_grad_kernel(normed, normed_c, cots, act, d_pre, out, held, sems):
+    tok = cots.shape[1]
+    run_copies([(normed, held.at[pl.ds(0, 2 * tok), :]), (normed_c, held.at[pl.ds(2 * tok, 2 * tok), :])], sems)
+    cots_all = cots[...].reshape(4 * tok, cots.shape[2])
     cols = act.shape[1]
     for r in range(8):
         block = pl.ds(r * 128, 128)
         out[block, 0:cols] = tn(held[:, block], d_pre[...]).astype(BF16)
-        out[block, cols:] = tn(act[:, block], cots[...]).astype(BF16)
+        out[block, cols:] = tn(act[:, block], cots_all).astype(BF16)
 
 
 def feed_out_kernel(act, weight, keep, send):
@@ -770,7 +777,7 @@
     return d_hidden, d_normed * y
 
 
-def norm_back_kernel(first_col, ids, hidden, part, other, base, base_y, told, low_out, sums_out):
+def norm_back_kernel(first_col, ids, hidden, part, other, base, told, low_out, sums_out):
     tok = hidden.shape[0] // 2
     width = hidden.shape[1]
     for f in range(2):
@@ -778,7 +785,7 @@
         d_normed = part[rows, :].astype(F32) + other[swap, :].astype(F32)
         scale = scale_of(ids, told.at[f], tok, first_col, width)
         d_hidden, d_scale = norm_back(hidden[rows, :].astype(F32), scale, d_normed)
-        added = (base, base_y)[f][...].astype(F32) + d_hidden
+        added = base[f].astype(F32) + d_hidden
         low_out[rows, :] = added.astype(low_out.dtype)
         if f == 0:
             sums_out[...] = nn(utt_picks(ids, told.at[0], tok), d_scale.astype(BF16))
@@ -902,7 +909,7 @@
 
 def stack(arrays, deps=()):
     shape = (len(arrays),) + arrays[0].shape
-    return call(stack_kernel, [sds(shape, arrays[0].dtype)], [VMEM] * len(arrays), [], list(arrays), deps=deps)[0]
+    return call(stack_kernel, [sds(shape, arrays[0].dtype), MARK], [VMEM] * len(arrays), [], list(arrays), deps=deps)
 
 
 def around(piece):
@@ -915,7 +922,7 @@
 
 
 def gather_pairs(piece, deps=()):
-    near = stack([piece, from_grp(piece, 2)], deps)
+    near, _ = stack([piece, from_grp(piece, 2)], deps)
     return near, from_grp(near, 1)
 
 
@@ -936,15 +943,7 @@
 
 
 def add_two(left, right, deps=()):
-    return call(
-        add_kernel,
-        [sds(left.shape, BF16)],
-        [VMEM] * 2,
-        [pltpu.VMEM(left.shape, BF16), pltpu.SemaphoreType.DMA],
-        [left, right],
-        deps=deps,
-        out_spec=HBM,
-    )[0]
+    return call(add_kernel, [sds(left.shape, BF16), MARK], [VMEM] * 2, [], [left, right], deps=deps)
 
 
 def exchange(array, cols):
@@ -1001,19 +1000,20 @@
         [],
         [ids, skip_weight, embed_here(times[0].astype(F32)), cond_weight],
     )
+    (qkv_piece,) = call(cut_qkv_kernel, [sds((128, 768), BF16)], [SMEM, VMEM], [], [ids, qkv_weight])
     (skip_same,) = call(
         gather_kernel,
         [sds((4 * skip_rows + 64, 256), BF16)],
         [VMEM] * 4,
         [],
         [skip_piece] + [from_seq(skip_piece, 2 * k) for k in range(1, 4)],
+        deps=[qkv_piece],
     )
     skip_other = from_seq(skip_same, 1)
     (joined,) = call(
         join_kernel, [sds((4, tok, 2 * width), BF16)], [VMEM] * 2, [], [hidden_in, skips], deps=[skip_piece]
     )
     inputs = lax.all_to_all(joined, "grp", 0, 0, tiled=True)
-    (qkv_piece,) = call(cut_qkv_kernel, [sds((128, 768), BF16)], [SMEM, VMEM], [], [ids, qkv_weight], deps=[joined])
     w_qkv = lax.all_gather(qkv_piece, "seq", axis=0, tiled=True)
     (feed_piece,) = call(
         cut_feed_kernel,
@@ -1034,8 +1034,7 @@
     inverse = jnp.exp(-math.log(10000.0) * jnp.arange(32, dtype=F32) / 32)
     turn_angles = jnp.arange(frames, dtype=F32)[:, None] * inverse[None, :]
     cos_half, sin_half = jnp.cos(turn_angles), jnp.sin(turn_angles)
-    cosine = jnp.concatenate([cos_half] * 4, axis=1)
-    sine = jnp.concatenate([-sin_half, sin_half] * 2, axis=1)
+    turns = jnp.concatenate([cos_half] * 4 + [-sin_half, sin_half] * 2, axis=1)
 
     h_cols, w_skip = call(
         h_zero_kernel,
@@ -1070,45 +1069,49 @@
     (out_picked,) = call(
         pick_kernel, [sds((2 * tok, width), BF16)], [SMEM] + [VMEM] * 4, [], [ids, out_piece] + out_came
     )
-    out_over = out_along_x(out_picked)
     (w_skip,) = call(copy_kernel, [sds(w_skip.shape, BF16)], [VMEM], [], [w_skip], deps=[packed])
     skip_y = from_grp(w_skip, 2)
+    w_out, out_mark = call(
+        choose_kernel,
+        [sds((2 * tok, width), BF16), MARK],
+        [SMEM] + [VMEM] * 2,
+        [],
+        [ids, out_picked, out_along_x(out_picked)],
+    )
+    skip_near, skip_mark = stack([w_skip, skip_y], [packed])
+    skip_far = from_grp(skip_near, 1)
     mixed, log_total = call(
         attend_kernel,
         [sds((8, tok, 128), BF16), sds((2, frames), F32)],
-        [SMEM] + [VMEM] * 4,
+        [SMEM] + [VMEM] * 3,
         [pltpu.VMEM((1, frames), F32)],
-        [ids, qkv, cosine, sine, told],
-        deps=[emb_all, out_over, skip_y],
+        [ids, qkv, turns, told],
+        deps=[out_mark, skip_mark],
     )
     attended_blocks = exchange(mixed, 128)
     (cot_piece,) = call(
         copy_kernel, [sds((tok, width), BF16)], [VMEM], [], [cotangent], deps=[mixed]
     )
-    cots = around(cot_piece)
-    keep, send, attended, w_out = call(
+    cots, cot_mark = stack(around(cot_piece))
+    keep, send, attended = call(
         project_kernel,
         [
             sds((2 * tok, width), F32),
             sds((2 * tok, width), BF16),
             sds((4 * tok, 256), BF16),
-            sds((2 * tok, width), BF16),
         ],
-        [SMEM, ANY, ANY, ANY],
-        [sem((9,))],
-        [ids, attended_blocks, out_picked, out_over],
-        deps=cots[1:],
+        [SMEM, ANY, VMEM],
+        [sem((8,))],
+        [ids, attended_blocks, w_out],
+        deps=[cot_mark],
     )
     h_part, h_part_y = halves_sum(keep, send)
-    skip_near = stack([w_skip, skip_y], [h_part])
-    skip_far = from_grp(skip_near, 1)
     h_one, normed_two = call(
         residual_kernel,
         [sds((2 * tok, width), F32), sds((2 * tok, width), BF16)],
         [SMEM] + [VMEM] * 4,
         [],
         [ids, h_zero, h_part, h_part_y, told],
-        deps=[skip_near],
     )
     normed_two_c = from_grp(normed_two, 1)
     quarter = ff // 4
@@ -1120,18 +1123,18 @@
             sds((2 * tok, width), F32),
             sds((2 * tok, width), BF16),
         ],
-        [SMEM] + [VMEM] * 7,
-        [],
-        [ids, normed_two, normed_two_c, *cots, w_feed],
+        [SMEM] + [VMEM] * 4,
+        [],
+        [ids, normed_two, normed_two_c, cots, w_feed],
     )
 
     d_part, d_part_y = halves_sum(keep, send)
     (feed_terms,) = call(
         feed_grad_kernel,
         [sds((width, quarter + width), BF16)],
-        [ANY] * 6 + [VMEM] * 2,
-        [pltpu.VMEM((4 * tok, width), BF16), pltpu.VMEM((4 * tok, width), BF16), sem((6,))],
-        [normed_two, normed_two_c, *cots, act, d_pre],
+        [ANY] * 2 + [VMEM] * 3,
+        [pltpu.VMEM((4 * tok, width), BF16), sem((2,))],
+        [normed_two, normed_two_c, cots, act, d_pre],
         deps=[d_part],
     )
     out_keep, out_send = call(
@@ -1145,9 +1148,9 @@
     d_h_one, sums_ffn = call(
         functools.partial(norm_back_kernel, width),
         [sds((2 * tok, width), BF16), sds((utts, width), F32)],
-        [SMEM] + [VMEM] * 6,
-        [],
-        [ids, h_one, d_part, d_part_y, cots[0], cots[1], told],
+        [SMEM] + [VMEM] * 5,
+        [],
+        [ids, h_one, d_part, d_part_y, cots, told],
         deps=[out_send],
         cost_us=100.0,
     )
@@ -1161,16 +1164,16 @@
     )
     d_att = exchange(d_att_packed, 128)
 
-    out_part = add_two(out_keep, from_grp(out_send, 1), [d_att_packed])
     feed_own = lax.psum_scatter(feed_terms, "seq", scatter_dimension=0, tiled=True)
     att_pieces = around(attended)
+    out_part, out_done = add_two(out_keep, from_grp(out_send, 1), att_pieces[1:])
     (d_packed,) = call(
         attend_back_kernel,
         [sds((8, tok, 384), BF16)],
-        [SMEM] + [VMEM] * 6,
+        [SMEM] + [VMEM] * 5,
         [pltpu.VMEM((frames, 128), F32), pltpu.VMEM((frames, 128), F32), pltpu.VMEM((1, frames), F32)],
-        [ids, qkv, d_att, cosine, sine, log_total, told],
-        deps=[out_part] + att_pieces[1:],
+        [ids, qkv, d_att, turns, log_total, told],
+        deps=[out_done],
     )
     d_qkv_blocks = exchange(d_packed, 384)
     (block_out,) = call(
@@ -1201,9 +1204,9 @@
     d_h_zero, sums_attn = call(
         functools.partial(norm_back_kernel, 0),
         [sds((2 * tok, width), BF16), sds((utts, width), F32)],
-        [SMEM] + [VMEM] * 6,
-        [],
-        [ids, h_zero, d_part, d_part_y, d_h_one[:tok], d_h_one[tok:], told],
+        [SMEM] + [VMEM] * 5,
+        [],
+        [ids, h_zero, d_part, d_part_y, d_h_one.reshape(2, tok, width), told],
         deps=[qkv_odd],
     )
     d_h_zero_c = from_grp(d_h_zero, 1)

time: 417 us -> 387 us (0.928)
  Pallas kernels: 141 us -> 80.2 us
  local copies, waits for them, and re-layouts: 14.7 us -> 43.4 us
  waiting for transfers between devices: 152 us -> 164 us
  starting transfers between devices: 80.9 us -> 74.3 us
    pallas_call x37 -> x39, Pallas kernels: 141 us -> 80.2 us  [call(): pl.pallas_call(with_deps, out_shape=tuple(out_shapes), in_specs=list(in_s...]
    unnamed x72 -> x134, local copies, waits for them, and re-layouts: 11.5 us -> 36.9 us
    ppermute x12, waiting for transfers between devices: 62.9 us -> 72.7 us  [from_seq(): return lax.ppermute(array, 'seq', swapped('seq', mask, 8))]
    ppermute x27, waiting for transfers between devices: 73.1 us -> 79.7 us  [from_grp(): return lax.ppermute(array, 'grp', swapped('grp', mask, 4))]
    ppermute x27, starting transfers between devices: 33.7 us -> 28.4 us  [from_grp(): return lax.ppermute(array, 'grp', swapped('grp', mask, 4))]
  transfers between devices with their start and end apart: 51 -> 51, of which waited for: 29 -> 29; matrix products, arithmetic and copies ran while one was open for 2% -> 3% of each run, Pallas kernels for 28% -> 17%
where the time goes in v3:
time: 387 us; the launch traced here: 381 us
  waiting for transfers between devices  164 us (42%)
  Pallas kernels  80.2 us (21%)
  starting transfers between devices  74.3 us (19%)
  local copies, waits for them, and re-layouts  43.4 us (11%)
  between operations  14.7 us (4%)
  other arithmetic  4.04 us (1%)
    pallas_call x39, Pallas kernels, call(): pl.pallas_call(with_deps, out_shape=tuple(out_shapes), in_specs=list(in_s...  80.2 us
    ppermute x27, waiting for transfers between devices, from_grp(): return lax.ppermute(array, 'grp', swapped('grp', mask, 4))  79.7 us
    ppermute x12, waiting for transfers between devices, from_seq(): return lax.ppermute(array, 'seq', swapped('seq', mask, 8))  72.7 us
    unnamed x134, local copies, waits for them, and re-layouts  36.9 us
    ppermute x27, starting transfers between devices, from_grp(): return lax.ppermute(array, 'grp', swapped('grp', mask, 4))  28.4 us
    all_to_all x4, starting transfers between devices, exchange(): return lax.all_to_all(array, 'seq', 0, 0, tiled=True)  24.6 us
    ppermute x12, starting transfers between devices, from_seq(): return lax.ppermute(array, 'seq', swapped('seq', mask, 8))  12.8 us
    all_to_all x4, waiting for transfers between devices, exchange(): return lax.all_to_all(array, 'seq', 0, 0, tiled=True)  8.26 us
  transfers between devices with their start and end apart: 51, of which 29 were waited for; matrix products, arithmetic and copies ran while one was open for 3% of the time, Pallas kernels for 17%

profile of v3, /device:TPU:9, one launch (start us, length us, event | category | flops | bytes accessed | tf_op | source)
XLA Modules:
  0.0 380.6 jit_solution(14254308195865331402)
XLA Ops:
  14.9 4.4 %all-to-all-start = ((bf16[4,128,2048]{2,1,0:T(8,128)(2,1)}), bf16[4,128,2048]{2,1,0:T(8,128)(2,1)S(1)}, u32[]{:S(2)}, u32[]{:S(2)}) async-start(bf16[4,128,2048]{2,1,0:T(8,128)(2,1)} %copy-done.5), calls=%async_computation | async-start | bytes 4194304 | tf_op jit(solution)/shard_map/all_to_all | solution.py:1016
  22.1 7.8 %collective-permute-done.refs_1_ = bf16[320,256]{1,0:T(8,128)(2,1)S(1)} collective-permute-done((bf16[320,256]{1,0:T(8,128)(2,1)S(1)}, bf16[320,256]{1,0:T(8,128)(2,1)S(1)}, u32[]{:S(2)}, u32[]{:S(2)}) %collective-permute-start) | collective-permute-done | bytes 163872 | tf_op jit(solution)/shard_map/ppermute | solution.py:336
  29.9 4.0 %collective-permute-done.1.refs_2_ = bf16[320,256]{1,0:T(8,128)(2,1)S(1)} collective-permute-done((bf16[320,256]{1,0:T(8,128)(2,1)S(1)}, bf16[320,256]{1,0:T(8,128)(2,1)S(1)}, u32[]{:S(2)}, u32[]{:S(2)}) %collective-permute-start.1) | collective-permute-done | bytes 163872 | tf_op jit(solution)/shard_map/ppermute | solution.py:336
  33.9 9.3 %collective-permute-done.2.refs_3_ = bf16[320,256]{1,0:T(8,128)(2,1)S(1)} collective-permute-done((bf16[320,256]{1,0:T(8,128)(2,1)S(1)}, bf16[320,256]{1,0:T(8,128)(2,1)S(1)}, u32[]{:S(2)}, u32[]{:S(2)}) %collective-permute-start.2) | collective-permute-done | bytes 163872 | tf_op jit(solution)/shard_map/ppermute | solution.py:336
  49.6 15.2 %collective-permute-done.3.refs_3_ = bf16[1088,256]{1,0:T(8,128)(2,1)} collective-permute-done((bf16[1088,256]{1,0:T(8,128)(2,1)S(1)}, bf16[1088,256]{1,0:T(8,128)(2,1)}, u32[]{:S(2)}, u32[]{:S(2)}) %collective-permute-start.3) | collective-permute-done | bytes 557088 | tf_op jit(solution)/shard_map/ppermute | solution.py:336
  65.7 3.2 shard_map.183
  73.5 3.0 collective-permute-done.8.refs_3_
  76.5 3.1 collective-permute-start.9
  82.3 4.0 %shard_map.184 = (bf16[512,1024]{1,0:T(8,128)(2,1)S(1)}, bf16[256,1024]{1,0:T(8,128)(2,1)S(1)}, bf16[8,128,384]{2,1,0:T(8,128)(2,1)}, f32[4,16,2048]{2,1,0:T(8,128)S(1)}) custom-call(s32[2]{0:T(128)S(1)} %pad_add_fusion.refs_0_, bf16[592,256]{1,0:T(8,128)(2,1)S(1)} %get-tuple-element.83.refs_1_, bf16[592,256]{1,0:T(8,128)(2,1)S(1)} %collective-permute-done.7.refs_2_, ...), custom_call_target="tpu_custom_call" | custom-call | tf_op jit(solution)/shard_map/pallas_call | solution.py:359
  88.2 6.2 %all-to-all-start.1 = ((bf16[8,128,384]{2,1,0:T(8,128)(2,1)}), bf16[8,128,384]{2,1,0:T(8,128)(2,1)S(1)}, u32[]{:S(2)}, u32[]{:S(2)}) async-start(bf16[8,128,384]{2,1,0:T(8,128)(2,1)} %get-tuple-element.85.refs_1_.refs_2_), calls=%async_computation.1 | async-start | bytes 1572864 | tf_op jit(solution)/shard_map/all_to_all | solution.py:950
  102.4 4.1 %concatenate.5.refs_2_.refs_3_ = f32[1024,256]{1,0:T(8,128)S(1)} concatenate(f32[1024,32]{1,0:T(8,128)} %get-tuple-element.149, f32[1024,32]{1,0:T(8,128)} %get-tuple-element.149, f32[1024,32]{1,0:T(8,128)} %get-tuple-element.149, f32[1024,32]{1,0:T(8,128)} %get-tuple-element.149, f32[1024,32]{1,0:T(8,128)} %get-tuple-element.148, f32[1024,32]{1,0:T(8,128)} %get-tuple-element.147, ...), dimensions={1} | concatenate | bytes 2097152 | tf_op jit(solution)/shard_map/concatenate | solution.py:1037
  111.5 7.9 %collective-permute-done.11.refs_1_ = bf16[2048,256]{1,0:T(8,128)(2,1)} collective-permute-done((bf16[2048,256]{1,0:T(8,128)(2,1)S(1)}, bf16[2048,256]{1,0:T(8,128)(2,1)}, u32[]{:S(2)}, u32[]{:S(2)}) %collective-permute-start.11) | collective-permute-done | bytes 1048608 | tf_op jit(solution)/shard_map/ppermute | solution.py:340
  122.0 7.6 %shard_map.189 = (bf16[8,128,128]{2,1,0:T(8,128)(2,1)}, f32[2,1024]{1,0:T(2,128)S(1)}) custom-call(s32[2]{0:T(128)S(1)} %pad_add_fusion.refs_0_, bf16[8,128,384]{2,1,0:T(8,128)(2,1)S(1)} %all-to-all-done.1.refs_1_, f32[1024,256]{1,0:T(8,128)S(1)} %concatenate.5.refs_2_.refs_3_, f32[4,16,2048]{2,1,0:T(8,128)S(1)} %get-tuple-element.86.refs_3_.refs_4_.refs_5_, ...), custom_call_target="tpu_custom_call" | custom-call | tf_op jit(solution)/shard_map/pallas_call | solution.py:359
  129.6 5.5 %all-to-all-start.2 = ((bf16[8,128,128]{2,1,0:T(8,128)(2,1)}), bf16[8,128,128]{2,1,0:T(8,128)(2,1)}, u32[]{:S(2)}, u32[]{:S(2)}) async-start(bf16[8,128,128]{2,1,0:T(8,128)(2,1)} %get-tuple-element.90.refs_1_), calls=%async_computation.2 | async-start | bytes 524288 | tf_op jit(solution)/shard_map/all_to_all | solution.py:950
  141.5 7.9 %collective-permute-done.14.refs_3_ = bf16[128,1024]{1,0:T(8,128)(2,1)S(1)} collective-permute-done((bf16[128,1024]{1,0:T(8,128)(2,1)S(1)}, bf16[128,1024]{1,0:T(8,128)(2,1)S(1)}, u32[]{:S(2)}, u32[]{:S(2)}) %collective-permute-start.14) | collective-permute-done | bytes 262176 | tf_op jit(solution)/shard_map/ppermute | solution.py:340
  156.8 12.2 %collective-permute-done.16.refs_3_ = bf16[256,1024]{1,0:T(8,128)(2,1)S(1)} collective-permute-done((bf16[256,1024]{1,0:T(8,128)(2,1)S(1)}, bf16[256,1024]{1,0:T(8,128)(2,1)S(1)}, u32[]{:S(2)}, u32[]{:S(2)}) %collective-permute-start.16) | collective-permute-done | bytes 524320 | tf_op jit(solution)/shard_map/ppermute | solution.py:340
  178.7 7.7 %shard_map.196 = (bf16[512,1024]{1,0:T(8,128)(2,1)S(1)}, bf16[512,1024]{1,0:T(8,128)(2,1)S(1)}, f32[256,1024]{1,0:T(8,128)S(1)}, bf16[256,1024]{1,0:T(8,128)(2,1)S(1)}) custom-call(s32[2]{0:T(128)S(1)} %pad_add_fusion.refs_0_, bf16[256,1024]{1,0:T(8,128)(2,1)S(1)} %copy-done.13, bf16[256,1024]{1,0:T(8,128)(2,1)S(1)} %copy-done.16, ...), custom_call_target="tpu_custom_call" | custom-call | tf_op jit(solution)/shard_map/pallas_call | solution.py:359
  209.7 7.0 %all-to-all-start.3 = ((bf16[8,128,128]{2,1,0:T(8,128)(2,1)}), bf16[8,128,128]{2,1,0:T(8,128)(2,1)}, u32[]{:S(2)}, u32[]{:S(2)}) async-start(bf16[8,128,128]{2,1,0:T(8,128)(2,1)} %copy-done.36), calls=%async_computation.3 | async-start | bytes 524288 | tf_op jit(solution)/shard_map/all_to_all | solution.py:950
  219.1 5.2 %collective-permute-done.20.refs_2_.refs_6_ = bf16[512,256]{1,0:T(8,128)(2,1)S(1)} collective-permute-done((bf16[512,256]{1,0:T(8,128)(2,1)}, bf16[512,256]{1,0:T(8,128)(2,1)S(1)}, u32[]{:S(2)}, u32[]{:S(2)}) %collective-permute-start.20) | collective-permute-done | bytes 262176 | tf_op jit(solution)/shard_map/ppermute | solution.py:340
  224.3 6.7 %collective-permute-done.22.refs_4_.refs_8_ = bf16[512,256]{1,0:T(8,128)(2,1)S(1)} collective-permute-done((bf16[512,256]{1,0:T(8,128)(2,1)}, bf16[512,256]{1,0:T(8,128)(2,1)S(1)}, u32[]{:S(2)}, u32[]{:S(2)}) %collective-permute-start.22) | collective-permute-done | bytes 262176 | tf_op jit(solution)/shard_map/ppermute | solution.py:340
  236.3 9.9 %shard_map.203.refs_3_ = bf16[8,128,384]{2,1,0:T(8,128)(2,1)} custom-call(s32[2]{0:T(128)S(1)} %pad_add_fusion.refs_0_, bf16[8,128,384]{2,1,0:T(8,128)(2,1)S(1)} %all-to-all-done.1.refs_1_, bf16[8,128,128]{2,1,0:T(8,128)(2,1)} %all-to-all-done.3.refs_2_, f32[1024,256]{1,0:T(8,128)S(1)} %concatenate.5.refs_2_.refs_3_, ...), custom_call_target="tpu_custom_call" | custom-call | tf_op jit(solution)/shard_map/pallas_call | solution.py:359
  246.2 5.9 %all-to-all-start.4 = ((bf16[8,128,384]{2,1,0:T(8,128)(2,1)}), bf16[8,128,384]{2,1,0:T(8,128)(2,1)}, u32[]{:S(2)}, u32[]{:S(2)}) async-start(bf16[8,128,384]{2,1,0:T(8,128)(2,1)} %shard_map.203.refs_3_), calls=%async_computation.4 | async-start | bytes 1572864 | tf_op jit(solution)/shard_map/all_to_all | solution.py:950
  255.8 5.5 %collective-permute-done.23.refs_2_ = bf16[128,1024]{1,0:T(8,128)(2,1)S(1)} collective-permute-done((bf16[128,1024]{1,0:T(8,128)(2,1)S(1)}, bf16[128,1024]{1,0:T(8,128)(2,1)S(1)}, u32[]{:S(2)}, u32[]{:S(2)}) %collective-permute-start.23) | collective-permute-done | bytes 262176 | tf_op jit(solution)/shard_map/ppermute | solution.py:340
  262.2 8.2 %all-to-all-done.4.refs_1_ = bf16[8,128,384]{2,1,0:T(8,128)(2,1)} async-done(((bf16[8,128,384]{2,1,0:T(8,128)(2,1)}), bf16[8,128,384]{2,1,0:T(8,128)(2,1)}, u32[]{:S(2)}, u32[]{:S(2)}) %all-to-all-start.4) | async-done | bytes 786464 | tf_op jit(solution)/shard_map/all_to_all | solution.py:950
  277.7 3.3 shard_map.207
  282.6 7.4 %collective-permute-done.27.refs_3_ = bf16[256,1024]{1,0:T(8,128)(2,1)S(1)} collective-permute-done((bf16[256,1024]{1,0:T(8,128)(2,1)S(1)}, bf16[256,1024]{1,0:T(8,128)(2,1)S(1)}, u32[]{:S(2)}, u32[]{:S(2)}) %collective-permute-start.27) | collective-permute-done | bytes 524320 | tf_op jit(solution)/shard_map/ppermute | solution.py:340
  298.6 8.1 %collective-permute-done.29.refs_1_ = bf16[4,128,1024]{2,1,0:T(8,128)(2,1)} collective-permute-done((bf16[4,128,1024]{2,1,0:T(8,128)(2,1)}, bf16[4,128,1024]{2,1,0:T(8,128)(2,1)}, u32[]{:S(2)}, u32[]{:S(2)}) %collective-permute-start.29) | collective-permute-done | bytes 1048608 | tf_op jit(solution)/shard_map/ppermute | solution.py:336
  311.0 7.6 %collective-permute-done.34.refs_2_ = bf16[1088,256]{1,0:T(8,128)(2,1)S(1)} collective-permute-done((bf16[1088,256]{1,0:T(8,128)(2,1)}, bf16[1088,256]{1,0:T(8,128)(2,1)S(1)}, u32[]{:S(2)}, u32[]{:S(2)}) %collective-permute-start.34) | collective-permute-done | bytes 557088 | tf_op jit(solution)/shard_map/ppermute | solution.py:336
  323.8 18.1 %collective-permute-done.33.refs_6_.refs_7_ = bf16[128,1024]{1,0:T(8,128)(2,1)S(1)} collective-permute-done((bf16[128,1024]{1,0:T(8,128)(2,1)S(1)}, bf16[128,1024]{1,0:T(8,128)(2,1)S(1)}, u32[]{:S(2)}, u32[]{:S(2)}) %collective-permute-start.33) | collective-permute-done | bytes 262176 | tf_op jit(solution)/shard_map/ppermute | solution.py:336
  341.9 4.4 %shard_map.212 = (bf16[128,1024]{1,0:T(8,128)(2,1)}, bf16[128,1024]{1,0:T(8,128)(2,1)}) custom-call(s32[2]{0:T(128)S(1)} %pad_add_fusion.refs_0_, bf16[256,1024]{1,0:T(8,128)(2,1)S(1)} %get-tuple-element.120.refs_1_, bf16[2,2048,256]{2,1,0:T(8,128)(2,1)} %get-tuple-element.121.refs_2_, bf16[2,2048,256]{2,1,0:T(8,128)(2,1)} %collective-permute-done.28.refs_3_, ...), custom_call_target="tpu_custom_call" | custom-call | tf_op jit(solution)/shard_map/pallas_call | solution.py:359
  353.2 11.0 %collective-permute-done.38.refs_2_ = bf16[128,1792]{1,0:T(8,128)(2,1)S(1)} collective-permute-done((bf16[128,1792]{1,0:T(8,128)(2,1)S(1)}, bf16[128,1792]{1,0:T(8,128)(2,1)S(1)}, u32[]{:S(2)}, u32[]{:S(2)}) %collective-permute-start.38) | collective-permute-done | bytes 458784 | tf_op jit(solution)/shard_map/ppermute | solution.py:340
  369.7 4.1 %shard_map.216 = (f32[128,3072]{1,0:T(8,128)}, f32[128,1024]{1,0:T(8,128)}, f32[256,1024]{1,0:T(8,128)}, f32[128,2048]{1,0:T(8,128)}) custom-call(s32[2]{0:T(128)S(1)} %pad_add_fusion.refs_0_, bf16[128,1792]{1,0:T(8,128)(2,1)S(1)} %shard_map.213.refs_2_.refs_1_, bf16[128,1792]{1,0:T(8,128)(2,1)S(1)} %collective-permute-done.38.refs_2_, ...), custom_call_target="tpu_custom_call" | custom-call | tf_op jit(solution)/shard_map/pallas_call | solution.py:359
  (259 shorter events, 140.3 us)
Async XLA Ops:
  7.2 73.6 %all-gather.3.cloned.1.call-start = ((), (), s32[]{:S(2)}) async-start(), calls=%async_computation.6 | async-start | bytes 1769472 | tf_op jit(solution)/shard_map/all_gather | solution.py:1017
  14.9 49.9 %all-to-all-start = ((bf16[4,128,2048]{2,1,0:T(8,128)(2,1)}), bf16[4,128,2048]{2,1,0:T(8,128)(2,1)S(1)}, u32[]{:S(2)}, u32[]{:S(2)}) async-start(bf16[4,128,2048]{2,1,0:T(8,128)(2,1)} %copy-done.5), calls=%async_computation | async-start | bytes 4194304 | tf_op jit(solution)/shard_map/all_to_all | solution.py:1016
  19.3 155.1 %all-gather.5.cloned.1.call-start = ((), (), s32[]{:S(2)}) async-start(), calls=%async_computation.7 | async-start | bytes 4718592 | tf_op jit(solution)/shard_map/all_gather | solution.py:1026
  19.3 10.6 %collective-permute-start = (bf16[320,256]{1,0:T(8,128)(2,1)S(1)}, bf16[320,256]{1,0:T(8,128)(2,1)S(1)}, u32[]{:S(2)}, u32[]{:S(2)}) collective-permute-start(bf16[320,256]{1,0:T(8,128)(2,1)S(1)} %shard_map.178.refs_2_.refs_0_), channel_id=1, source_target_pairs={{0,2},{1,3},{2,0},{3,1},{4,6},{5,7},{6,4},{7,5},{8,10},{9,11},{10,... | collective-permute-start | bytes 491528 | tf_op jit(solution)/shard_map/ppermute | solution.py:336
  19.4 14.5 %collective-permute-start.1 = (bf16[320,256]{1,0:T(8,128)(2,1)S(1)}, bf16[320,256]{1,0:T(8,128)(2,1)S(1)}, u32[]{:S(2)}, u32[]{:S(2)}) collective-permute-start(bf16[320,256]{1,0:T(8,128)(2,1)S(1)} %shard_map.178.refs_2_.refs_0_), channel_id=1, source_target_pairs={{0,4},{1,5},{2,6},{3,7},{4,0},{5,1},{6,2},{7,3},{8,12},{9,13},{10,... | collective-permute-start | bytes 491528 | tf_op jit(solution)/shard_map/ppermute | solution.py:336
  21.9 21.3 %collective-permute-start.2 = (bf16[320,256]{1,0:T(8,128)(2,1)S(1)}, bf16[320,256]{1,0:T(8,128)(2,1)S(1)}, u32[]{:S(2)}, u32[]{:S(2)}) collective-permute-start(bf16[320,256]{1,0:T(8,128)(2,1)S(1)} %shard_map.178.refs_2_.refs_0_), channel_id=1, source_target_pairs={{0,6},{1,7},{2,4},{3,5},{4,2},{5,3},{6,0},{7,1},{8,14},{9,15},{10,... | collective-permute-start | bytes 491528 | tf_op jit(solution)/shard_map/ppermute | solution.py:336
  43.3 21.5 %collective-permute-start.3 = (bf16[1088,256]{1,0:T(8,128)(2,1)S(1)}, bf16[1088,256]{1,0:T(8,128)(2,1)}, u32[]{:S(2)}, u32[]{:S(2)}) collective-permute-start(bf16[1088,256]{1,0:T(8,128)(2,1)S(1)} %shard_map.181.refs_1_.refs_2_), channel_id=1, source_target_pairs={{0,1},{1,0},{2,3},{3,2},{4,5},{5,4},{6,7},{7,6},{8,9},{9,8},{10,11... | collective-permute-start | bytes 1671176 | tf_op jit(solution)/shard_map/ppermute | solution.py:336
  88.2 33.8 %all-to-all-start.1 = ((bf16[8,128,384]{2,1,0:T(8,128)(2,1)}), bf16[8,128,384]{2,1,0:T(8,128)(2,1)S(1)}, u32[]{:S(2)}, u32[]{:S(2)}) async-start(bf16[8,128,384]{2,1,0:T(8,128)(2,1)} %get-tuple-element.85.refs_1_.refs_2_), calls=%async_computation.1 | async-start | bytes 1572864 | tf_op jit(solution)/shard_map/all_to_all | solution.py:950
  94.5 24.8 %collective-permute-start.11 = (bf16[2048,256]{1,0:T(8,128)(2,1)S(1)}, bf16[2048,256]{1,0:T(8,128)(2,1)}, u32[]{:S(2)}, u32[]{:S(2)}) collective-permute-start(bf16[2048,256]{1,0:T(8,128)(2,1)S(1)} %shard_map.187.refs_0_), channel_id=1, source_target_pairs={{0,16},{8,24},{16,0},{24,8},{1,17},{9,25},{17,1},{25,9},{2,18},{10... | collective-permute-start | bytes 3145736 | tf_op jit(solution)/shard_map/ppermute | solution.py:340
  98.1 10.8 %collective-permute-start.10 = (bf16[256,1024]{1,0:T(8,128)(2,1)}, bf16[256,1024]{1,0:T(8,128)(2,1)}, u32[]{:S(2)}, u32[]{:S(2)}) collective-permute-start(bf16[256,1024]{1,0:T(8,128)(2,1)} %shard_map.185.refs_1_), channel_id=1, source_target_pairs={{0,1},{2,3},{4,5},{6,7},{9,8},{11,10},{13,12},{15,14},{16,17},{18,... | collective-permute-start | bytes 1572872 | tf_op jit(solution)/shard_map/ppermute | solution.py:970
  129.6 19.9 %all-to-all-start.2 = ((bf16[8,128,128]{2,1,0:T(8,128)(2,1)}), bf16[8,128,128]{2,1,0:T(8,128)(2,1)}, u32[]{:S(2)}, u32[]{:S(2)}) async-start(bf16[8,128,128]{2,1,0:T(8,128)(2,1)} %get-tuple-element.90.refs_1_), calls=%async_computation.2 | async-start | bytes 524288 | tf_op jit(solution)/shard_map/all_to_all | solution.py:950
  135.1 162.4 %reduce-scatter.2.cloned.1.call-start = ((), (), s32[]{:S(2)}) async-start(), calls=%async_computation.8 | async-start | bytes 4718592 | tf_op jit(solution)/shard_map/reduce_scatter | solution.py:1167
  155.6 13.4 %collective-permute-start.16 = (bf16[256,1024]{1,0:T(8,128)(2,1)S(1)}, bf16[256,1024]{1,0:T(8,128)(2,1)S(1)}, u32[]{:S(2)}, u32[]{:S(2)}) collective-permute-start(bf16[256,1024]{1,0:T(8,128)(2,1)S(1)} %get-tuple-element.96), channel_id=1, source_target_pairs={{0,16},{8,24},{16,0},{24,8},{1,17},{9,25},{17,1},{25,9},{2,18},{10... | collective-permute-start | bytes 1572872 | tf_op jit(solution)/shard_map/ppermute | solution.py:340
  189.3 13.5 %collective-permute-start.24 = (bf16[256,1024]{1,0:T(8,128)(2,1)}, bf16[256,1024]{1,0:T(8,128)(2,1)}, u32[]{:S(2)}, u32[]{:S(2)}) collective-permute-start(bf16[256,1024]{1,0:T(8,128)(2,1)} %get-tuple-element.109), channel_id=1, source_target_pairs={{0,16},{8,24},{16,0},{24,8},{1,17},{9,25},{17,1},{25,9},{2,18},{10... | collective-permute-start | bytes 1572872 | tf_op jit(solution)/shard_map/ppermute | solution.py:340
  206.1 24.9 %collective-permute-start.19 = (bf16[256,1024]{1,0:T(8,128)(2,1)}, bf16[256,1024]{1,0:T(8,128)(2,1)}, u32[]{:S(2)}, u32[]{:S(2)}) collective-permute-start(bf16[256,1024]{1,0:T(8,128)(2,1)} %get-tuple-element.106.refs_6_), channel_id=1, source_target_pairs={{0,8},{8,0},{16,24},{24,16},{1,9},{9,1},{17,25},{25,17},{2,10},{10... | collective-permute-start | bytes 1572872 | tf_op jit(solution)/shard_map/ppermute | solution.py:340
  209.7 26.6 %all-to-all-start.3 = ((bf16[8,128,128]{2,1,0:T(8,128)(2,1)}), bf16[8,128,128]{2,1,0:T(8,128)(2,1)}, u32[]{:S(2)}, u32[]{:S(2)}) async-start(bf16[8,128,128]{2,1,0:T(8,128)(2,1)} %copy-done.36), calls=%async_computation.3 | async-start | bytes 524288 | tf_op jit(solution)/shard_map/all_to_all | solution.py:950
  219.1 11.9 %collective-permute-start.22 = (bf16[512,256]{1,0:T(8,128)(2,1)}, bf16[512,256]{1,0:T(8,128)(2,1)S(1)}, u32[]{:S(2)}, u32[]{:S(2)}) collective-permute-start(bf16[512,256]{1,0:T(8,128)(2,1)} %copy-done.52), channel_id=1, source_target_pairs={{0,24},{8,16},{16,8},{24,0},{1,25},{9,17},{17,9},{25,1},{2,26},{10... | collective-permute-start | bytes 786440 | tf_op jit(solution)/shard_map/ppermute | solution.py:340
  246.2 24.2 %all-to-all-start.4 = ((bf16[8,128,384]{2,1,0:T(8,128)(2,1)}), bf16[8,128,384]{2,1,0:T(8,128)(2,1)}, u32[]{:S(2)}, u32[]{:S(2)}) async-start(bf16[8,128,384]{2,1,0:T(8,128)(2,1)} %shard_map.203.refs_3_), calls=%async_computation.4 | async-start | bytes 1572864 | tf_op jit(solution)/shard_map/all_to_all | solution.py:950
  275.0 45.3 %collective-permute-start.28 = (bf16[2,2048,256]{2,1,0:T(8,128)(2,1)}, bf16[2,2048,256]{2,1,0:T(8,128)(2,1)}, u32[]{:S(2)}, u32[]{:S(2)}) collective-permute-start(bf16[2,2048,256]{2,1,0:T(8,128)(2,1)} %get-tuple-element.121.refs_2_), channel_id=1, source_target_pairs={{0,8},{8,0},{16,24},{24,16},{1,9},{9,1},{17,25},{25,17},{2,10},{10... | collective-permute-start | bytes 6291464 | tf_op jit(solution)/shard_map/ppermute | solution.py:340
  276.6 13.3 %collective-permute-start.27 = (bf16[256,1024]{1,0:T(8,128)(2,1)S(1)}, bf16[256,1024]{1,0:T(8,128)(2,1)S(1)}, u32[]{:S(2)}, u32[]{:S(2)}) collective-permute-start(bf16[256,1024]{1,0:T(8,128)(2,1)S(1)} %get-tuple-element.116), channel_id=1, source_target_pairs={{0,16},{8,24},{16,0},{24,8},{1,17},{9,25},{17,1},{25,9},{2,18},{10... | collective-permute-start | bytes 1572872 | tf_op jit(solution)/shard_map/ppermute | solution.py:340
  282.0 24.7 %collective-permute-start.29 = (bf16[4,128,1024]{2,1,0:T(8,128)(2,1)}, bf16[4,128,1024]{2,1,0:T(8,128)(2,1)}, u32[]{:S(2)}, u32[]{:S(2)}) collective-permute-start(bf16[4,128,1024]{2,1,0:T(8,128)(2,1)} %get-tuple-element.119.refs_6_), channel_id=1, source_target_pairs={{0,1},{1,0},{2,3},{3,2},{4,5},{5,4},{6,7},{7,6},{8,9},{9,8},{10,11... | collective-permute-start | bytes 3145736 | tf_op jit(solution)/shard_map/ppermute | solution.py:336
  296.3 22.3 %collective-permute-start.34 = (bf16[1088,256]{1,0:T(8,128)(2,1)}, bf16[1088,256]{1,0:T(8,128)(2,1)S(1)}, u32[]{:S(2)}, u32[]{:S(2)}) collective-permute-start(bf16[1088,256]{1,0:T(8,128)(2,1)} %get-tuple-element.125.refs_2_), channel_id=1, source_target_pairs={{0,1},{1,0},{2,3},{3,2},{4,5},{5,4},{6,7},{7,6},{8,9},{9,8},{10,11... | collective-permute-start | bytes 1671176 | tf_op jit(solution)/shard_map/ppermute | solution.py:336
  297.4 52.7 %collective-permute-start.41 = (bf16[128,2048]{1,0:T(8,128)(2,1)}, bf16[128,2048]{1,0:T(8,128)(2,1)S(1)}, u32[]{:S(2)}, u32[]{:S(2)}) collective-permute-start(bf16[128,2048]{1,0:T(8,128)(2,1)} %reduce-scatter.2.cloned.1.call-done.refs_0_), channel_id=1, source_target_pairs={{0,16},{8,24},{16,0},{24,8},{1,17},{9,25},{17,1},{25,9},{2,18},{10... | collective-permute-start | bytes 1572872 | tf_op jit(solution)/shard_map/ppermute | solution.py:340
  308.2 14.0 %collective-permute-start.31 = (bf16[128,1024]{1,0:T(8,128)(2,1)S(1)}, bf16[128,1024]{1,0:T(8,128)(2,1)S(1)}, u32[]{:S(2)}, u32[]{:S(2)}) collective-permute-start(bf16[128,1024]{1,0:T(8,128)(2,1)S(1)} %get-tuple-element.126), channel_id=1, source_target_pairs={{0,2},{1,3},{2,0},{3,1},{4,6},{5,7},{6,4},{7,5},{8,10},{9,11},{10,... | collective-permute-start | bytes 786440 | tf_op jit(solution)/shard_map/ppermute | solution.py:336
  310.7 12.7 %collective-permute-start.32 = (bf16[128,1024]{1,0:T(8,128)(2,1)S(1)}, bf16[128,1024]{1,0:T(8,128)(2,1)S(1)}, u32[]{:S(2)}, u32[]{:S(2)}) collective-permute-start(bf16[128,1024]{1,0:T(8,128)(2,1)S(1)} %get-tuple-element.127), channel_id=1, source_target_pairs={{0,4},{1,5},{2,6},{3,7},{4,0},{5,1},{6,2},{7,3},{8,12},{9,13},{10,... | collective-permute-start | bytes 786440 | tf_op jit(solution)/shard_map/ppermute | solution.py:336
  318.6 23.3 %collective-permute-start.33 = (bf16[128,1024]{1,0:T(8,128)(2,1)S(1)}, bf16[128,1024]{1,0:T(8,128)(2,1)S(1)}, u32[]{:S(2)}, u32[]{:S(2)}) collective-permute-start(bf16[128,1024]{1,0:T(8,128)(2,1)S(1)} %get-tuple-element.128), channel_id=1, source_target_pairs={{0,6},{1,7},{2,4},{3,5},{4,2},{5,3},{6,0},{7,1},{8,14},{9,15},{10,... | collective-permute-start | bytes 786440 | tf_op jit(solution)/shard_map/ppermute | solution.py:336
  320.3 26.1 %collective-permute-start.35 = (bf16[320,256]{1,0:T(8,128)(2,1)S(1)}, bf16[320,256]{1,0:T(8,128)(2,1)S(1)}, u32[]{:S(2)}, u32[]{:S(2)}) collective-permute-start(bf16[320,256]{1,0:T(8,128)(2,1)S(1)} %get-tuple-element.135), channel_id=1, source_target_pairs={{0,2},{1,3},{2,0},{3,1},{4,6},{5,7},{6,4},{7,5},{8,10},{9,11},{10,... | collective-permute-start | bytes 491528 | tf_op jit(solution)/shard_map/ppermute | solution.py:336
  322.3 24.1 %collective-permute-start.36 = (bf16[320,256]{1,0:T(8,128)(2,1)S(1)}, bf16[320,256]{1,0:T(8,128)(2,1)S(1)}, u32[]{:S(2)}, u32[]{:S(2)}) collective-permute-start(bf16[320,256]{1,0:T(8,128)(2,1)S(1)} %get-tuple-element.136), channel_id=1, source_target_pairs={{0,4},{1,5},{2,6},{3,7},{4,0},{5,1},{6,2},{7,3},{8,12},{9,13},{10,... | collective-permute-start | bytes 491528 | tf_op jit(solution)/shard_map/ppermute | solution.py:336
  323.4 25.6 %collective-permute-start.37 = (bf16[320,256]{1,0:T(8,128)(2,1)S(1)}, bf16[320,256]{1,0:T(8,128)(2,1)S(1)}, u32[]{:S(2)}, u32[]{:S(2)}) collective-permute-start(bf16[320,256]{1,0:T(8,128)(2,1)S(1)} %get-tuple-element.137), channel_id=1, source_target_pairs={{0,6},{1,7},{2,4},{3,5},{4,2},{5,3},{6,0},{7,1},{8,14},{9,15},{10,... | collective-permute-start | bytes 491528 | tf_op jit(solution)/shard_map/ppermute | solution.py:336
  350.8 14.4 %collective-permute-start.42 = (bf16[2,128,2048]{2,1,0:T(8,128)(2,1)S(1)}, bf16[2,128,2048]{2,1,0:T(8,128)(2,1)S(1)}, u32[]{:S(2)}, u32[]{:S(2)}) collective-permute-start(bf16[2,128,2048]{2,1,0:T(8,128)(2,1)S(1)} %get-tuple-element.138.refs_1_), channel_id=1, source_target_pairs={{0,8},{8,0},{16,24},{24,16},{1,9},{9,1},{17,25},{25,17},{2,10},{10... | collective-permute-start | bytes 3145736 | tf_op jit(solution)/shard_map/ppermute | solution.py:340
  352.0 12.2 %collective-permute-start.38 = (bf16[128,1792]{1,0:T(8,128)(2,1)S(1)}, bf16[128,1792]{1,0:T(8,128)(2,1)S(1)}, u32[]{:S(2)}, u32[]{:S(2)}) collective-permute-start(bf16[128,1792]{1,0:T(8,128)(2,1)S(1)} %shard_map.213.refs_2_.refs_1_), channel_id=1, source_target_pairs={{0,16},{8,24},{16,0},{24,8},{1,17},{9,25},{17,1},{25,9},{2,18},{10... | collective-permute-start | bytes 1376264 | tf_op jit(solution)/shard_map/ppermute | solution.py:340
  352.8 15.3 %collective-permute-start.39 = (bf16[128,1792]{1,0:T(8,128)(2,1)S(1)}, bf16[128,1792]{1,0:T(8,128)(2,1)}, u32[]{:S(2)}, u32[]{:S(2)}) collective-permute-start(bf16[128,1792]{1,0:T(8,128)(2,1)S(1)} %shard_map.213.refs_2_.refs_1_), channel_id=1, source_target_pairs={{0,8},{8,0},{16,24},{24,16},{1,9},{9,1},{17,25},{25,17},{2,10},{10... | collective-permute-start | bytes 1376264 | tf_op jit(solution)/shard_map/ppermute | solution.py:340
  (86 other events, 526.5 us)
Sparse Core Ops, SparseCore 0:
  10.8 60.1 all-gather.2
  73.1 83.1 all-gather.4
  196.1 101.2 reduce-scatter.1
